TPU v7x, 128 devices: a whole 4x4x4 slice. The times are simulated.
128 devices in a mesh: seq: 16 (over z, x_lo, core), tensor: 8 (over y, x_hi).
Axes of the slice: x: 4 (x_hi: 2, x_lo: 2; x = x_hi * 2 + x_lo), y: 4, z: 4, core: 2. Of those that a mesh axis runs over, the one named last changes fastest.
Arguments:
- tokens: bfloat16 [4096, 2048], P('seq'), may hold values from -6 to 6
- cotangent: bfloat16 [4096, 2048], P('seq'), may hold values from -6 to 6
- exits: int32 [4096], P('seq'), may hold values from 0 to 23, as said below
- lengths: int32 [4], replicated, may hold values from 1 to 2048, 4096 in all
- panels: float32 [384, 64, 2048], P(('tensor', 'seq'))
- panel_mom: float32 [384, 64, 2048], P(('tensor', 'seq')), may hold values from -80 to 80
- unit_bias: float32 [32, 384], P('tensor'), may hold values from -1.75 to 1.75
- unit_bias_mom: float32 [32, 384], P('tensor'), may hold values from -112 to 112
- gains: float32 [2, 2048], replicated, may hold values from 0.5 to 1.5
- gains_mom: float32 [2, 2048], replicated, may hold values from -192 to 192
- vec_bias: float32 [4, 2048], replicated, may hold values from -1.75 to 1.75
- vec_bias_mom: float32 [4, 2048], replicated, may hold values from -192 to 192
Outputs:
- output: bfloat16 [4096, 2048], P('seq')
- input_grad: float32 [4096, 2048], P('seq')
- new_panels: float32 [384, 64, 2048], P(('tensor', 'seq'))
- new_panel_mom: float32 [384, 64, 2048], P(('tensor', 'seq'))
- new_unit_bias: float32 [32, 384], P('tensor')
- new_unit_bias_mom: float32 [32, 384], P('tensor')
- new_gains: float32 [2, 2048], replicated
- new_gains_mom: float32 [2, 2048], replicated
- new_vec_bias: float32 [4, 2048], replicated
- new_vec_bias_mom: float32 [4, 2048], replicated
Inputs may be any that keep to these rules, and one draw needn't show every extreme that they name: `exits`: constant over aligned bands of 32 positions; the share of bands with exit layer 12 or more rises from about 0.3 at the first position to 0.9 at the last. `lengths`: they sum to 4096; the longest is 2048.
All inputs are finite; a program needn't handle non-finite values.
Results may differ from a plain program's by a relative error of at most 0.035.
Values may be sent and summed in bfloat16 or wider, within the bound.
A program may use at most 128 MiB of HBM per device.

v0:
```python
import math

import jax
import jax.numpy as jnp
from jax import lax
from jax.sharding import PartitionSpec as P

LAYER = 12
NS_ITERS = 5


EPS = 1e-05
NS_A = 3.4445
NS_B = -4.775
NS_C = 2.0315
LR_MATRIX = 0.5
LR_VECTOR = 0.002
DECAY = 0.5
HIGH = lax.Precision.HIGHEST


def times_t(left, right):
    return lax.dot_general(
        left, right, (((1,), (1,)), ((), ())), preferred_element_type=jnp.float32
    )


def inner_rows(left, right):
    return lax.dot_general(
        left, right, (((0,), (0,)), ((), ())), preferred_element_type=jnp.float32
    )


def plain(left, right):
    return jnp.dot(left, right, preferred_element_type=jnp.float32)


def normalize(values, gain, shift):
    mean = jnp.mean(values, axis=-1, keepdims=True)
    centred = values - mean
    factor = lax.rsqrt(jnp.mean(centred * centred, axis=-1, keepdims=True) + EPS)
    return (centred * factor * gain + shift, centred * factor, factor)


def norm_back(grad, unit, factor, gain):
    d_gain = jnp.sum(grad * unit, axis=0)
    d_shift = jnp.sum(grad, axis=0)
    d_unit = grad * gain
    d_in = factor * (
        d_unit
        - jnp.mean(d_unit, axis=-1, keepdims=True)
        - unit * jnp.mean(d_unit * unit, axis=-1, keepdims=True)
    )
    return (d_in, d_gain, d_shift)


def orthogonalize(moment):
    current = moment * lax.rsqrt(jnp.sum(moment * moment, axis=(1, 2), keepdims=True) + 1e-06)
    for sweep in range(NS_ITERS):
        gram = jnp.einsum("pij,pkj->pik", current, current, precision=HIGH)
        poly = NS_B * gram + NS_C * jnp.einsum("pij,pjk->pik", gram, gram, precision=HIGH)
        current = NS_A * current + jnp.einsum("pij,pjk->pik", poly, current, precision=HIGH)
    return current


def per_device(
    tokens,
    cotangent,
    exits,
    lengths,
    panels,
    panel_mom,
    unit_bias,
    unit_bias_mom,
    gains,
    gains_mom,
    vec_bias,
    vec_bias_mom,
):
    rows, width = tokens.shape
    groups = unit_bias.shape[0]
    head_dim = panels.shape[1]
    ranks = lax.axis_size("seq")
    total = rows * ranks
    positions = lax.axis_index("seq") * rows + jnp.arange(rows, dtype=jnp.int32)
    ends = jnp.cumsum(lengths)
    segment = jnp.sum((positions[:, None] >= ends[None, :]).astype(jnp.int32), axis=1)
    alive = (exits >= LAYER).astype(jnp.int32)
    live = alive.astype(jnp.float32)[:, None]
    scale = head_dim ** (-0.5)
    block = math.gcd(total, 512)
    count = total // block
    begins = jnp.arange(count, dtype=jnp.int32) * block
    stack = lax.all_gather(panels.astype(jnp.bfloat16), "seq", axis=0, tiled=True).reshape(
        groups, 12, head_dim, width
    )
    w_query = stack[:, 0].reshape(groups * head_dim, width)
    w_key = stack[:, 1].reshape(groups * head_dim, width)
    w_value = stack[:, 2].reshape(groups * head_dim, width)
    w_out = stack[:, 3].reshape(groups * head_dim, width)
    w_in = stack[:, 4:8].reshape(groups * 4 * head_dim, width)
    w_back = stack[:, 8:12].reshape(groups * 4 * head_dim, width)
    b_query = unit_bias[:, :head_dim].reshape(-1)
    b_value = unit_bias[:, head_dim : 2 * head_dim].reshape(-1)
    b_in = unit_bias[:, 2 * head_dim :].reshape(-1)
    x_full = tokens.astype(jnp.float32)
    normed1, unit1, factor1 = normalize(x_full, gains[0], vec_bias[2])
    low1 = normed1.astype(jnp.bfloat16)
    query = (times_t(low1, w_query) + b_query).astype(jnp.bfloat16)
    keys = times_t(low1, w_key).astype(jnp.bfloat16)
    values = (times_t(low1, w_value) + b_value).astype(jnp.bfloat16)
    q_heads = query.reshape(rows, groups, head_dim)
    top = jnp.full((groups, rows), -1e30, jnp.float32)
    accum = jnp.zeros((rows, groups, head_dim), jnp.float32)
    k_piece = lax.all_gather(keys, "seq", axis=0, tiled=True)
    v_piece = lax.all_gather(values, "seq", axis=0, tiled=True)
    s_piece = lax.all_gather(segment, "seq", axis=0, tiled=True)
    a_piece = lax.all_gather(alive, "seq", axis=0, tiled=True)
    span = k_piece.shape[0]
    k_pos = jnp.arange(span, dtype=jnp.int32)
    allowed = (segment[:, None] == s_piece[None, :]) & (positions[:, None] >= k_pos[None, :])
    allowed = allowed & (alive[:, None] > 0) & (a_piece[None, :] > 0)
    score = (
        jnp.einsum(
            "qhe,khe->hqk",
            q_heads,
            k_piece.reshape(span, groups, head_dim),
            preferred_element_type=jnp.float32,
        )
        * scale
    )
    score = jnp.where(allowed[None], score, -1e30)
    new_top = jnp.maximum(top, jnp.max(score, axis=2))
    weight = jnp.where(allowed[None], jnp.exp(score - new_top[:, :, None]), 0.0)
    fade = jnp.exp(top - new_top)
    weight_sum = jnp.sum(weight, axis=2)
    mixed = jnp.einsum(
        "hqk,khe->qhe",
        weight.astype(jnp.bfloat16),
        v_piece.reshape(span, groups, head_dim),
        preferred_element_type=jnp.float32,
    )
    accum = accum * fade.T[:, :, None] + mixed
    top, weight_sum, accum = (new_top, weight_sum, accum)
    safe_sum = jnp.maximum(weight_sum, 1.0)
    attn_full = accum / safe_sum.T[:, :, None]
    log_total = top + jnp.log(safe_sum)
    attn_low = attn_full.reshape(rows, groups * head_dim).astype(jnp.bfloat16)
    attn_whole = lax.psum(plain(attn_low, w_out).astype(jnp.bfloat16), "tensor").astype(jnp.float32)
    hidden = x_full + live * (attn_whole + vec_bias[0])
    normed2, unit2, factor2 = normalize(hidden, gains[1], vec_bias[3])
    low2 = normed2.astype(jnp.bfloat16)
    pre = times_t(low2, w_in) + b_in
    act_low = jax.nn.gelu(pre, approximate=False).astype(jnp.bfloat16)
    ffn_whole = lax.psum(plain(act_low, w_back).astype(jnp.bfloat16), "tensor").astype(jnp.float32)
    output = hidden + live * (ffn_whole + vec_bias[1])
    grad_out = cotangent.astype(jnp.float32)
    d_ffn = (live * grad_out).astype(jnp.bfloat16)
    d_b2 = jnp.sum(d_ffn.astype(jnp.float32), axis=0)
    d_w_back = inner_rows(act_low, d_ffn)
    d_act = times_t(d_ffn, w_back)
    gelu_value, gelu_pull = jax.vjp(lambda value: jax.nn.gelu(value, approximate=False), pre)
    d_pre = gelu_pull(d_act)[0].astype(jnp.bfloat16)
    d_b1 = jnp.sum(d_pre.astype(jnp.float32), axis=0)
    d_w_in = inner_rows(d_pre, low2)
    d_norm2 = lax.psum(plain(d_pre, w_in).astype(jnp.bfloat16), "tensor").astype(jnp.float32)
    d_hidden_norm, d_gain2, d_shift2 = norm_back(d_norm2, unit2, factor2, gains[1])
    d_hidden = grad_out + d_hidden_norm
    d_branch = (live * d_hidden).astype(jnp.bfloat16)
    d_bo = jnp.sum(d_branch.astype(jnp.float32), axis=0)
    d_w_out = inner_rows(attn_low, d_branch)
    d_attn = times_t(d_branch, w_out).astype(jnp.bfloat16)
    d_heads = d_attn.reshape(rows, groups, head_dim)
    delta = jnp.einsum("qhe,qhe->hq", d_heads.astype(jnp.float32), attn_full)
    all_keys, all_values, all_seg, all_alive = (
        lax.all_gather(keys, "seq", axis=0, tiled=True),
        lax.all_gather(values, "seq", axis=0, tiled=True),
        lax.all_gather(segment, "seq", axis=0, tiled=True),
        lax.all_gather(alive, "seq", axis=0, tiled=True),
    )

    def back_block(d_query, blocked):
        k_blk, v_blk, s_blk, a_blk, begin = blocked
        k_pos = begin + jnp.arange(block, dtype=jnp.int32)
        allowed = (segment[:, None] == s_blk[None, :]) & (positions[:, None] >= k_pos[None, :])
        allowed = allowed & (alive[:, None] > 0) & (a_blk[None, :] > 0)
        k_h = k_blk.reshape(block, groups, head_dim)
        v_h = v_blk.reshape(block, groups, head_dim)
        score = jnp.einsum("qhe,khe->hqk", q_heads, k_h, preferred_element_type=jnp.float32) * scale
        prob = jnp.where(allowed[None], jnp.exp(score - log_total[:, :, None]), 0.0)
        d_val = jnp.einsum(
            "hqk,qhe->khe", prob.astype(jnp.bfloat16), d_heads, preferred_element_type=jnp.float32
        )
        d_prob = jnp.einsum("qhe,khe->hqk", d_heads, v_h, preferred_element_type=jnp.float32)
        d_score = (prob * (d_prob - delta[:, :, None])).astype(jnp.bfloat16)
        d_query = d_query + jnp.einsum(
            "hqk,khe->qhe", d_score, k_h, preferred_element_type=jnp.float32
        )
        d_key = jnp.einsum("hqk,qhe->khe", d_score, q_heads, preferred_element_type=jnp.float32)
        return (
            d_query,
            (d_key.reshape(block, groups * head_dim), d_val.reshape(block, groups * head_dim)),
        )

    blocked_in = (
        all_keys.reshape(count, block, -1),
        all_values.reshape(count, block, -1),
        all_seg.reshape(count, block),
        all_alive.reshape(count, block),
        begins,
    )
    d_query, (d_key_all, d_val_all) = lax.scan(
        back_block, jnp.zeros((rows, groups, head_dim), jnp.float32), blocked_in
    )
    d_key_all = d_key_all.reshape(total, groups * head_dim) * scale
    d_val_all = d_val_all.reshape(total, groups * head_dim)
    d_key_mine, d_val_mine = (
        lax.psum_scatter(
            d_key_all.astype(jnp.bfloat16), "seq", scatter_dimension=0, tiled=True
        ).astype(jnp.float32),
        lax.psum_scatter(
            d_val_all.astype(jnp.bfloat16), "seq", scatter_dimension=0, tiled=True
        ).astype(jnp.float32),
    )
    d_q = (d_query.reshape(rows, groups * head_dim) * scale).astype(jnp.bfloat16)
    d_k = d_key_mine.astype(jnp.bfloat16)
    d_v = d_val_mine.astype(jnp.bfloat16)
    d_bq = jnp.sum(d_q.astype(jnp.float32), axis=0)
    d_bv = jnp.sum(d_v.astype(jnp.float32), axis=0)
    d_w_query = inner_rows(d_q, low1)
    d_w_key = inner_rows(d_k, low1)
    d_w_value = inner_rows(d_v, low1)
    d_norm1_part = plain(d_q, w_query) + plain(d_k, w_key) + plain(d_v, w_value)
    d_norm1 = lax.psum(d_norm1_part.astype(jnp.bfloat16), "tensor").astype(jnp.float32)
    d_input_norm, d_gain1, d_shift1 = norm_back(d_norm1, unit1, factor1, gains[0])
    input_grad = d_hidden + d_input_norm
    grad_stack = jnp.concatenate(
        [
            d_w_query.reshape(groups, 1, head_dim, width),
            d_w_key.reshape(groups, 1, head_dim, width),
            d_w_value.reshape(groups, 1, head_dim, width),
            d_w_out.reshape(groups, 1, head_dim, width),
            d_w_in.reshape(groups, 4, head_dim, width),
            d_w_back.reshape(groups, 4, head_dim, width),
        ],
        axis=1,
    ).reshape(groups * 12, head_dim, width)
    unit_grad = jnp.concatenate(
        [
            d_bq.reshape(groups, head_dim),
            d_bv.reshape(groups, head_dim),
            d_b1.reshape(groups, 4 * head_dim),
        ],
        axis=1,
    )
    gain_grad = jnp.stack([d_gain1, d_gain2])
    shift_grad = jnp.stack([d_bo, d_b2, d_shift1, d_shift2])
    unit_sum, gain_sum, shift_sum = (
        lax.psum(unit_grad.astype(jnp.bfloat16), "seq").astype(jnp.float32),
        lax.psum(gain_grad.astype(jnp.bfloat16), "seq").astype(jnp.float32),
        lax.psum(shift_grad.astype(jnp.bfloat16), "seq").astype(jnp.float32),
    )
    mine = lax.psum_scatter(
        grad_stack.astype(jnp.bfloat16), "seq", scatter_dimension=0, tiled=True
    ).astype(jnp.float32)
    moment = DECAY * panel_mom + mine
    direction = orthogonalize(moment)
    size_w = jnp.sum(panels * panels, axis=(1, 2), keepdims=True)
    size_u = jnp.sum(direction * direction, axis=(1, 2), keepdims=True)
    new_panels = panels - LR_MATRIX * jnp.sqrt(size_w) * lax.rsqrt(size_u + 1e-06) * direction
    unit_moment = DECAY * unit_bias_mom + unit_sum
    gains_moment = DECAY * gains_mom + gain_sum
    vec_moment = DECAY * vec_bias_mom + shift_sum
    return (
        output.astype(jnp.bfloat16),
        input_grad,
        new_panels,
        moment,
        unit_bias - LR_VECTOR * unit_moment,
        unit_moment,
        gains - LR_VECTOR * gains_moment,
        gains_moment,
        vec_bias - LR_VECTOR * vec_moment,
        vec_moment,
    )


def solution(mesh):
    return jax.shard_map(
        per_device,
        mesh=mesh,
        in_specs=(
            P("seq", None),
            P("seq", None),
            P("seq"),
            P(),
            P(("tensor", "seq"), None, None),
            P(("tensor", "seq"), None, None),
            P("tensor", None),
            P("tensor", None),
            P(),
            P(),
            P(),
            P(),
        ),
        out_specs=(
            P("seq", None),
            P("seq", None),
            P(("tensor", "seq"), None, None),
            P(("tensor", "seq"), None, None),
            P("tensor", None),
            P("tensor", None),
            P(),
            P(),
            P(),
            P(),
        ),
        check_vma=False,
    )
```

profile of v0, /device:TPU:0, one launch (start us, length us, event | category | flops | bytes accessed | tf_op | source)
XLA Modules:
  0.0 918.8 jit_solution(12526772486726534003)
XLA Ops:
  12.9 72.6 %all-gather.6.cloned.1.call-done = bf16[48,64,2048]{2,1,0:T(8,128)(2,1)} async-done(((bf16[3,64,2048]{2,1,0:T(8,128)(2,1)}), bf16[48,64,2048]{2,1,0:T(8,128)(2,1)}) %all-gather.6.cloned.1.call-update) | async-done | bytes 12582928 | tf_op jit(solution)/shard_map/all_gather | solution.py:94
  85.5 4.0 fusion.90
  92.4 19.2 %all-gather.1 = s32[16,1,256]{2,1,0:T(1,128)S(1)} all-gather(s32[1,1,256]{2,1,0:T(1,128)} %bitcast.6), channel_id=1, replica_groups=mesh['seq'=16,'tensor'=8] {'seq'}, dimensions={0}, use_global_device_ids=true | all-gather | bytes 17408 | tf_op jit(solution)/shard_map/all_gather | solution.py:118
  113.3 16.3 %all-gather = s32[16,1,256]{2,1,0:T(1,128)S(1)} all-gather(s32[1,1,256]{2,1,0:T(1,128)S(1)} %bitcast.256), channel_id=1, replica_groups=mesh['seq'=16,'tensor'=8] {'seq'}, dimensions={0}, use_global_device_ids=true | all-gather | bytes 17408 | tf_op jit(solution)/shard_map/all_gather | solution.py:117
  133.6 4.1 copy.75
  137.6 4.8 fusion.6
  142.5 5.0 fusion.7
  148.8 13.9 %all-gather.10.cloned.1.call-done = bf16[4096,256]{1,0:T(8,128)(2,1)} async-done(((bf16[256,256]{1,0:T(8,128)(2,1)}), bf16[4096,256]{1,0:T(8,128)(2,1)}) %all-gather.10.cloned.1.call-update) | async-done | bytes 2097168 | tf_op jit(solution)/shard_map/all_gather | solution.py:116
  162.8 4.1 copy.76
  166.9 9.0 fusion.94
  178.6 6.1 fusion.89
  184.6 84.3 %all-reduce.6.cloned.1.call-done = bf16[256,2048]{1,0:T(8,128)(2,1)} async-done(((bf16[256,2048]{1,0:T(8,128)(2,1)}), bf16[256,2048]{1,0:T(8,128)(2,1)}) %all-reduce.6.cloned.1.call-update) | async-done | bytes 1048592 | tf_op jit(solution)/shard_map/psum | solution.py:149
  271.5 6.8 multiply_convert_fusion.2
  285.7 86.7 %all-reduce.8.cloned.1.call-done = bf16[256,2048]{1,0:T(8,128)(2,1)} async-done(((bf16[256,2048]{1,0:T(8,128)(2,1)}), bf16[256,2048]{1,0:T(8,128)(2,1)}) %all-reduce.8.cloned.1.call-update) | async-done | bytes 1048592 | tf_op jit(solution)/shard_map/psum | solution.py:166
  380.6 126.8 %while.15 = (s32[]{:T(128)}, f32[256,4,64]{0,2,1:T(8,128)}, f32[8,512,256]{2,1,0:T(8,128)}, bf16[8,512,256]{2,1,0:T(8,128)(2,1)}, bf16[8,512,256]{2,1,0:T(8,128)...) while((s32[]{:T(128)}, f32[256,4,64]{0,2,1:T(8,128)}, ...), condition=%wide.region_14.15_spmd.clone, body=%wide.region_13.14_spmd.clone.sunk | while | flops 340002304 | bytes 17589984 | solution.py:212
  507.4 3.9 multiply_convert_fusion
  512.6 4.6 convolution_convert_fusion
  525.0 49.2 %reduce-scatter.4.cloned.1.call-done = bf16[256,256]{1,0:T(8,128)(2,1)} async-done(((bf16[4096,256]{1,0:T(8,128)(2,1)}), bf16[256,256]{1,0:T(8,128)(2,1)}) %reduce-scatter.4.cloned.1.call-update) | async-done | bytes 131088 | tf_op jit(solution)/shard_map/reduce_scatter | solution.py:218
  577.7 61.9 %reduce-scatter.6.cloned.1.call-done = bf16[256,256]{1,0:T(8,128)(2,1)} async-done(((bf16[4096,256]{1,0:T(8,128)(2,1)}), bf16[256,256]{1,0:T(8,128)(2,1)}) %reduce-scatter.6.cloned.1.call-update) | async-done | bytes 131088 | tf_op jit(solution)/shard_map/reduce_scatter | solution.py:221
  651.3 4.5 copy-done.9
  656.8 91.8 %all-reduce.10.cloned.1.call-done = (bf16[256,2048]{1,0:T(8,128)(2,1)}, bf16[256,2048]{1,0:T(8,128)(2,1)}) async-done(((bf16[256,2048]{1,0:T(8,128)(2,1)}, bf16[256,2048]{1,0:T(8,128)(2,1)}), (bf16[256,2048]{1,0:T(8,128)(2,1)}, bf16[256,2048]{1,0:T(8,128)(2,1)})) %all-reduce.10.cloned.1.call-update) | async-done | bytes 2097168 | tf_op jit(solution)/shard_map/psum | solution.py:155
  752.4 58.3 %all-reduce = (bf16[4,384]{1,0:T(4,128)(2,1)S(1)}, bf16[2,2048]{1,0:T(2,128)(2,1)S(1)}, bf16[4,2048]{1,0:T(4,128)(2,1)S(1)}) all-reduce(bf16[4,384]{1,0:T(4,128)(2,1)S(1)} %pad_maximum_fusion.2, bf16[2,2048]{1,0:T(2,128)(2,1)S(1)} %pad_maximum_fusion.1, ...), channel_id=1, replica_groups=mesh['seq'=16,'tensor'=8] {'seq'}, use_global_device_ids=true, to_apply=%region_27.28 | all-reduce | flops 13824 | bytes 55296 | tf_op jit(solution)/shard_map/psum | solution.py:259
  812.6 5.1 fusion.34
  817.7 73.1 %reduce-scatter.8.cloned.1.call-done = bf16[3,64,2048]{2,1,0:T(8,128)(2,1)} async-done(((bf16[48,64,2048]{2,1,0:T(8,128)(2,1)}), bf16[3,64,2048]{2,1,0:T(8,128)(2,1)}) %reduce-scatter.8.cloned.1.call-update) | async-done | bytes 786448 | tf_op jit(solution)/shard_map/reduce_scatter | solution.py:263
  (404 shorter events, 213.7 us)
Async XLA Ops:
  7.2 78.3 %all-gather.6.cloned.1.call-start = ((), (), s32[]{:S(2)}) async-start(), calls=%async_computation.3 | async-start | bytes 13369344 | tf_op jit(solution)/shard_map/all_gather | solution.py:94
  11.0 122.6 %all-gather.8.cloned.1.call-start = ((), (), s32[]{:S(2)}) async-start(), calls=%async_computation.4 | async-start | bytes 2228224 | tf_op jit(solution)/shard_map/all_gather | solution.py:115
  11.8 363.8 %copy-start.37 = (f32[1,2048]{1,0:T(1,128)}, f32[1,2048]{1,0:T(1,128)S(1)}, u32[]{:S(2)}) copy-start(f32[1,2048]{1,0:T(1,128)S(1)} %get-tuple-element.308) | copy-start | bytes 24580
  12.4 259.1 %copy-start.60 = (f32[1,2048]{1,0:T(1,128)}, f32[1,2048]{1,0:T(1,128)S(1)}, u32[]{:S(2)}) copy-start(f32[1,2048]{1,0:T(1,128)S(1)} %get-tuple-element.304) | copy-start | bytes 24580
  12.9 118.4 %copy-start.6 = (bf16[256,2048]{1,0:T(8,128)(2,1)}, bf16[256,2048]{1,0:T(8,128)(2,1)S(1)}, u32[]{:S(2)}) copy-start(bf16[256,2048]{1,0:T(8,128)(2,1)S(1)} %fusion.31) | copy-start | bytes 3145732
  91.6 71.2 %all-gather.10.cloned.1.call-start = ((), (), s32[]{:S(2)}) async-start(), calls=%async_computation.5 | async-start | bytes 2228224 | tf_op jit(solution)/shard_map/all_gather | solution.py:116
  92.4 283.1 %copy-start.41 = (f32[256]{0:T(256)}, f32[256]{0:T(256)S(1)}, u32[]{:S(2)}) copy-start(f32[256]{0:T(256)S(1)} %get-tuple-element.314) | copy-start | bytes 3076
  112.9 156.0 %all-reduce.6.cloned.1.call-start = ((), (), s32[]{:S(2)}) async-start(), calls=%async_computation.6 | async-start | bytes 2097152 | tf_op jit(solution)/shard_map/psum | solution.py:149
  178.0 194.3 %all-reduce.8.cloned.1.call-start = ((), (), s32[]{:S(2)}) async-start(), calls=%async_computation.7 | async-start | bytes 2097152 | tf_op jit(solution)/shard_map/psum | solution.py:166
  270.7 104.8 %copy-start.56 = (f32[256]{0:T(256)}, f32[256]{0:T(256)S(1)}, u32[]{:S(2)}) copy-start(f32[256]{0:T(256)S(1)} %broadcast_multiply_fusion.4) | copy-start | bytes 3076
  271.4 104.1 %copy-start.58 = (f32[256]{0:T(256)}, f32[256]{0:T(256)S(1)}, u32[]{:S(2)}) copy-start(f32[256]{0:T(256)S(1)} %add_rsqrt_fusion) | copy-start | bytes 3076
  283.5 290.7 %reduce-scatter.4.cloned.1.call-start = ((), (), s32[]{:S(2)}) async-start(), calls=%async_computation.8 | async-start | bytes 2228224 | tf_op jit(solution)/shard_map/reduce_scatter | solution.py:218
  511.3 128.3 %reduce-scatter.6.cloned.1.call-start = ((), (), s32[]{:S(2)}) async-start(), calls=%async_computation.9 | async-start | bytes 2228224 | tf_op jit(solution)/shard_map/reduce_scatter | solution.py:221
  512.1 236.5 %all-reduce.10.cloned.1.call-start = ((), (), s32[]{:S(2)}) async-start(), calls=%async_computation.11 | async-start | bytes 4194304 | tf_op jit(solution)/shard_map/psum | solution.py:155
  643.0 247.8 %reduce-scatter.8.cloned.1.call-start = ((), (), s32[]{:S(2)}) async-start(), calls=%async_computation.10 | async-start | bytes 13369344 | tf_op jit(solution)/shard_map/reduce_scatter | solution.py:263
  655.8 94.2 %copy-start.36 = (f32[1,2048]{1,0:T(1,128)S(1)}, f32[1,2048]{1,0:T(1,128)}, u32[]{:S(2)}) copy-start(f32[1,2048]{1,0:T(1,128)} %copy-done.35) | copy-start | bytes 24580
  655.8 94.2 %copy-start.48 = (f32[256]{0:T(256)S(1)}, f32[256]{0:T(256)}, u32[]{:S(2)}) copy-start(f32[256]{0:T(256)} %copy-done.47) | copy-start | bytes 3076
  655.9 154.8 %copy-start.44 = (f32[4,384]{1,0:T(4,128)S(1)}, f32[4,384]{1,0:T(4,128)}, u32[]{:S(2)}) copy-start(f32[4,384]{1,0:T(4,128)} %param.20) | copy-start | bytes 18436
  655.9 154.8 %copy-start.62 = (f32[4,384]{1,0:T(4,128)S(1)}, f32[4,384]{1,0:T(4,128)}, u32[]{:S(2)}) copy-start(f32[4,384]{1,0:T(4,128)} %param.21) | copy-start | bytes 18436
  655.9 155.4 %copy-start.40 = (f32[2,2048]{1,0:T(2,128)S(1)}, f32[2,2048]{1,0:T(2,128)}, u32[]{:S(2)}) copy-start(f32[2,2048]{1,0:T(2,128)} %param.22) | copy-start | bytes 49156
  655.9 155.4 %copy-start.53 = (f32[2,2048]{1,0:T(2,128)S(1)}, f32[2,2048]{1,0:T(2,128)}, u32[]{:S(2)}) copy-start(f32[2,2048]{1,0:T(2,128)} %param.23) | copy-start | bytes 49156
  655.9 156.0 %copy-start.34 = (f32[4,2048]{1,0:T(4,128)S(1)}, f32[4,2048]{1,0:T(4,128)}, u32[]{:S(2)}) copy-start(f32[4,2048]{1,0:T(4,128)} %param.24) | copy-start | bytes 98308
  655.9 156.0 %copy-start.45 = (f32[4,2048]{1,0:T(4,128)S(1)}, f32[4,2048]{1,0:T(4,128)}, u32[]{:S(2)}) copy-start(f32[4,2048]{1,0:T(4,128)} %param.25) | copy-start | bytes 98308
  655.9 156.7 %copy-start.46 = (f32[1,2048]{1,0:T(1,128)S(1)}, f32[1,2048]{1,0:T(1,128)}, u32[]{:S(2)}) copy-start(f32[1,2048]{1,0:T(1,128)} %get-tuple-element.303) | copy-start | bytes 24580
  (54 other events, 616.7 us)
Sparse Core Ops, SparseCore 0:
  11.1 74.3 all-gather.5
  91.8 35.0 all-gather.7
  128.5 34.2 all-gather.9
  178.1 90.6 all-reduce.5
  283.6 88.6 all-reduce.7
  511.5 62.6 reduce-scatter.3
  576.6 62.9 reduce-scatter.5
  643.1 105.3 all-reduce.9
  751.0 139.7 reduce-scatter.7
where the time goes:
time: 930 us; the launch traced here: 919 us
  waiting for transfers between devices  534 us (57%)
  matrix products  123 us (13%)
  blocking collectives  93.8 us (10%)
  local copies, waits for them, and re-layouts  91.2 us (10%)
  other arithmetic  59.9 us (6%)
  between operations  15.3 us (2%)
    psum x1, waiting for transfers between devices, per_device(): lax.psum(plain(act_low, w_back).astype(jnp.bfloat16), 'tensor')  91.8 us
    psum x1, waiting for transfers between devices, per_device(): lax.psum(plain(d_pre, w_in).astype(jnp.bfloat16), 'tensor')  86.7 us
    psum x1, waiting for transfers between devices, per_device(): lax.psum(plain(attn_low, w_out).astype(jnp.bfloat16), 'tensor')  84.3 us
    reduce_scatter x1, waiting for transfers between devices, per_device(): lax.psum_scatter(grad_stack.astype(jnp.bfloat16), 'seq', scatter_dimensio...  73.1 us
    all_gather x1, waiting for transfers between devices, per_device(): lax.all_gather(panels.astype(jnp.bfloat16), 'seq', axis=0, tiled=True)  72.6 us
    reduce_scatter x1, waiting for transfers between devices, per_device(): lax.psum_scatter(d_val_all.astype(jnp.bfloat16), 'seq', scatter_dimension...  61.9 us
    psum x1, blocking collectives, per_device(): lax.psum(unit_grad.astype(jnp.bfloat16), 'seq').astype(jnp.float32)  58.3 us
    reduce_scatter x1, waiting for transfers between devices, per_device(): lax.psum_scatter(d_key_all.astype(jnp.bfloat16), 'seq', scatter_dimension...  49.2 us
  transfers between devices with their start and end apart: 9, of which 8 were waited for; matrix products, arithmetic and copies ran while one was open for 7% of the time, Pallas kernels for 0%

commit v1 on v0

v1 whole, which is shorter than its diff:
```python
import functools
import math

import jax
import jax.numpy as jnp
from jax import lax
from jax.experimental import pallas as pl
from jax.experimental.pallas import tpu as pltpu
from jax.sharding import PartitionSpec as P

LAYER = 12
NS_ITERS = 5
EPS = 1e-05
NS_A = 3.4445
NS_B = -4.775
NS_C = 2.0315
LR_MATRIX = 0.5
LR_VECTOR = 0.002
DECAY = 0.5
HIGH = lax.Precision.HIGHEST
MESH = pl.DeviceIdType.MESH

ROWS = 256
WIDTH = 2048
GROUPS = 4
HD = 64
SPAN = GROUPS * HD
UNITS = 4 * SPAN
SHARD = 32
EXT = ROWS + 16
MASKED = -1e30
FLOOR = -1e28
BF = jnp.bfloat16
F32 = jnp.float32

Z_STEPS = (1, 3, 2)
T_STEPS = tuple((dy, dx) for dy in (2, 1, 3, 0) for dx in (1, 0) if (dy, dx) != (0, 0))


def nt(left, right):
    return lax.dot_general(left, right, (((1,), (1,)), ((), ())), preferred_element_type=F32)


def nn(left, right):
    return jnp.dot(left, right, preferred_element_type=F32)


def normalize(values, gain, shift):
    mean = jnp.mean(values, axis=-1, keepdims=True)
    centred = values - mean
    factor = lax.rsqrt(jnp.mean(centred * centred, axis=-1, keepdims=True) + EPS)
    return centred * factor * gain + shift, centred * factor, factor


class Place:
    def __init__(self):
        self.s = lax.axis_index("seq")
        self.t = lax.axis_index("tensor")
        self.z, self.x, self.c = self.s // 4, (self.s // 2) % 2, self.s % 2
        self.chip = self.s // 2
        self.y, self.h = self.t // 2, self.t % 2

    def seq(self, z, x, c):
        return {"seq": z * 4 + x * 2 + c}

    def sibling(self):
        return self.seq(self.z, self.x, 1 - self.c)

    def across(self):
        return self.seq(self.z, 1 - self.x, self.c)

    def along(self, step):
        return self.seq((self.z + step) % 4, self.x, self.c)

    def chip_at(self, step):
        return {"seq": (self.chip + step) * 2 + self.c}

    def tensor_at(self, dy, dx):
        return ((self.y + dy) % 4) * 2 + (self.h + dx) % 2

    def greet(self):
        barrier = pltpu.get_barrier_semaphore()
        count = 0
        for dz in range(4):
            for dx in range(2):
                if (dz, dx) != (0, 0):
                    to = self.seq((self.z + dz) % 4, (self.x + dx) % 2, self.c)
                    pl.semaphore_signal(barrier, inc=1, device_id=to, device_id_type=MESH)
                    count += 1
        pl.semaphore_signal(barrier, inc=1, device_id=self.sibling(), device_id_type=MESH)
        count += 1
        for dy, dx in T_STEPS:
            to = {"tensor": self.tensor_at(dy, dx)}
            pl.semaphore_signal(barrier, inc=1, device_id=to, device_id_type=MESH)
            count += 1
        pl.semaphore_wait(barrier, count)


def remote(src, dst, send, recv, to):
    return pltpu.make_async_remote_copy(
        src_ref=src, dst_ref=dst, send_sem=send, recv_sem=recv, device_id=to, device_id_type=MESH
    )


def scatter_copies(place, part, land, send, recv):
    out = []
    for i, (dy, dx) in enumerate(T_STEPS):
        to = place.tensor_at(dy, dx)
        rows = pl.ds(pl.multiple_of(to * SHARD, SHARD), SHARD)
        out.append(remote(part.at[rows], land.at[i], send.at[i], recv.at[i], {"tensor": to}))
    return out


def scatter_sum(place, part, land):
    mine = pl.ds(pl.multiple_of(place.t * SHARD, SHARD), SHARD)
    total = part[mine, :].astype(F32)
    for i in range(len(T_STEPS)):
        total = total + land[i].astype(F32)
    return total


def gather_copies(place, whole, send, recv):
    mine = pl.ds(pl.multiple_of(place.t * SHARD, SHARD), SHARD)
    out = []
    for i, (dy, dx) in enumerate(T_STEPS):
        to = place.tensor_at(dy, dx)
        out.append(remote(whole.at[mine], whole.at[mine], send.at[i], recv.at[i], {"tensor": to}))
    return out


def column_of(row):
    n = row.shape[1]
    down = lax.broadcasted_iota(jnp.int32, (n, n), 0)
    over = lax.broadcasted_iota(jnp.int32, (n, n), 1)
    return jnp.sum(jnp.where(down == over, row, 0.0), axis=1, keepdims=True)


def segment_of(positions, lengths):
    end = jnp.int32(0)
    segment = jnp.zeros(positions.shape, F32)
    for i in range(4):
        end = end + lengths[i]
        segment = segment + jnp.where(positions >= end, 1.0, 0.0)
    return segment


def query_code(place, lengths, alive_row):
    at = place.s * ROWS + lax.broadcasted_iota(jnp.int32, (1, ROWS), 1)
    return jnp.where(alive_row > 0.5, segment_of(at, lengths), -2.0), at


def block_bias(place, lengths, window, dist, core, code, at):
    first = ((place.chip - dist) * 2 + core) * ROWS
    keys = first + lax.broadcasted_iota(jnp.int32, (ROWS, 1), 0)
    live = column_of(window[dist, core, ROWS:EXT, 0:ROWS].astype(F32)[0:1])
    key_code = jnp.where(live > 0.5, segment_of(keys, lengths), -1.0)
    same = jnp.where(key_code == code, 0.0, MASKED)
    return jnp.where(keys <= at, same, MASKED)


def head_rows(values, head):
    owner = lax.broadcasted_iota(jnp.int32, values.shape, 0) // HD
    return jnp.where(owner == head, values, jnp.zeros_like(values))


class Panels:
    def __init__(self, place, store, recv, across, along, beside):
        self.p, self.store, self.recv = place, store, recv
        self.sx, self.sz, self.sc = across, along, beside
        p = place
        self.own = 4 * p.z + 2 * p.x + p.c
        self.nbr = 4 * p.z + 2 * (1 - p.x) + p.c

    def piece(self, which, i, send, to):
        ref = self.store.at[which, i]
        return remote(ref, ref, send, self.recv.at[which, i], to)

    def to_across(self, i):
        return self.piece(self.own, i, self.sx.at[i], self.p.across())

    def to_along(self, kind, n, i):
        which = self.own if kind == 0 else self.nbr
        return self.piece(which, i, self.sz.at[kind, n, i], self.p.along(Z_STEPS[n]))

    def to_beside(self, slot, which, i):
        return self.piece(which, i, self.sc.at[slot, i], self.p.sibling())

    def from_along(self, kind, n):
        x = self.p.x if kind == 0 else 1 - self.p.x
        return 4 * ((self.p.z - Z_STEPS[n]) % 4) + 2 * x + self.p.c

    def arrived(self, which, i):
        self.piece(which, i, self.sx.at[0], self.p.sibling()).wait_recv()

    def own_across(self, i):
        self.to_across(i).start()

    def own_along(self, i):
        for n in range(3):
            self.to_along(0, n, i).start()
        self.to_beside(0, self.own, i).start()

    def nbr_on(self, i):
        self.arrived(self.nbr, i)
        for n in range(3):
            self.to_along(1, n, i).start()
        self.to_beside(1, self.nbr, i).start()

    def along_on(self, kind, i):
        for n in range(3):
            which = self.from_along(kind, n)
            self.arrived(which, i)
            self.to_beside(2 + 3 * kind + n, which, i).start()

    def beside_in(self, x, i):
        for u in range(4):
            self.arrived(4 * u + 2 * x + 1 - self.p.c, i)

    def drain(self, i):
        self.to_across(i).wait_send()
        for kind in range(2):
            for n in range(3):
                self.to_along(kind, n, i).wait_send()
        self.to_beside(0, self.own, i).wait_send()
        self.to_beside(1, self.nbr, i).wait_send()
        for kind in range(2):
            for n in range(3):
                self.to_beside(2 + 3 * kind + n, self.from_along(kind, n), i).wait_send()

    def kind_panels(self, j):
        return jnp.concatenate([self.store[4 * u + j // 3, j % 3] for u in range(GROUPS)], axis=0)

    def kind_columns(self, first, count, cols):
        parts = [
            self.store[4 * u + j // 3, j % 3, :, cols]
            for j in range(first, first + count)
            for u in range(GROUPS)
        ]
        return jnp.concatenate(parts, axis=0)


def gelu_parts(f):
    cdf = 0.5 * (1.0 + lax.erf(f * (2.0 ** -0.5)))
    pdf = jnp.exp(-0.5 * f * f) * (1.0 / math.sqrt(2.0 * math.pi))
    return f * cdf, cdf + f * pdf


def forward_kernel(
    lengths, tokens, cotangent, alive_row, alive_col, panels, bias_t, gains, shifts,
    low1_out, qt_out, window_out, ot_out, lse_out, hidden_out, low2_out, gt_out, dft_out, ffn_out, dn2_out, store_out,
    store, window, low1, qt, acc, top, mass, part, land, whole, g_rows, df_rows, dft, gt, dffn,
    w_recv, w_across, w_along, w_beside, kv_send, kv_recv, kv_bsend, kv_brecv, rs_send, rs_recv, ag_send, ag_recv, out_sem,
):
    p = Place()
    w = Panels(p, store, w_recv, w_across, w_along, w_beside)
    first = 1 - p.c
    p.greet()

    for i in range(3):
        store[w.own, i] = panels[i].astype(BF)

    order = (1, 2, 0)

    @pl.when((p.x == 0) & (p.c == 0))
    def _():
        for i in order:
            w.own_across(i)
            w.own_along(i)

    def norm1(r, carry):
        rows = pl.ds(pl.multiple_of(r * 32, 32), 32)
        normed, _, _ = normalize(tokens[rows, :].astype(F32), gains[0:1, :], shifts[2:3, :])
        low1[rows, :] = normed.astype(BF)
        dffn[rows, :] = (cotangent[rows, :].astype(F32) * alive_col[rows, :]).astype(BF)
        return carry

    lax.fori_loop(0, ROWS // 32, norm1, 0)

    for i in order:
        @pl.when((p.x == 1) & (p.c == 0))
        def _():
            w.nbr_on(i)
            w.along_on(1, i)

        @pl.when((p.x == 0) & (p.c == 0))
        def _():
            w.along_on(0, i)

        @pl.when(p.c == 1)
        def _():
            w.beside_in(0, i)

        made = nt(w.kind_panels(i), low1[...])
        if i == 1:
            window[0, p.c, 0:ROWS, 0:SPAN] = made.astype(BF).T
        elif i == 2:
            bias = jnp.concatenate([bias_t[HD : 2 * HD, u : u + 1] for u in range(GROUPS)], axis=0)
            window[0, p.c, 0:ROWS, SPAN : 2 * SPAN] = (made + bias).astype(BF).T
            row = jnp.broadcast_to(alive_row[...], (16, ROWS)).astype(BF)
            window[0, p.c, ROWS:EXT, 0:SPAN] = row
            window[0, p.c, ROWS:EXT, SPAN : 2 * SPAN] = jnp.zeros((16, SPAN), BF)
            mine = window.at[0, p.c]
            remote(mine, mine, kv_bsend.at[0], kv_brecv.at[0], p.sibling()).start()
            for d in (2, 1, 4, 3):
                @pl.when(p.chip + d < 8)
                def _():
                    remote(mine, window.at[d, p.c], kv_send.at[d], kv_recv.at[d], p.chip_at(d)).start()
        else:
            bias = jnp.concatenate([bias_t[0:HD, u : u + 1] for u in range(GROUPS)], axis=0)
            qt[...] = (made + bias).astype(BF)

    @pl.when(p.c == 1)
    def _():
        w.own_across(0)

        @pl.when(p.x == 0)
        def _():
            w.own_along(0)

    @pl.when((p.c == 0) & (p.x == 1))
    def _():
        w.own_across(0)

    @pl.when((p.c == 1) | (p.x == 1))
    def _():
        for i in (1, 2):
            w.own_across(i)

    acc[...] = jnp.zeros_like(acc)
    top[...] = jnp.full_like(top, FLOOR)
    mass[...] = jnp.zeros_like(mass)
    code, at = query_code(p, lengths, alive_row[...])
    scaled = (qt[...].astype(F32) * (HD ** -0.5)).astype(BF)

    def attend(d, core):
        bias = block_bias(p, lengths, window, d, core, code, at)
        keys = window[d, core, 0:ROWS, 0:SPAN]
        values_t = window[d, core, 0:ROWS, SPAN : 2 * SPAN].T
        for u in range(GROUPS):
            heads = slice(u * HD, (u + 1) * HD)
            score = nn(keys, head_rows(scaled, u)) + bias
            old = top[u : u + 1, :]
            new = jnp.maximum(old, jnp.max(score, axis=0, keepdims=True))
            weight = jnp.exp(score - new)
            fade = jnp.exp(old - new)
            top[u : u + 1, :] = new
            mass[u : u + 1, :] = mass[u : u + 1, :] * fade + jnp.sum(weight, axis=0, keepdims=True)
            acc[heads, :] = acc[heads, :] * fade + nn(values_t[heads, :], weight.astype(BF))

    def attend_chip(d):
        def body(core, carry):
            use = (p.chip - d >= 0) & ~((d == 0) & (core > p.c)) & ~((d == 4) & (core < p.c))

            @pl.when(use)
            def _():
                attend(d, core)

            return carry

        lax.fori_loop(0, 2, body, 0)

    def kv_in(d):
        @pl.when(p.chip - d >= 0)
        def _():
            got = window.at[d, p.c]
            remote(got, got, kv_send.at[d], kv_recv.at[d], p.sibling()).wait_recv()
            remote(got, got, kv_bsend.at[d], kv_brecv.at[d], p.sibling()).start()

    def kv_beside(d):
        @pl.when(p.chip - d >= 0)
        def _():
            got = window.at[d, 1 - p.c]
            remote(got, got, kv_bsend.at[d], kv_brecv.at[d], p.sibling()).wait_recv()

    kv_beside(0)
    kv_in(1)
    attend_chip(0)

    @pl.when((p.c == 1) & (p.x == 1))
    def _():
        w.nbr_on(0)

    kv_beside(1)
    kv_in(2)
    attend_chip(1)
    kv_beside(2)
    kv_in(3)
    attend_chip(2)
    kv_beside(3)
    kv_in(4)

    @pl.when((p.c == 1) & (p.x == 1))
    def _():
        w.own_along(0)

    @pl.when((p.c == 0) & (p.x == 1))
    def _():
        w.own_along(0)

    @pl.when((p.c == 1) | (p.x == 1))
    def _():
        for i in (1, 2):
            w.own_along(i)

    attend_chip(3)
    kv_beside(4)

    @pl.when(p.c == 1)
    def _():
        @pl.when(p.x == 0)
        def _():
            w.along_on(0, 0)

        @pl.when(p.x == 1)
        def _():
            w.along_on(1, 0)

    attend_chip(4)

    total = jnp.maximum(mass[...], 1e-30)
    lse_out[...] = top[...] + jnp.log(total)
    for u in range(GROUPS):
        heads = slice(u * HD, (u + 1) * HD)
        acc[heads, :] = acc[heads, :] / total[u : u + 1, :]
    ot_out[...] = acc[...]
    o_rows = acc[...].astype(BF).T

    @pl.when(p.c == 0)
    def _():
        w.beside_in(0, 0)

    def project(n, carry):
        cols = pl.ds(pl.multiple_of(n * 256, 256), 256)
        part[:, cols] = nn(o_rows, w.kind_columns(3, 1, cols)).astype(BF)
        return carry

    lax.fori_loop(0, WIDTH // 256, project, 0)
    scatter = scatter_copies(p, part, land, rs_send, rs_recv)
    for copy in scatter:
        copy.start()

    @pl.when((p.c == 0) & (p.x == 0))
    def _():
        w.nbr_on(0)

    @pl.when((p.c == 1) & (p.x == 0))
    def _():
        w.nbr_on(0)

    @pl.when((p.c == 1) | (p.x == 0))
    def _():
        for i in (1, 2):
            w.nbr_on(i)

    for copy in scatter:
        copy.wait()
    mine = pl.ds(pl.multiple_of(p.t * SHARD, SHARD), SHARD)
    summed = scatter_sum(p, part, land)
    hidden = tokens[mine, :].astype(F32) + alive_col[mine, :] * (summed + shifts[0:1, :])
    hidden_out[...] = hidden
    normed, _, _ = normalize(hidden, gains[1:2, :], shifts[3:4, :])
    whole[mine, :] = normed.astype(BF)
    gather = gather_copies(p, whole, ag_send, ag_recv)
    for copy in gather:
        copy.start()

    @pl.when((p.c == 1) & (p.x == 0))
    def _():
        w.along_on(1, 0)

    @pl.when((p.c == 1) & (p.x == 1))
    def _():
        w.along_on(0, 0)

    @pl.when((p.c == 0) & (p.x == 0))
    def _():
        w.along_on(1, 0)

    @pl.when((p.c == 0) & (p.x == 1))
    def _():
        w.along_on(0, 0)

    for i in (1, 2):
        @pl.when((p.c == 1) | (p.x == 1))
        def _():
            w.along_on(0, i)

        @pl.when((p.c == 1) | (p.x == 0))
        def _():
            w.along_on(1, i)

    for copy in gather:
        copy.wait()

    @pl.when(p.c == 0)
    def _():
        w.beside_in(0, 1)
        w.beside_in(0, 2)

    for i in range(3):
        w.beside_in(1, i)

    out_copies = [
        pltpu.make_async_copy(store, store_out, out_sem.at[0]),
        pltpu.make_async_copy(window, window_out, out_sem.at[1]),
        pltpu.make_async_copy(whole, low2_out, out_sem.at[2]),
        pltpu.make_async_copy(low1, low1_out, out_sem.at[3]),
        pltpu.make_async_copy(qt, qt_out, out_sem.at[4]),
    ]
    for copy in out_copies:
        copy.start()

    for n in range(4):
        pre = nt(w.kind_panels(4 + n), whole[...])
        at_bias = 2 * HD + n * HD
        pre = pre + jnp.concatenate([bias_t[at_bias : at_bias + HD, u : u + 1] for u in range(GROUPS)], axis=0)
        value, slope = gelu_parts(pre)
        d_act = nt(w.kind_panels(8 + n), dffn[...])
        low_value, low_grad = value.astype(BF), (d_act * slope).astype(BF)
        units = slice(n * SPAN, (n + 1) * SPAN)
        gt[units, :] = low_value
        dft[units, :] = low_grad
        g_rows[:, units] = low_value.T
        df_rows[:, units] = low_grad.T
    gt_out[...] = gt[...]
    dft_out[...] = dft[...]

    def feed(n, carry):
        cols = pl.ds(pl.multiple_of(n * 256, 256), 256)
        dn2_out[:, cols] = nn(df_rows[...], w.kind_columns(4, 4, cols)).astype(BF)
        ffn_out[:, cols] = nn(g_rows[...], w.kind_columns(8, 4, cols)).astype(BF)
        return carry

    lax.fori_loop(0, WIDTH // 256, feed, 0)

    for i in range(3):
        w.drain(i)
    mine_kv = window.at[0, p.c]
    for d in range(1, 5):
        @pl.when(p.chip + d < 8)
        def _():
            remote(mine_kv, mine_kv, kv_send.at[d], kv_recv.at[d], p.sibling()).wait_send()
    for d in range(5):
        @pl.when(p.chip - d >= 0)
        def _():
            remote(mine_kv, mine_kv, kv_bsend.at[d], kv_brecv.at[d], p.sibling()).wait_send()
    for copy in out_copies:
        copy.wait()


def forward_call(lengths, tokens, cotangent, alive_row, alive_col, panels, bias_t, gains, shifts):
    vmem = pl.BlockSpec(memory_space=pltpu.VMEM)
    anywhere = pl.BlockSpec(memory_space=pl.ANY)
    shape = jax.ShapeDtypeStruct
    dma = pltpu.SemaphoreType.DMA
    return pl.pallas_call(
        forward_kernel,
        in_specs=[pl.BlockSpec(memory_space=pltpu.SMEM)] + [vmem] * 8,
        out_specs=[anywhere, anywhere, anywhere, vmem, vmem, vmem, anywhere, vmem, vmem, vmem, vmem, anywhere],
        out_shape=[
            shape((ROWS, WIDTH), BF),
            shape((SPAN, ROWS), BF),
            shape((5, 2, EXT, 2 * SPAN), BF),
            shape((SPAN, ROWS), F32),
            shape((8, ROWS), F32),
            shape((SHARD, WIDTH), F32),
            shape((ROWS, WIDTH), BF),
            shape((UNITS, ROWS), BF),
            shape((UNITS, ROWS), BF),
            shape((ROWS, WIDTH), BF),
            shape((ROWS, WIDTH), BF),
            shape((16, 3, HD, WIDTH), BF),
        ],
        scratch_shapes=[
            pltpu.VMEM((16, 3, HD, WIDTH), BF),
            pltpu.VMEM((5, 2, EXT, 2 * SPAN), BF),
            pltpu.VMEM((ROWS, WIDTH), BF),
            pltpu.VMEM((SPAN, ROWS), BF),
            pltpu.VMEM((SPAN, ROWS), F32),
            pltpu.VMEM((8, ROWS), F32),
            pltpu.VMEM((8, ROWS), F32),
            pltpu.VMEM((ROWS, WIDTH), BF),
            pltpu.VMEM((7, SHARD, WIDTH), BF),
            pltpu.VMEM((ROWS, WIDTH), BF),
            pltpu.VMEM((ROWS, UNITS), BF),
            pltpu.VMEM((ROWS, UNITS), BF),
            pltpu.VMEM((UNITS, ROWS), BF),
            pltpu.VMEM((UNITS, ROWS), BF),
            pltpu.VMEM((ROWS, WIDTH), BF),
            dma((16, 3)), dma((3,)), dma((2, 3, 3)), dma((8, 3)),
            dma((5,)), dma((5,)), dma((5,)), dma((5,)),
            dma((7,)), dma((7,)), dma((7,)), dma((7,)), dma((5,)),
        ],
        compiler_params=pltpu.CompilerParams(
            collective_id=0, has_side_effects=True, vmem_limit_bytes=56 * 2**20
        ),
        name="layer_forward",
    )(lengths, tokens, cotangent, alive_row, alive_col, panels, bias_t, gains, shifts)


def times_t(left, right):
    return nt(left, right)


def inner_rows(left, right):
    return lax.dot_general(left, right, (((0,), (0,)), ((), ())), preferred_element_type=F32)


plain = nn


def norm_back(grad, unit, factor, gain):
    d_gain = jnp.sum(grad * unit, axis=0)
    d_shift = jnp.sum(grad, axis=0)
    d_unit = grad * gain
    d_in = factor * (
        d_unit
        - jnp.mean(d_unit, axis=-1, keepdims=True)
        - unit * jnp.mean(d_unit * unit, axis=-1, keepdims=True)
    )
    return (d_in, d_gain, d_shift)


def orthogonalize(moment):
    current = moment * lax.rsqrt(jnp.sum(moment * moment, axis=(1, 2), keepdims=True) + 1e-06)
    for sweep in range(NS_ITERS):
        gram = jnp.einsum("pij,pkj->pik", current, current, precision=HIGH)
        poly = NS_B * gram + NS_C * jnp.einsum("pij,pjk->pik", gram, gram, precision=HIGH)
        current = NS_A * current + jnp.einsum("pij,pjk->pik", poly, current, precision=HIGH)
    return current


def per_device(
    tokens, cotangent, exits, lengths, panels, panel_mom,
    unit_bias, unit_bias_mom, gains, gains_mom, vec_bias, vec_bias_mom,
):
    rows, width = tokens.shape
    groups, head_dim = GROUPS, HD
    total = rows * lax.axis_size("seq")
    scale = head_dim ** (-0.5)
    live = (exits >= LAYER).astype(F32)[:, None]
    alive = (exits >= LAYER).astype(jnp.int32)
    positions = lax.axis_index("seq") * rows + jnp.arange(rows, dtype=jnp.int32)
    ends = jnp.cumsum(lengths)
    segment = jnp.sum((positions[:, None] >= ends[None, :]).astype(jnp.int32), axis=1)
    block = math.gcd(total, 512)
    count = total // block
    begins = jnp.arange(count, dtype=jnp.int32) * block
    low1, qt, window, ot, lse, hidden32, low2, gt, dft, ffn_part, dn2_part, store = forward_call(
        lengths, tokens, cotangent, live.reshape(1, rows), live, panels, unit_bias.T, gains, vec_bias
    )
    core = lax.axis_index("seq") % 2
    mine_kv = lax.dynamic_index_in_dim(window[0], core, 0, keepdims=False)
    keys, values = mine_kv[:rows, :SPAN], mine_kv[:rows, SPAN:]
    query = qt.T
    q_heads = query.reshape(rows, groups, head_dim)
    log_total = lse[:groups]
    attn_full = ot.T.reshape(rows, groups, head_dim)
    attn_low = ot.T.astype(BF)
    stack = store.reshape(groups, 12, head_dim, width)
    w_query = stack[:, 0].reshape(groups * head_dim, width)
    w_key = stack[:, 1].reshape(groups * head_dim, width)
    w_value = stack[:, 2].reshape(groups * head_dim, width)
    w_out = stack[:, 3].reshape(groups * head_dim, width)
    x_full = tokens.astype(F32)
    _, unit1, factor1 = normalize(x_full, gains[0], vec_bias[2])
    hidden = lax.all_gather(hidden32, "tensor", axis=0, tiled=True)
    _, unit2, factor2 = normalize(hidden, gains[1], vec_bias[3])
    ffn_whole = lax.psum(ffn_part, "tensor").astype(F32)
    output = hidden + live * (ffn_whole + vec_bias[1])
    grad_out = cotangent.astype(F32)
    d_ffn = (live * grad_out).astype(BF)
    d_b2 = jnp.sum(d_ffn.astype(F32), axis=0)
    d_w_back = nn(gt, d_ffn).reshape(4, groups, head_dim, width).transpose(1, 0, 2, 3)
    d_b1 = jnp.sum(dft.astype(F32), axis=1).reshape(4, groups, head_dim).transpose(1, 0, 2)
    d_w_in = nn(dft, low2).reshape(4, groups, head_dim, width).transpose(1, 0, 2, 3)
    d_norm2 = lax.psum(dn2_part, "tensor").astype(F32)
    d_hidden_norm, d_gain2, d_shift2 = norm_back(d_norm2, unit2, factor2, gains[1])
    d_hidden = grad_out + d_hidden_norm
    d_branch = (live * d_hidden).astype(BF)
    d_bo = jnp.sum(d_branch.astype(F32), axis=0)
    d_w_out = inner_rows(attn_low, d_branch)
    d_attn = times_t(d_branch, w_out).astype(BF)
    d_heads = d_attn.reshape(rows, groups, head_dim)
    delta = jnp.einsum("qhe,qhe->hq", d_heads.astype(F32), attn_full)
    all_keys, all_values, all_seg, all_alive = (
        lax.all_gather(keys, "seq", axis=0, tiled=True),
        lax.all_gather(values, "seq", axis=0, tiled=True),
        lax.all_gather(segment, "seq", axis=0, tiled=True),
        lax.all_gather(alive, "seq", axis=0, tiled=True),
    )

    def back_block(d_query, blocked):
        k_blk, v_blk, s_blk, a_blk, begin = blocked
        k_pos = begin + jnp.arange(block, dtype=jnp.int32)
        allowed = (segment[:, None] == s_blk[None, :]) & (positions[:, None] >= k_pos[None, :])
        allowed = allowed & (alive[:, None] > 0) & (a_blk[None, :] > 0)
        k_h = k_blk.reshape(block, groups, head_dim)
        v_h = v_blk.reshape(block, groups, head_dim)
        score = jnp.einsum("qhe,khe->hqk", q_heads, k_h, preferred_element_type=F32) * scale
        prob = jnp.where(allowed[None], jnp.exp(score - log_total[:, :, None]), 0.0)
        d_val = jnp.einsum("hqk,qhe->khe", prob.astype(BF), d_heads, preferred_element_type=F32)
        d_prob = jnp.einsum("qhe,khe->hqk", d_heads, v_h, preferred_element_type=F32)
        d_score = (prob * (d_prob - delta[:, :, None])).astype(BF)
        d_query = d_query + jnp.einsum("hqk,khe->qhe", d_score, k_h, preferred_element_type=F32)
        d_key = jnp.einsum("hqk,qhe->khe", d_score, q_heads, preferred_element_type=F32)
        return (d_query, (d_key.reshape(block, SPAN), d_val.reshape(block, SPAN)))

    blocked_in = (
        all_keys.reshape(count, block, -1),
        all_values.reshape(count, block, -1),
        all_seg.reshape(count, block),
        all_alive.reshape(count, block),
        begins,
    )
    d_query, (d_key_all, d_val_all) = lax.scan(
        back_block, jnp.zeros((rows, groups, head_dim), F32), blocked_in
    )
    d_key_all = d_key_all.reshape(total, SPAN) * scale
    d_val_all = d_val_all.reshape(total, SPAN)
    d_key_mine, d_val_mine = (
        lax.psum_scatter(d_key_all.astype(BF), "seq", scatter_dimension=0, tiled=True).astype(F32),
        lax.psum_scatter(d_val_all.astype(BF), "seq", scatter_dimension=0, tiled=True).astype(F32),
    )
    d_q = (d_query.reshape(rows, SPAN) * scale).astype(BF)
    d_k = d_key_mine.astype(BF)
    d_v = d_val_mine.astype(BF)
    d_bq = jnp.sum(d_q.astype(F32), axis=0)
    d_bv = jnp.sum(d_v.astype(F32), axis=0)
    d_w_query = inner_rows(d_q, low1)
    d_w_key = inner_rows(d_k, low1)
    d_w_value = inner_rows(d_v, low1)
    d_norm1_part = plain(d_q, w_query) + plain(d_k, w_key) + plain(d_v, w_value)
    d_norm1 = lax.psum(d_norm1_part.astype(BF), "tensor").astype(F32)
    d_input_norm, d_gain1, d_shift1 = norm_back(d_norm1, unit1, factor1, gains[0])
    input_grad = d_hidden + d_input_norm
    grad_stack = jnp.concatenate(
        [
            d_w_query.reshape(groups, 1, head_dim, width),
            d_w_key.reshape(groups, 1, head_dim, width),
            d_w_value.reshape(groups, 1, head_dim, width),
            d_w_out.reshape(groups, 1, head_dim, width),
            d_w_in,
            d_w_back,
        ],
        axis=1,
    ).reshape(groups * 12, head_dim, width)
    unit_grad = jnp.concatenate(
        [
            d_bq.reshape(groups, head_dim),
            d_bv.reshape(groups, head_dim),
            d_b1.reshape(groups, 4 * head_dim),
        ],
        axis=1,
    )
    gain_grad = jnp.stack([d_gain1, d_gain2])
    shift_grad = jnp.stack([d_bo, d_b2, d_shift1, d_shift2])
    unit_sum, gain_sum, shift_sum = (
        lax.psum(unit_grad.astype(BF), "seq").astype(F32),
        lax.psum(gain_grad.astype(BF), "seq").astype(F32),
        lax.psum(shift_grad.astype(BF), "seq").astype(F32),
    )
    mine = lax.psum_scatter(grad_stack.astype(BF), "seq", scatter_dimension=0, tiled=True).astype(F32)
    moment = DECAY * panel_mom + mine
    direction = orthogonalize(moment)
    size_w = jnp.sum(panels * panels, axis=(1, 2), keepdims=True)
    size_u = jnp.sum(direction * direction, axis=(1, 2), keepdims=True)
    new_panels = panels - LR_MATRIX * jnp.sqrt(size_w) * lax.rsqrt(size_u + 1e-06) * direction
    unit_moment = DECAY * unit_bias_mom + unit_sum
    gains_moment = DECAY * gains_mom + gain_sum
    vec_moment = DECAY * vec_bias_mom + shift_sum
    return (
        output.astype(BF), input_grad, new_panels, moment,
        unit_bias - LR_VECTOR * unit_moment, unit_moment,
        gains - LR_VECTOR * gains_moment, gains_moment,
        vec_bias - LR_VECTOR * vec_moment, vec_moment,
    )


def solution(mesh):
    held = P(("tensor", "seq"), None, None)
    return jax.shard_map(
        per_device,
        mesh=mesh,
        in_specs=(
            P("seq", None), P("seq", None), P("seq"), P(), held, held,
            P("tensor", None), P("tensor", None), P(), P(), P(), P(),
        ),
        out_specs=(
            P("seq", None), P("seq", None), held, held,
            P("tensor", None), P("tensor", None), P(), P(), P(), P(),
        ),
        check_vma=False,
    )
```

time: 930 us -> 897 us (0.965)
  Pallas kernels: 0 us -> 115 us
  waiting for transfers between devices: 534 us -> 427 us
  matrix products: 123 us -> 74.7 us
  blocking collectives: 93.8 us -> 113 us
    pallas_call x0 -> x1, Pallas kernels: none -> 115 us  [forward_call(): pl.pallas_call(forward_kernel, in_specs=[pl.BlockSpec(memory_space=pltpu....]
    psum x3 -> x2, waiting for transfers between devices: 263 us -> 179 us  [the longest x1 90 us: per_device(): ffn_whole = lax.psum(ffn_part, 'tensor').astype(F32)]
    dot_general x54 -> x46, matrix products: 95.4 us -> 55.6 us  [the longest x5 13.4 us: nn(): return jnp.dot(left, right, preferred_element_type=F32)]
    all_gather x3, waiting for transfers between devices: 86.6 us -> 65 us  [the longest x1 35.6 us: per_device(): lax.all_gather(keys, 'seq', axis=0, tiled=True)]
    all_gather x2, blocking collectives: 35.5 us -> 46.6 us  [the longest x1 30 us: per_device(): lax.all_gather(segment, 'seq', axis=0, tiled=True)]
  transfers between devices with their start and end apart: 9 -> 8, of which waited for: 8 -> 8; matrix products, arithmetic and copies ran while one was open for 7% -> 6% of each run, Pallas kernels for 0% -> 0%
where the time goes in v1:
time: 897 us; the launch traced here: 887 us
  waiting for transfers between devices  427 us (48%)
  Pallas kernels  115 us (13%)
  blocking collectives  113 us (13%)
  local copies, waits for them, and re-layouts  87.1 us (10%)
  matrix products  74.7 us (8%)
  other arithmetic  53.1 us (6%)
  between operations  15 us (2%)
    pallas_call x1, Pallas kernels, forward_call(): pl.pallas_call(forward_kernel, in_specs=[pl.BlockSpec(memory_space=pltpu....  115 us
    psum x1, waiting for transfers between devices, per_device(): ffn_whole = lax.psum(ffn_part, 'tensor').astype(F32)  90 us
    psum x1, waiting for transfers between devices, per_device(): d_norm2 = lax.psum(dn2_part, 'tensor').astype(F32)  88.7 us
    psum x1, blocking collectives, per_device(): lax.psum(unit_grad.astype(BF), 'seq').astype(F32)  66.6 us
    reduce_scatter x1, waiting for transfers between devices, per_device(): lax.psum_scatter(grad_stack.astype(BF), 'seq', scatter_dimension=0, tiled...  65.2 us
    reduce_scatter x1, waiting for transfers between devices, per_device(): lax.psum_scatter(d_val_all.astype(BF), 'seq', scatter_dimension=0, tiled=...  63.2 us
    reduce_scatter x1, waiting for transfers between devices, per_device(): lax.psum_scatter(d_key_all.astype(BF), 'seq', scatter_dimension=0, tiled=...  53.5 us
    all_gather x1, waiting for transfers between devices, per_device(): lax.all_gather(keys, 'seq', axis=0, tiled=True)  35.6 us
  transfers between devices with their start and end apart: 8, of which 8 were waited for; matrix products, arithmetic and copies ran while one was open for 6% of the time, Pallas kernels for 0%

profile of v1, /device:TPU:0, one launch (start us, length us, event | category | flops | bytes accessed | tf_op | source)
XLA Modules:
  0.0 886.6 jit_solution(3027918876783590442)
XLA Ops:
  10.8 115.1 %layer_forward.1 = (bf16[256,2048]{1,0:T(8,128)(2,1)}, bf16[256,256]{1,0:T(8,128)(2,1)}, bf16[5,2,272,512]{3,2,1,0:T(8,128)(2,1)}, f32[256,256]{1,0:T(8,128)}, f...) custom-call(s32[4]{0:T(128)} %lengths.1, ...), custom_call_target="tpu_custom_call" | custom-call | tf_op jit(solution)/shard_map/layer_forward/pallas_call | solution.py:556
  130.7 30.0 %all-gather = s32[16,1,256]{2,1,0:T(1,128)S(1)} all-gather(s32[1,1,256]{2,1,0:T(1,128)} %bitcast.11), channel_id=1, replica_groups=mesh['seq'=16,'tensor'=8] {'seq'}, dimensions={0}, use_global_device_ids=true | all-gather | bytes 17408 | tf_op jit(solution)/shard_map/all_gather | solution.py:689
  161.4 16.6 %all-gather.1 = s32[16,1,256]{2,1,0:T(1,128)S(1)} all-gather(s32[1,1,256]{2,1,0:T(1,128)} %bitcast.12), channel_id=1, replica_groups=mesh['seq'=16,'tensor'=8] {'seq'}, dimensions={0}, use_global_device_ids=true | all-gather | bytes 17408 | tf_op jit(solution)/shard_map/all_gather | solution.py:690
  179.8 4.4 fusion.49
  184.2 3.7 all-gather.6.cloned.1.call-done
  190.5 88.7 %all-reduce.5.cloned.1.call-done = bf16[256,2048]{1,0:T(8,128)(2,1)} async-done(((bf16[256,2048]{1,0:T(8,128)(2,1)}), bf16[256,2048]{1,0:T(8,128)(2,1)}) %all-reduce.5.cloned.1.call-update) | async-done | bytes 1048592 | tf_op jit(solution)/shard_map/psum | solution.py:677
  279.1 2.8 fusion.26
  282.0 3.2 fusion.47
  287.2 25.7 %all-gather.10.cloned.1.call-done = bf16[4096,256]{1,0:T(8,128)(2,1)} async-done(((bf16[256,256]{1,0:T(8,128)(2,1)}), bf16[4096,256]{1,0:T(8,128)(2,1)}) %all-gather.10.cloned.1.call-update) | async-done | bytes 2097168 | tf_op jit(solution)/shard_map/all_gather | solution.py:688
  312.9 35.6 %all-gather.8.cloned.1.call-done = bf16[4096,256]{1,0:T(8,128)(2,1)} async-done(((bf16[256,256]{1,0:T(8,128)(2,1)}), bf16[4096,256]{1,0:T(8,128)(2,1)}) %all-gather.8.cloned.1.call-update) | async-done | bytes 2097168 | tf_op jit(solution)/shard_map/all_gather | solution.py:687
  348.5 125.0 %while.15 = (s32[]{:T(128)}, f32[256,4,64]{0,2,1:T(8,128)}, f32[8,512,256]{2,1,0:T(8,128)}, bf16[8,512,256]{2,1,0:T(8,128)(2,1)}, bf16[8,512,256]{2,1,0:T(8,128)...) while((s32[]{:T(128)}, f32[256,4,64]{0,2,1:T(8,128)}, ...), condition=%wide.region_11.12_spmd.clone, body=%wide.region_10.11_spmd.clone.sunk | while | flops 340002304 | bytes 19688200 | solution.py:716
  473.5 4.0 multiply_convert_fusion
  478.9 3.2 convolution_convert_fusion.1
  482.1 3.3 convolution_convert_fusion
  488.5 53.5 %reduce-scatter.4.cloned.1.call-done = bf16[256,256]{1,0:T(8,128)(2,1)} async-done(((bf16[4096,256]{1,0:T(8,128)(2,1)}), bf16[256,256]{1,0:T(8,128)(2,1)}) %reduce-scatter.4.cloned.1.call-update) | async-done | bytes 131088 | tf_op jit(solution)/shard_map/reduce_scatter | solution.py:722
  542.1 2.4 convolution_add_fusion.1
  544.5 63.2 %reduce-scatter.6.cloned.1.call-done = bf16[256,256]{1,0:T(8,128)(2,1)} async-done(((bf16[4096,256]{1,0:T(8,128)(2,1)}), bf16[256,256]{1,0:T(8,128)(2,1)}) %reduce-scatter.6.cloned.1.call-update) | async-done | bytes 131088 | tf_op jit(solution)/shard_map/reduce_scatter | solution.py:723
  607.7 2.7 fusion.12
  618.4 5.1 copy.68
  626.8 90.0 %all-reduce.7.cloned.1.call-done = (bf16[256,2048]{1,0:T(8,128)(2,1)}, bf16[256,2048]{1,0:T(8,128)(2,1)}) async-done(((bf16[256,2048]{1,0:T(8,128)(2,1)}, bf16[256,2048]{1,0:T(8,128)(2,1)}), (bf16[256,2048]{1,0:T(8,128)(2,1)}, bf16[256,2048]{1,0:T(8,128)(2,1)})) %all-reduce.7.cloned.1.call-update) | async-done | bytes 2097168 | tf_op jit(solution)/shard_map/psum | solution.py:669
  718.2 2.2 fusion.28
  720.5 66.6 %all-reduce = (bf16[4,384]{1,0:T(4,128)(2,1)S(1)}, bf16[2,2048]{1,0:T(2,128)(2,1)S(1)}, bf16[4,2048]{1,0:T(4,128)(2,1)S(1)}) all-reduce(bf16[4,384]{1,0:T(4,128)(2,1)S(1)} %pad_maximum_fusion.2, bf16[2,2048]{1,0:T(2,128)(2,1)S(1)} %pad_maximum_fusion.1, ...), channel_id=1, replica_groups=mesh['seq'=16,'tensor'=8] {'seq'}, use_global_device_ids=true, to_apply=%region_24.25 | all-reduce | flops 13824 | bytes 55296 | tf_op jit(solution)/shard_map/psum | solution.py:759
  789.0 2.7 add_convert_fusion
  793.9 65.2 %reduce-scatter.8.cloned.1.call-done = bf16[3,64,2048]{2,1,0:T(8,128)(2,1)} async-done(((bf16[48,64,2048]{2,1,0:T(8,128)(2,1)}), bf16[3,64,2048]{2,1,0:T(8,128)(2,1)}) %reduce-scatter.8.cloned.1.call-update) | async-done | bytes 786448 | tf_op jit(solution)/shard_map/reduce_scatter | solution.py:763
  (371 shorter events, 181.2 us)
Async XLA Ops:
  7.2 180.7 %all-gather.6.cloned.1.call-start = ((), (), s32[]{:S(2)}) async-start(), calls=%async_computation.3 | async-start | bytes 2359296 | tf_op jit(solution)/shard_map/all_gather | solution.py:667
  125.9 3.4 copy-start.44
  125.9 4.0 copy-start.45
  125.9 53.3 %copy-start.31 = (f32[2,2048]{1,0:T(2,128)S(1)}, f32[2,2048]{1,0:T(2,128)}, u32[]{:S(2)}) copy-start(f32[2,2048]{1,0:T(2,128)} %gains.1) | copy-start | bytes 49156
  125.9 153.2 %all-reduce.5.cloned.1.call-start = ((), (), s32[]{:S(2)}) async-start(), calls=%async_computation.4 | async-start | bytes 2097152 | tf_op jit(solution)/shard_map/psum | solution.py:677
  126.7 186.2 %all-gather.10.cloned.1.call-start = ((), (), s32[]{:S(2)}) async-start(), calls=%async_computation.6 | async-start | bytes 2228224 | tf_op jit(solution)/shard_map/all_gather | solution.py:688
  128.6 219.9 %all-gather.8.cloned.1.call-start = ((), (), s32[]{:S(2)}) async-start(), calls=%async_computation.5 | async-start | bytes 2228224 | tf_op jit(solution)/shard_map/all_gather | solution.py:687
  129.2 412.9 %reduce-scatter.4.cloned.1.call-start = ((), (), s32[]{:S(2)}) async-start(), calls=%async_computation.7 | async-start | bytes 2228224 | tf_op jit(solution)/shard_map/reduce_scatter | solution.py:722
  190.5 91.5 %copy-start.8 = (bf16[256,2048]{1,0:T(8,128)(2,1)S(1)}, bf16[256,2048]{1,0:T(8,128)(2,1)}, u32[]{:S(2)}) copy-start(bf16[256,2048]{1,0:T(8,128)(2,1)} %cotangent.1) | copy-start | bytes 3145732
  190.5 91.5 %copy-start.34 = (f32[256]{0:T(256)S(1)}, f32[256]{0:T(256)}, u32[]{:S(2)}) copy-start(f32[256]{0:T(256)} %copy-done.33) | copy-start | bytes 3076
  282.0 4.2 copy-start.20
  282.0 4.2 copy-start.26
  477.5 130.2 %reduce-scatter.6.cloned.1.call-start = ((), (), s32[]{:S(2)}) async-start(), calls=%async_computation.8 | async-start | bytes 2228224 | tf_op jit(solution)/shard_map/reduce_scatter | solution.py:723
  478.1 238.7 %all-reduce.7.cloned.1.call-start = ((), (), s32[]{:S(2)}) async-start(), calls=%async_computation.10 | async-start | bytes 4194304 | tf_op jit(solution)/shard_map/psum | solution.py:669
  482.1 3.4 copy-start.11
  610.5 248.6 %reduce-scatter.8.cloned.1.call-start = ((), (), s32[]{:S(2)}) async-start(), calls=%async_computation.9 | async-start | bytes 13369344 | tf_op jit(solution)/shard_map/reduce_scatter | solution.py:763
  625.8 92.4 %copy-start.32 = (f32[1,2048]{1,0:T(1,128)S(1)}, f32[1,2048]{1,0:T(1,128)}, u32[]{:S(2)}) copy-start(f32[1,2048]{1,0:T(1,128)} %get-tuple-element.305) | copy-start | bytes 24580
  626.0 161.1 %copy-start.37 = (f32[4,384]{1,0:T(4,128)S(1)}, f32[4,384]{1,0:T(4,128)}, u32[]{:S(2)}) copy-start(f32[4,384]{1,0:T(4,128)} %param.20) | copy-start | bytes 18436
  626.1 161.1 %copy-start.43 = (f32[4,384]{1,0:T(4,128)S(1)}, f32[4,384]{1,0:T(4,128)}, u32[]{:S(2)}) copy-start(f32[4,384]{1,0:T(4,128)} %param.21) | copy-start | bytes 18436
  626.1 161.7 %copy-start.42 = (f32[2,2048]{1,0:T(2,128)S(1)}, f32[2,2048]{1,0:T(2,128)}, u32[]{:S(2)}) copy-start(f32[2,2048]{1,0:T(2,128)} %param.23) | copy-start | bytes 49156
  626.1 162.3 %copy-start.36 = (f32[4,2048]{1,0:T(4,128)S(1)}, f32[4,2048]{1,0:T(4,128)}, u32[]{:S(2)}) copy-start(f32[4,2048]{1,0:T(4,128)} %param.25) | copy-start | bytes 98308
  626.5 162.5 %copy-start.1 = (f32[256,2048]{1,0:T(8,128)S(1)}, f32[256,2048]{1,0:T(8,128)}, u32[]{:S(2)}) copy-start(f32[256,2048]{1,0:T(8,128)} %all-gather.6.cloned.1.call-done) | copy-start | bytes 6291460
  791.7 67.3 %copy-start.23 = (f32[3,64,2048]{2,1,0:T(8,128)S(1)}, f32[3,64,2048]{2,1,0:T(8,128)}, u32[]{:S(2)}) copy-start(f32[3,64,2048]{2,1,0:T(8,128)} %param.19) | copy-start | bytes 4718596
  860.6 3.6 copy-start.7
  (44 other events, 79.6 us)
Sparse Core Ops, SparseCore 0:
  126.0 61.7 all-gather.5
  190.4 88.7 all-reduce.4
  280.9 32.0 all-gather.9
  314.5 33.9 all-gather.7
  477.6 64.4 reduce-scatter.3
  544.9 62.7 reduce-scatter.5
  610.9 105.8 all-reduce.6
  719.2 139.7 reduce-scatter.7

commit v2 on v1

--- a/solution.py
+++ b/solution.py
@@ -247,7 +247,8 @@
 
 def forward_kernel(
     lengths, tokens, cotangent, alive_row, alive_col, panels, bias_t, gains, shifts,
-    low1_out, qt_out, window_out, ot_out, lse_out, hidden_out, low2_out, gt_out, dft_out, ffn_out, dn2_out, store_out,
+    low1_out, qt_out, window_out, ot_out, lse_out, hidden_out, low2_out, gt_out, dft_out, ffn_out, dn2_out, proj_out,
+    dffn_out, unit_out,
     store, window, low1, qt, acc, top, mass, part, land, whole, g_rows, df_rows, dft, gt, dffn,
     w_recv, w_across, w_along, w_beside, kv_send, kv_recv, kv_bsend, kv_brecv, rs_send, rs_recv, ag_send, ag_recv, out_sem,
 ):
@@ -501,12 +502,15 @@
         w.beside_in(1, i)
 
     out_copies = [
-        pltpu.make_async_copy(store, store_out, out_sem.at[0]),
+        pltpu.make_async_copy(dffn, dffn_out, out_sem.at[0]),
         pltpu.make_async_copy(window, window_out, out_sem.at[1]),
         pltpu.make_async_copy(whole, low2_out, out_sem.at[2]),
         pltpu.make_async_copy(low1, low1_out, out_sem.at[3]),
         pltpu.make_async_copy(qt, qt_out, out_sem.at[4]),
     ]
+    for u in range(GROUPS):
+        out_copies.append(pltpu.make_async_copy(store.at[4 * u], proj_out.at[u, 0:3], out_sem.at[5 + 2 * u]))
+        out_copies.append(pltpu.make_async_copy(store.at[4 * u + 1, 0], proj_out.at[u, 3], out_sem.at[6 + 2 * u]))
     for copy in out_copies:
         copy.start()
 
@@ -521,7 +525,11 @@
         gt[units, :] = low_value
         dft[units, :] = low_grad
         g_rows[:, units] = low_value.T
-        df_rows[:, units] = low_grad.T
+        turned = low_grad.T
+        df_rows[:, units] = turned
+        unit_out[2 + n : 3 + n, :] = jnp.sum(turned.astype(F32), axis=0, keepdims=True)
+    unit_out[0:2, :] = jnp.zeros((2, SPAN), F32)
+    unit_out[6:8, :] = jnp.zeros((2, SPAN), F32)
     gt_out[...] = gt[...]
     dft_out[...] = dft[...]
 
@@ -556,7 +564,7 @@
     return pl.pallas_call(
         forward_kernel,
         in_specs=[pl.BlockSpec(memory_space=pltpu.SMEM)] + [vmem] * 8,
-        out_specs=[anywhere, anywhere, anywhere, vmem, vmem, vmem, anywhere, vmem, vmem, vmem, vmem, anywhere],
+        out_specs=[anywhere, anywhere, anywhere, vmem, vmem, vmem, anywhere, vmem, vmem, vmem, vmem, anywhere, anywhere, vmem],
         out_shape=[
             shape((ROWS, WIDTH), BF),
             shape((SPAN, ROWS), BF),
@@ -569,7 +577,9 @@
             shape((UNITS, ROWS), BF),
             shape((ROWS, WIDTH), BF),
             shape((ROWS, WIDTH), BF),
-            shape((16, 3, HD, WIDTH), BF),
+            shape((GROUPS, 4, HD, WIDTH), BF),
+            shape((ROWS, WIDTH), BF),
+            shape((8, SPAN), F32),
         ],
         scratch_shapes=[
             pltpu.VMEM((16, 3, HD, WIDTH), BF),
@@ -589,7 +599,7 @@
             pltpu.VMEM((ROWS, WIDTH), BF),
             dma((16, 3)), dma((3,)), dma((2, 3, 3)), dma((8, 3)),
             dma((5,)), dma((5,)), dma((5,)), dma((5,)),
-            dma((7,)), dma((7,)), dma((7,)), dma((7,)), dma((5,)),
+            dma((7,)), dma((7,)), dma((7,)), dma((7,)), dma((13,)),
         ],
         compiler_params=pltpu.CompilerParams(
             collective_id=0, has_side_effects=True, vmem_limit_bytes=56 * 2**20
@@ -598,179 +608,564 @@
     )(lengths, tokens, cotangent, alive_row, alive_col, panels, bias_t, gains, shifts)
 
 
-def times_t(left, right):
-    return nt(left, right)
-
-
-def inner_rows(left, right):
-    return lax.dot_general(left, right, (((0,), (0,)), ((), ())), preferred_element_type=F32)
-
-
-plain = nn
+def head_columns(values, head):
+    owner = lax.broadcasted_iota(jnp.int32, values.shape, 1) // HD
+    return jnp.where(owner == head, values, jnp.zeros_like(values))
 
 
 def norm_back(grad, unit, factor, gain):
-    d_gain = jnp.sum(grad * unit, axis=0)
-    d_shift = jnp.sum(grad, axis=0)
+    d_gain = jnp.sum(grad * unit, axis=0, keepdims=True)
+    d_shift = jnp.sum(grad, axis=0, keepdims=True)
     d_unit = grad * gain
     d_in = factor * (
         d_unit
         - jnp.mean(d_unit, axis=-1, keepdims=True)
         - unit * jnp.mean(d_unit * unit, axis=-1, keepdims=True)
     )
-    return (d_in, d_gain, d_shift)
-
-
-def orthogonalize(moment):
-    current = moment * lax.rsqrt(jnp.sum(moment * moment, axis=(1, 2), keepdims=True) + 1e-06)
+    return d_in, d_gain, d_shift
+
+
+class PanelSums:
+    def __init__(self, place, grads, pair, line, last, result, sems):
+        self.p, self.grads = place, grads
+        self.pair, self.line, self.last, self.result = pair, line, last, result
+        self.pair_send, self.pair_recv, self.line_send, self.line_recv, self.last_send, self.last_recv = sems
+
+    def kind(self, k):
+        return (k // 2 + self.p.x) % 2
+
+    def pair_copy(self, u, k, i):
+        return remote(
+            self.grads.at[4 * u + k, i],
+            self.pair.at[2 * u + k // 2, i],
+            self.pair_send.at[2 * u + k // 2, i],
+            self.pair_recv.at[2 * u + k // 2, i],
+            self.p.sibling(),
+        )
+
+    def to_pair(self, k, i):
+        @pl.when(self.p.c != k % 2)
+        def _():
+            for u in range(GROUPS):
+                self.pair_copy(u, k, i).start()
+
+    def line_copy(self, n, k, i):
+        head = (self.p.z + Z_STEPS[n]) % 4
+        kind = self.kind(k)
+        return remote(
+            self.grads.at[4 * head + k, i],
+            self.line.at[n, kind, i],
+            self.line_send.at[n, kind, i],
+            self.line_recv.at[n, kind, i],
+            self.p.along(Z_STEPS[n]),
+        )
+
+    def pair_add(self, k, i):
+        @pl.when(self.p.c == k % 2)
+        def _():
+            def add(step, carry):
+                u, rows = step // 4, pl.ds(pl.multiple_of((step % 4) * 16, 16), 16)
+                self.grads[4 * u + k, i, rows, :] = (
+                    self.grads[4 * u + k, i, rows, :].astype(F32)
+                    + self.pair[2 * u + k // 2, i, rows, :].astype(F32)
+                ).astype(BF)
+                return carry
+
+            for u in range(GROUPS):
+                self.pair_copy(u, k, i).wait_recv()
+            lax.fori_loop(0, 4 * GROUPS, add, 0)
+            for n in range(3):
+                self.line_copy(n, k, i).start()
+
+    def across_copy(self, k, i):
+        return remote(
+            self.grads.at[4 * self.p.z + k, i],
+            self.last.at[i],
+            self.last_send.at[i],
+            self.last_recv.at[i],
+            self.p.across(),
+        )
+
+    def line_add(self, k, i):
+        kind = self.kind(k)
+
+        @pl.when(self.p.c == k % 2)
+        def _():
+            for n in range(3):
+                self.line_copy(n, k, i).wait_recv()
+
+            def add(step, carry):
+                rows = pl.ds(pl.multiple_of(step * 16, 16), 16)
+                total = self.grads[4 * self.p.z + k, i, rows, :].astype(F32)
+                for n in range(3):
+                    total = total + self.line[n, kind, i, rows, :].astype(F32)
+                self.grads[4 * self.p.z + k, i, rows, :] = total.astype(BF)
+
+                @pl.when(self.p.x == k // 2)
+                def _():
+                    self.result[i, rows, :] = total
+
+                return carry
+
+            lax.fori_loop(0, HD // 16, add, 0)
+
+            @pl.when(self.p.x != k // 2)
+            def _():
+                self.across_copy(k, i).start()
+
+    def last_add(self, i):
+        own = 2 * self.p.x + self.p.c
+        self.across_copy(own, i).wait_recv()
+        self.result[i] = self.result[i] + self.last[i].astype(F32)
+
+    def drain(self):
+        for k in range(4):
+            for i in range(3):
+                @pl.when(self.p.c != k % 2)
+                def _():
+                    for u in range(GROUPS):
+                        self.pair_copy(u, k, i).wait_send()
+
+                @pl.when(self.p.c == k % 2)
+                def _():
+                    for n in range(3):
+                        self.line_copy(n, k, i).wait_send()
+
+                    @pl.when(self.p.x != k // 2)
+                    def _():
+                        self.across_copy(k, i).wait_send()
+
+
+def backward_kernel(
+    lengths, alive_row, alive_col, gains, shifts, dn2_part, gt, dft, ot, lse, hidden, unit_rows, qt,
+    tokens_any, cot_any, dffn_any, low2_any, low1_any, window_any, proj_any, ffn_any,
+    out_any, grad_any, result, vec_out, unit_out,
+    grads, pair, line, last, window, d_kv, kv_pair, kv_far, dffn, low2, low1, proj, ffn_part, x_mine, cot_mine,
+    branch, out_whole, in_whole, dn1_part, land, q_rows, q_cols, do_rows, do_cols, delta, dqt, dkv_sum, d_hidden,
+    bank, bank_land, small, small_pair, small_all, bank_back,
+    rs_send, rs_recv, ag_send, ag_recv, pair_send, pair_recv, line_send, line_recv, last_send, last_recv,
+    kv_bsend, kv_brecv, kv_send, kv_recv, v1_send, v1_recv, v2_send, v2_recv, v3_send, v3_recv, v4_send, v4_recv,
+    load_sem, out_sem,
+):
+    p = Place()
+    sums = PanelSums(
+        p, grads, pair, line, last, result,
+        (pair_send, pair_recv, line_send, line_recv, last_send, last_recv),
+    )
+    mine = pl.ds(pl.multiple_of(p.t * SHARD, SHARD), SHARD)
+    sources = [
+        (dffn_any, dffn), (low2_any, low2), (tokens_any.at[mine], x_mine), (cot_any.at[mine], cot_mine),
+        (proj_any, proj), (window_any, window), (low1_any, low1), (ffn_any, ffn_part),
+    ]
+    loads = [pltpu.make_async_copy(a, b, load_sem.at[n]) for n, (a, b) in enumerate(sources)]
+    for load in loads:
+        load.start()
+    p.greet()
+    first_scatter = scatter_copies(p, dn2_part, land.at[0], rs_send.at[0], rs_recv.at[0])
+    for copy in first_scatter:
+        copy.start()
+
+    def kinds_grad(j, left, right):
+        def tile(n, carry):
+            cols = pl.ds(pl.multiple_of(n * 256, 256), 256)
+            made = nn(left, right[:, cols]).astype(BF)
+            for u in range(GROUPS):
+                grads[4 * u + j // 3, j % 3, :, cols] = made[u * HD : (u + 1) * HD]
+            return carry
+
+        lax.fori_loop(0, WIDTH // 256, tile, 0)
+
+    loads[0].wait()
+    loads[1].wait()
+    for n in (0, 1, 2, 3):
+        kinds_grad(8 + n, gt[n * SPAN : (n + 1) * SPAN, :], dffn)
+        sums.to_pair((8 + n) // 3, (8 + n) % 3)
+    for n in (2, 3, 0, 1):
+        kinds_grad(4 + n, dft[n * SPAN : (n + 1) * SPAN, :], low2)
+        sums.to_pair((4 + n) // 3, (4 + n) % 3)
+
+    loads[2].wait()
+    loads[3].wait()
+    live = alive_col[mine, :]
+    grad_out = cot_mine[...].astype(F32)
+    _, unit2, factor2 = normalize(hidden[...], gains[1:2, :], shifts[3:4, :])
+    for copy in first_scatter:
+        copy.wait()
+    d_norm2 = scatter_sum(p, dn2_part, land.at[0])
+    d_in, d_gain2, d_shift2 = norm_back(d_norm2, unit2, factor2, gains[1:2, :])
+    d_hidden[...] = grad_out + d_in
+    d_branch = (live * d_hidden[...]).astype(BF)
+    branch[mine, :] = d_branch
+    first_gather = gather_copies(p, branch, ag_send.at[0], ag_recv.at[0])
+    for copy in first_gather:
+        copy.start()
+
+    def to_bank(row, values):
+        for n in range(8):
+            bank[n, row : row + 1, :] = values[:, n * 256 : (n + 1) * 256]
+
+    to_bank(1, d_gain2)
+    to_bank(2, jnp.sum(d_branch.astype(F32), axis=0, keepdims=True))
+    to_bank(3, jnp.sum(live * grad_out, axis=0, keepdims=True))
+    to_bank(5, d_shift2)
+    to_bank(6, jnp.zeros((1, WIDTH), F32))
+    to_bank(7, jnp.zeros((1, WIDTH), F32))
+
+    early = ((3, 0), (3, 1), (3, 2), (2, 2), (2, 0), (2, 1), (1, 1), (1, 2))
+    for k, i in early:
+        sums.pair_add(k, i)
+
+    loads[4].wait()
+    loads[5].wait()
+    scaled = (qt[...].astype(F32) * (HD ** -0.5)).astype(BF)
+    scaled_rows = scaled.T
+    for u in range(GROUPS):
+        q_rows[u] = head_rows(scaled, u)
+        q_cols[u] = head_columns(scaled_rows, u)
+    dqt[...] = jnp.zeros_like(dqt)
+    dkv_sum[...] = jnp.zeros_like(dkv_sum)
+    code, at = query_code(p, lengths, alive_row[...])
+
+    for copy in first_gather:
+        copy.wait()
+    w_out = jnp.concatenate([proj[u, 3] for u in range(GROUPS)], axis=0)
+    do_t = nt(w_out, branch[...]).astype(BF)
+    do_turned = do_t.T
+    for u in range(GROUPS):
+        heads = slice(u * HD, (u + 1) * HD)
+        do_rows[u] = head_rows(do_t, u)
+        do_cols[u] = head_columns(do_turned, u)
+        delta[u : u + 1, :] = jnp.sum(do_t[heads, :].astype(F32) * ot[heads, :], axis=0, keepdims=True)
+    loads[7].wait()
+    out_scatter = scatter_copies(p, ffn_part, land.at[1], rs_send.at[1], rs_recv.at[1])
+    for copy in out_scatter:
+        copy.start()
+    kinds_grad(3, ot[...].astype(BF), branch)
+    sums.to_pair(1, 0)
+
+    def kv_pair_copy(d):
+        return remote(d_kv.at[d, 1 - p.c], kv_pair.at[d], kv_bsend.at[d], kv_brecv.at[d], p.sibling())
+
+    def kv_far_copy(d):
+        return remote(d_kv.at[d, p.c], kv_far.at[d], kv_send.at[d], kv_recv.at[d], p.chip_at(-d))
+
+    def finish(d):
+        @pl.when(p.chip - d >= 0)
+        def _():
+            @pl.when(((p.c == 0) & (d <= 3)) | ((p.c == 1) & (d >= 1)))
+            def _():
+                kv_pair_copy(d).wait_recv()
+                d_kv[d, p.c] = (d_kv[d, p.c].astype(F32) + kv_pair[d].astype(F32)).astype(BF)
+
+            @pl.when(d >= 1)
+            def _():
+                kv_far_copy(d).start()
+
+    def block_back(step, carry):
+        d = 4 - step // 2
+        core = (1 - p.c + step) % 2
+        use = (p.chip - d >= 0) & ~((d == 0) & (core > p.c)) & ~((d == 4) & (core < p.c))
+
+        @pl.when(use)
+        def _():
+            bias = block_bias(p, lengths, window, d, core, code, at)
+            keys = window[d, core, 0:ROWS, 0:SPAN]
+            values = window[d, core, 0:ROWS, SPAN : 2 * SPAN]
+            keys_t = keys.T
+            d_key = jnp.zeros((ROWS, SPAN), F32)
+            d_value = jnp.zeros((ROWS, SPAN), F32)
+            for u in range(GROUPS):
+                heads = slice(u * HD, (u + 1) * HD)
+                prob = jnp.exp(nn(keys, q_rows[u]) + bias - lse[u : u + 1, :])
+                d_prob = nn(values, do_rows[u])
+                d_score = (prob * (d_prob - delta[u : u + 1, :])).astype(BF)
+                d_value = d_value + nn(prob.astype(BF), do_cols[u])
+                d_key = d_key + nn(d_score, q_cols[u])
+                dqt[heads, :] = dqt[heads, :] + nn(keys_t[heads, :], d_score)
+            d_kv[d, core, :, 0:SPAN] = d_key.astype(BF)
+            d_kv[d, core, :, SPAN : 2 * SPAN] = d_value.astype(BF)
+
+            @pl.when(core != p.c)
+            def _():
+                kv_pair_copy(d).start()
+
+        @pl.when((step % 2 == 1) & (step > 1))
+        def _():
+            finish(d + 1)
+
+        return carry
+
+    lax.fori_loop(0, 10, block_back, 0)
+    finish(0)
+    sums.pair_add(1, 0)
+
+    dq_t = (dqt[...] * (HD ** -0.5)).astype(BF)
+    dq = dq_t.T
+    small[8:16, :] = unit_rows[...]
+    small[8:9, :] = jnp.sum(dq.astype(F32), axis=0, keepdims=True)
+    loads[6].wait()
+    kinds_grad(0, dq_t, low1)
+    sums.to_pair(0, 0)
+
+    for copy in out_scatter:
+        copy.wait()
+    summed = scatter_sum(p, ffn_part, land.at[1])
+    out_whole[mine, :] = (hidden[...] + live * (summed + shifts[1:2, :])).astype(BF)
+
+    dkv_sum[...] = d_kv[0, p.c].astype(F32)
+    for d in (1, 2, 3, 4):
+        @pl.when(p.chip + d < 8)
+        def _():
+            kv_far_copy(d).wait_recv()
+            dkv_sum[...] = dkv_sum[...] + kv_far[d].astype(F32)
+
+    dkv = dkv_sum[...].astype(BF)
+    dkv_t = dkv.T
+    small[9:10, :] = jnp.sum(dkv[:, SPAN:].astype(F32), axis=0, keepdims=True)
+
+    def norm1_part(n, carry):
+        cols = pl.ds(pl.multiple_of(n * 256, 256), 256)
+        total = jnp.zeros((ROWS, 256), F32)
+        for i, left in enumerate((dq, dkv[:, :SPAN], dkv[:, SPAN:])):
+            total = total + nn(left, jnp.concatenate([proj[u, i, :, cols] for u in range(GROUPS)], axis=0))
+        dn1_part[:, cols] = total.astype(BF)
+        return carry
+
+    lax.fori_loop(0, WIDTH // 256, norm1_part, 0)
+    last_scatter = scatter_copies(p, dn1_part, land.at[2], rs_send.at[2], rs_recv.at[2])
+    for copy in last_scatter:
+        copy.start()
+    kinds_grad(1, dkv_t[:SPAN], low1)
+    sums.to_pair(0, 1)
+    kinds_grad(2, dkv_t[SPAN:], low1)
+    sums.to_pair(0, 2)
+    for i in range(3):
+        sums.pair_add(0, i)
+    out_gather = gather_copies(p, out_whole, ag_send.at[1], ag_recv.at[1])
+    for copy in out_gather:
+        copy.start()
+    for k, i in early:
+        sums.line_add(k, i)
+    sums.line_add(1, 0)
+
+    _, unit1, factor1 = normalize(x_mine[...].astype(F32), gains[0:1, :], shifts[2:3, :])
+    for copy in last_scatter:
+        copy.wait()
+    d_norm1 = scatter_sum(p, dn1_part, land.at[2])
+    d_in, d_gain1, d_shift1 = norm_back(d_norm1, unit1, factor1, gains[0:1, :])
+    in_whole[mine, :] = (d_hidden[...] + d_in).astype(BF)
+    last_gather = gather_copies(p, in_whole, ag_send.at[2], ag_recv.at[2])
+    for copy in last_gather:
+        copy.start()
+    to_bank(0, d_gain1)
+    to_bank(4, d_shift1)
+
+    slices = []
+    for n, (dy, dx) in enumerate(T_STEPS):
+        to = p.tensor_at(dy, dx)
+        slices.append(remote(bank.at[to], bank_land.at[n], v1_send.at[n], v1_recv.at[n], {"tensor": to}))
+    for copy in slices:
+        copy.start()
+    for copy in slices:
+        copy.wait()
+    total = bank[p.t]
+    for n in range(len(T_STEPS)):
+        total = total + bank_land[n]
+    small[0:8, :] = total
+    pair_small = remote(small, small_pair, v2_send, v2_recv, p.sibling())
+    pair_small.start()
+
+    for i in range(3):
+        sums.line_add(0, i)
+
+    pair_small.wait()
+    here = p.z * 2 + p.x
+    small_all[here] = small[...] + small_pair[...]
+    spread = []
+    for n in range(1, 8):
+        to = p.seq((p.z + n // 2) % 4, (p.x + n % 2) % 2, p.c)
+        spread.append(remote(small_all.at[here], small_all.at[here], v3_send.at[n - 1], v3_recv.at[n - 1], to))
+    for copy in spread:
+        copy.start()
+    for i in range(3):
+        sums.last_add(i)
+    for copy in spread:
+        copy.wait()
+    total = small_all[0]
+    for n in range(1, 8):
+        total = total + small_all[n]
+    bank_back[p.t] = total[0:8, :]
+    unit_out[...] = total[8:16, :]
+    back = []
+    for n, (dy, dx) in enumerate(T_STEPS):
+        to = {"tensor": p.tensor_at(dy, dx)}
+        back.append(remote(bank_back.at[p.t], bank_back.at[p.t], v4_send.at[n], v4_recv.at[n], to))
+    for copy in back:
+        copy.start()
+
+    for copy in out_gather:
+        copy.wait()
+    for copy in last_gather:
+        copy.wait()
+    stores = [
+        pltpu.make_async_copy(out_whole, out_any, out_sem.at[0]),
+        pltpu.make_async_copy(in_whole, grad_any, out_sem.at[1]),
+    ]
+    for copy in stores:
+        copy.start()
+    for copy in back:
+        copy.wait()
+    vec_out[...] = bank_back[...]
+    sums.drain()
+    for d in range(5):
+        @pl.when((p.chip - d >= 0) & (((p.c == 1) & (d <= 3)) | ((p.c == 0) & (d >= 1))))
+        def _():
+            kv_pair_copy(d).wait_send()
+
+        if d >= 1:
+            @pl.when(p.chip - d >= 0)
+            def _():
+                kv_far_copy(d).wait_send()
+
+    for copy in stores:
+        copy.wait()
+
+
+def backward_call(
+    lengths, alive_row, alive_col, gains, shifts, dn2_part, gt, dft, ot, lse, hidden, unit_rows, qt,
+    tokens, cotangent, dffn, low2, low1, window, proj, ffn_part,
+):
+    vmem = pl.BlockSpec(memory_space=pltpu.VMEM)
+    anywhere = pl.BlockSpec(memory_space=pl.ANY)
+    shape = jax.ShapeDtypeStruct
+    dma = pltpu.SemaphoreType.DMA
+    rows_low = pltpu.VMEM((ROWS, WIDTH), BF)
+    shard_low = pltpu.VMEM((SHARD, WIDTH), BF)
+    masked = pltpu.VMEM((GROUPS, SPAN, ROWS), BF)
+    return pl.pallas_call(
+        backward_kernel,
+        in_specs=[pl.BlockSpec(memory_space=pltpu.SMEM)] + [vmem] * 12 + [anywhere] * 8,
+        out_specs=[anywhere, anywhere, vmem, vmem, vmem],
+        out_shape=[
+            shape((ROWS, WIDTH), BF),
+            shape((ROWS, WIDTH), BF),
+            shape((3, HD, WIDTH), F32),
+            shape((8, 8, 256), F32),
+            shape((8, SPAN), F32),
+        ],
+        scratch_shapes=[
+            pltpu.VMEM((16, 3, HD, WIDTH), BF),
+            pltpu.VMEM((8, 3, HD, WIDTH), BF),
+            pltpu.VMEM((3, 2, 3, HD, WIDTH), BF),
+            pltpu.VMEM((3, HD, WIDTH), BF),
+            pltpu.VMEM((5, 2, EXT, 2 * SPAN), BF),
+            pltpu.VMEM((5, 2, ROWS, 2 * SPAN), BF),
+            pltpu.VMEM((5, ROWS, 2 * SPAN), BF),
+            pltpu.VMEM((5, ROWS, 2 * SPAN), BF),
+            rows_low, rows_low, rows_low,
+            pltpu.VMEM((GROUPS, 4, HD, WIDTH), BF),
+            rows_low, shard_low, shard_low,
+            rows_low, rows_low, rows_low, rows_low,
+            pltpu.VMEM((3, 7, SHARD, WIDTH), BF),
+            masked, masked, masked, masked,
+            pltpu.VMEM((8, ROWS), F32),
+            pltpu.VMEM((SPAN, ROWS), F32),
+            pltpu.VMEM((ROWS, 2 * SPAN), F32),
+            pltpu.VMEM((SHARD, WIDTH), F32),
+            pltpu.VMEM((8, 8, 256), F32),
+            pltpu.VMEM((7, 8, 256), F32),
+            pltpu.VMEM((16, 256), F32),
+            pltpu.VMEM((16, 256), F32),
+            pltpu.VMEM((8, 16, 256), F32),
+            pltpu.VMEM((8, 8, 256), F32),
+            dma((3, 7)), dma((3, 7)), dma((3, 7)), dma((3, 7)),
+            dma((8, 3)), dma((8, 3)), dma((3, 2, 3)), dma((3, 2, 3)), dma((3,)), dma((3,)),
+            dma((5,)), dma((5,)), dma((5,)), dma((5,)),
+            dma((7,)), dma((7,)), dma, dma, dma((7,)), dma((7,)), dma((7,)), dma((7,)),
+            dma((8,)), dma((2,)),
+        ],
+        compiler_params=pltpu.CompilerParams(
+            collective_id=1, has_side_effects=True, vmem_limit_bytes=60 * 2**20
+        ),
+        name="layer_backward",
+    )(
+        lengths, alive_row, alive_col, gains, shifts, dn2_part, gt, dft, ot, lse, hidden, unit_rows, qt,
+        tokens, cotangent, dffn, low2, low1, window, proj, ffn_part,
+    )
+
+
+def high(left, right):
+    return jnp.dot(left, right, precision=HIGH, preferred_element_type=F32)
+
+
+def muon_kernel(grads, panel_mom, panels, new_panels, new_mom):
+    count = panels.shape[0]
+    eye = jnp.where(
+        lax.broadcasted_iota(jnp.int32, (HD, HD), 0) == lax.broadcasted_iota(jnp.int32, (HD, HD), 1), 1.0, 0.0
+    )
+    scale, gram, chain = [], [], [None] * count
+    for n in range(count):
+        moment = DECAY * panel_mom[n] + grads[n]
+        new_mom[n] = moment
+        factor = lax.rsqrt(jnp.sum(moment * moment, axis=(0, 1), keepdims=True) + 1e-06)
+        current = moment * factor
+        scale.append(factor)
+        gram.append(
+            lax.dot_general(
+                current, current, (((1,), (1,)), ((), ())), precision=HIGH, preferred_element_type=F32
+            )
+        )
     for sweep in range(NS_ITERS):
-        gram = jnp.einsum("pij,pkj->pik", current, current, precision=HIGH)
-        poly = NS_B * gram + NS_C * jnp.einsum("pij,pjk->pik", gram, gram, precision=HIGH)
-        current = NS_A * current + jnp.einsum("pij,pjk->pik", poly, current, precision=HIGH)
-    return current
+        squares = [high(a, a) for a in gram]
+        steps = [NS_A * eye + NS_B * a + NS_C * s for a, s in zip(gram, squares)]
+        chain = [m if sweep == 0 else high(m, c) for m, c in zip(steps, chain)]
+        if sweep < NS_ITERS - 1:
+            halves = [high(m, a) for m, a in zip(steps, gram)]
+            gram = [high(h, m) for h, m in zip(halves, steps)]
+    for n in range(count):
+        direction = high(chain[n], new_mom[n] * scale[n])
+        size_u = jnp.sum(direction * direction, axis=(0, 1), keepdims=True)
+        held = panels[n]
+        size_w = jnp.sum(held * held, axis=(0, 1), keepdims=True)
+        new_panels[n] = held - LR_MATRIX * jnp.sqrt(size_w) * lax.rsqrt(size_u + 1e-06) * direction
+
+
+def muon_call(grads, panel_mom, panels):
+    vmem = pl.BlockSpec(memory_space=pltpu.VMEM)
+    shape = jax.ShapeDtypeStruct(panels.shape, F32)
+    return pl.pallas_call(
+        muon_kernel,
+        in_specs=[vmem] * 3,
+        out_specs=[vmem, vmem],
+        out_shape=[shape, shape],
+        compiler_params=pltpu.CompilerParams(vmem_limit_bytes=32 * 2**20),
+        name="panel_step",
+    )(grads, panel_mom, panels)
 
 
 def per_device(
     tokens, cotangent, exits, lengths, panels, panel_mom,
     unit_bias, unit_bias_mom, gains, gains_mom, vec_bias, vec_bias_mom,
 ):
-    rows, width = tokens.shape
-    groups, head_dim = GROUPS, HD
-    total = rows * lax.axis_size("seq")
-    scale = head_dim ** (-0.5)
-    live = (exits >= LAYER).astype(F32)[:, None]
-    alive = (exits >= LAYER).astype(jnp.int32)
-    positions = lax.axis_index("seq") * rows + jnp.arange(rows, dtype=jnp.int32)
-    ends = jnp.cumsum(lengths)
-    segment = jnp.sum((positions[:, None] >= ends[None, :]).astype(jnp.int32), axis=1)
-    block = math.gcd(total, 512)
-    count = total // block
-    begins = jnp.arange(count, dtype=jnp.int32) * block
-    low1, qt, window, ot, lse, hidden32, low2, gt, dft, ffn_part, dn2_part, store = forward_call(
-        lengths, tokens, cotangent, live.reshape(1, rows), live, panels, unit_bias.T, gains, vec_bias
+    live = (exits >= LAYER).astype(F32)
+    alive_row, alive_col = live[None, :], live[:, None]
+    (
+        low1, qt, window, ot, lse, hidden, low2, gt, dft, ffn_part, dn2_part, proj, dffn, unit_rows,
+    ) = forward_call(
+        lengths, tokens, cotangent, alive_row, alive_col, panels, unit_bias.T, gains, vec_bias
     )
-    core = lax.axis_index("seq") % 2
-    mine_kv = lax.dynamic_index_in_dim(window[0], core, 0, keepdims=False)
-    keys, values = mine_kv[:rows, :SPAN], mine_kv[:rows, SPAN:]
-    query = qt.T
-    q_heads = query.reshape(rows, groups, head_dim)
-    log_total = lse[:groups]
-    attn_full = ot.T.reshape(rows, groups, head_dim)
-    attn_low = ot.T.astype(BF)
-    stack = store.reshape(groups, 12, head_dim, width)
-    w_query = stack[:, 0].reshape(groups * head_dim, width)
-    w_key = stack[:, 1].reshape(groups * head_dim, width)
-    w_value = stack[:, 2].reshape(groups * head_dim, width)
-    w_out = stack[:, 3].reshape(groups * head_dim, width)
-    x_full = tokens.astype(F32)
-    _, unit1, factor1 = normalize(x_full, gains[0], vec_bias[2])
-    hidden = lax.all_gather(hidden32, "tensor", axis=0, tiled=True)
-    _, unit2, factor2 = normalize(hidden, gains[1], vec_bias[3])
-    ffn_whole = lax.psum(ffn_part, "tensor").astype(F32)
-    output = hidden + live * (ffn_whole + vec_bias[1])
-    grad_out = cotangent.astype(F32)
-    d_ffn = (live * grad_out).astype(BF)
-    d_b2 = jnp.sum(d_ffn.astype(F32), axis=0)
-    d_w_back = nn(gt, d_ffn).reshape(4, groups, head_dim, width).transpose(1, 0, 2, 3)
-    d_b1 = jnp.sum(dft.astype(F32), axis=1).reshape(4, groups, head_dim).transpose(1, 0, 2)
-    d_w_in = nn(dft, low2).reshape(4, groups, head_dim, width).transpose(1, 0, 2, 3)
-    d_norm2 = lax.psum(dn2_part, "tensor").astype(F32)
-    d_hidden_norm, d_gain2, d_shift2 = norm_back(d_norm2, unit2, factor2, gains[1])
-    d_hidden = grad_out + d_hidden_norm
-    d_branch = (live * d_hidden).astype(BF)
-    d_bo = jnp.sum(d_branch.astype(F32), axis=0)
-    d_w_out = inner_rows(attn_low, d_branch)
-    d_attn = times_t(d_branch, w_out).astype(BF)
-    d_heads = d_attn.reshape(rows, groups, head_dim)
-    delta = jnp.einsum("qhe,qhe->hq", d_heads.astype(F32), attn_full)
-    all_keys, all_values, all_seg, all_alive = (
-        lax.all_gather(keys, "seq", axis=0, tiled=True),
-        lax.all_gather(values, "seq", axis=0, tiled=True),
-        lax.all_gather(segment, "seq", axis=0, tiled=True),
-        lax.all_gather(alive, "seq", axis=0, tiled=True),
+    output, input_grad, panel_grads, vec_sums, unit_sums = backward_call(
+        lengths, alive_row, alive_col, gains, vec_bias, dn2_part, gt, dft, ot, lse, hidden, unit_rows, qt,
+        tokens, cotangent, dffn, low2, low1, window, proj, ffn_part,
     )
-
-    def back_block(d_query, blocked):
-        k_blk, v_blk, s_blk, a_blk, begin = blocked
-        k_pos = begin + jnp.arange(block, dtype=jnp.int32)
-        allowed = (segment[:, None] == s_blk[None, :]) & (positions[:, None] >= k_pos[None, :])
-        allowed = allowed & (alive[:, None] > 0) & (a_blk[None, :] > 0)
-        k_h = k_blk.reshape(block, groups, head_dim)
-        v_h = v_blk.reshape(block, groups, head_dim)
-        score = jnp.einsum("qhe,khe->hqk", q_heads, k_h, preferred_element_type=F32) * scale
-        prob = jnp.where(allowed[None], jnp.exp(score - log_total[:, :, None]), 0.0)
-        d_val = jnp.einsum("hqk,qhe->khe", prob.astype(BF), d_heads, preferred_element_type=F32)
-        d_prob = jnp.einsum("qhe,khe->hqk", d_heads, v_h, preferred_element_type=F32)
-        d_score = (prob * (d_prob - delta[:, :, None])).astype(BF)
-        d_query = d_query + jnp.einsum("hqk,khe->qhe", d_score, k_h, preferred_element_type=F32)
-        d_key = jnp.einsum("hqk,qhe->khe", d_score, q_heads, preferred_element_type=F32)
-        return (d_query, (d_key.reshape(block, SPAN), d_val.reshape(block, SPAN)))
-
-    blocked_in = (
-        all_keys.reshape(count, block, -1),
-        all_values.reshape(count, block, -1),
-        all_seg.reshape(count, block),
-        all_alive.reshape(count, block),
-        begins,
-    )
-    d_query, (d_key_all, d_val_all) = lax.scan(
-        back_block, jnp.zeros((rows, groups, head_dim), F32), blocked_in
-    )
-    d_key_all = d_key_all.reshape(total, SPAN) * scale
-    d_val_all = d_val_all.reshape(total, SPAN)
-    d_key_mine, d_val_mine = (
-        lax.psum_scatter(d_key_all.astype(BF), "seq", scatter_dimension=0, tiled=True).astype(F32),
-        lax.psum_scatter(d_val_all.astype(BF), "seq", scatter_dimension=0, tiled=True).astype(F32),
-    )
-    d_q = (d_query.reshape(rows, SPAN) * scale).astype(BF)
-    d_k = d_key_mine.astype(BF)
-    d_v = d_val_mine.astype(BF)
-    d_bq = jnp.sum(d_q.astype(F32), axis=0)
-    d_bv = jnp.sum(d_v.astype(F32), axis=0)
-    d_w_query = inner_rows(d_q, low1)
-    d_w_key = inner_rows(d_k, low1)
-    d_w_value = inner_rows(d_v, low1)
-    d_norm1_part = plain(d_q, w_query) + plain(d_k, w_key) + plain(d_v, w_value)
-    d_norm1 = lax.psum(d_norm1_part.astype(BF), "tensor").astype(F32)
-    d_input_norm, d_gain1, d_shift1 = norm_back(d_norm1, unit1, factor1, gains[0])
-    input_grad = d_hidden + d_input_norm
-    grad_stack = jnp.concatenate(
-        [
-            d_w_query.reshape(groups, 1, head_dim, width),
-            d_w_key.reshape(groups, 1, head_dim, width),
-            d_w_value.reshape(groups, 1, head_dim, width),
-            d_w_out.reshape(groups, 1, head_dim, width),
-            d_w_in,
-            d_w_back,
-        ],
-        axis=1,
-    ).reshape(groups * 12, head_dim, width)
-    unit_grad = jnp.concatenate(
-        [
-            d_bq.reshape(groups, head_dim),
-            d_bv.reshape(groups, head_dim),
-            d_b1.reshape(groups, 4 * head_dim),
-        ],
-        axis=1,
-    )
-    gain_grad = jnp.stack([d_gain1, d_gain2])
-    shift_grad = jnp.stack([d_bo, d_b2, d_shift1, d_shift2])
-    unit_sum, gain_sum, shift_sum = (
-        lax.psum(unit_grad.astype(BF), "seq").astype(F32),
-        lax.psum(gain_grad.astype(BF), "seq").astype(F32),
-        lax.psum(shift_grad.astype(BF), "seq").astype(F32),
-    )
-    mine = lax.psum_scatter(grad_stack.astype(BF), "seq", scatter_dimension=0, tiled=True).astype(F32)
-    moment = DECAY * panel_mom + mine
-    direction = orthogonalize(moment)
-    size_w = jnp.sum(panels * panels, axis=(1, 2), keepdims=True)
-    size_u = jnp.sum(direction * direction, axis=(1, 2), keepdims=True)
-    new_panels = panels - LR_MATRIX * jnp.sqrt(size_w) * lax.rsqrt(size_u + 1e-06) * direction
+    new_panels, moment = muon_call(panel_grads, panel_mom, panels)
+    vec_sums = vec_sums.transpose(1, 0, 2).reshape(8, WIDTH)
+    unit_sum = unit_sums[0:6].reshape(6, GROUPS, HD).transpose(1, 0, 2).reshape(GROUPS, 6 * HD)
     unit_moment = DECAY * unit_bias_mom + unit_sum
-    gains_moment = DECAY * gains_mom + gain_sum
-    vec_moment = DECAY * vec_bias_mom + shift_sum
+    gains_moment = DECAY * gains_mom + vec_sums[0:2]
+    vec_moment = DECAY * vec_bias_mom + vec_sums[2:6]
     return (
-        output.astype(BF), input_grad, new_panels, moment,
+        output, input_grad.astype(F32), new_panels, moment,
         unit_bias - LR_VECTOR * unit_moment, unit_moment,
         gains - LR_VECTOR * gains_moment, gains_moment,
         vec_bias - LR_VECTOR * vec_moment, vec_moment,

time: 897 us -> 309 us (0.34); the launches traced: 887 us -> 309 us
  waiting for transfers between devices: 427 us -> 0 us
  Pallas kernels: 115 us -> 295 us
  blocking collectives: 113 us -> 0 us
  local copies, waits for them, and re-layouts: 87.1 us -> 7.29 us
  matrix products: 74.7 us -> 0 us
  other arithmetic: 53.1 us -> 5.5 us
  between operations: 15 us -> 0.73 us
    reduce_scatter x3 -> x0, waiting for transfers between devices: 182 us -> none  [the longest x1 65.2 us: per_device(): lax.psum_scatter(grad_stack.astype(BF), 'seq', scatter_dimension=0, tiled...]
    pallas_call x0 -> x2, Pallas kernels: none -> 180 us  [the longest x1 172 us: backward_call(): pl.pallas_call(backward_kernel, in_specs=[pl.BlockSpec(memory_space=pltpu...]
    psum x2 -> x0, waiting for transfers between devices: 179 us -> none  [the longest x1 90 us: per_device(): ffn_whole = lax.psum(ffn_part, 'tensor').astype(F32)]
    dot_general x65 -> x0, matrix products: 74.7 us -> none  [the longest x5 13.4 us: nn(): return jnp.dot(left, right, preferred_element_type=F32)]
    psum x1 -> x0, blocking collectives: 66.6 us -> none  [per_device(): lax.psum(unit_grad.astype(BF), 'seq').astype(F32)]
    all_gather x3 -> x0, waiting for transfers between devices: 65 us -> none  [the longest x1 35.6 us: per_device(): lax.all_gather(keys, 'seq', axis=0, tiled=True)]
    all_gather x2 -> x0, blocking collectives: 46.6 us -> none  [the longest x1 30 us: per_device(): lax.all_gather(segment, 'seq', axis=0, tiled=True)]
    dynamic_slice x40 -> x0, local copies, waits for them, and re-layouts: 31.3 us -> none  [per_device(): lax.scan(back_block, jnp.zeros((rows, groups, head_dim), F32), blocked_in)]
  transfers between devices with their start and end apart: 8 -> 0, of which waited for: 8 -> 0; matrix products, arithmetic and copies ran while one was open for 6% -> 0% of each run, Pallas kernels for 0% -> 0%
where the time goes in v2:
time: 309 us
  Pallas kernels  295 us (95%)
  local copies, waits for them, and re-layouts  7.29 us (2%)
  other arithmetic  5.5 us (2%)
    pallas_call x1, Pallas kernels, backward_call(): pl.pallas_call(backward_kernel, in_specs=[pl.BlockSpec(memory_space=pltpu...  172 us
    pallas_call x1, Pallas kernels, forward_call(): pl.pallas_call(forward_kernel, in_specs=[pl.BlockSpec(memory_space=pltpu....  115 us
    pallas_call x1, Pallas kernels, muon_call(): pl.pallas_call(muon_kernel, in_specs=[vmem] * 3, out_specs=[vmem, vmem],...  7.81 us

profile of v2, /device:TPU:0, one launch (start us, length us, event | category | flops | bytes accessed | tf_op | source)
XLA Modules:
  0.0 308.7 jit_solution(633541929664692475)
XLA Ops:
  0.6 0.7 compare_convert_fusion
  1.3 0.8 copy.26.alive_col
  2.1 1.5 copy.24
  3.6 0.0 copy-done.8
  3.6 115.2 %layer_forward.1 = (bf16[256,2048]{1,0:T(8,128)(2,1)}, bf16[256,256]{1,0:T(8,128)(2,1)}, bf16[5,2,272,512]{3,2,1,0:T(8,128)(2,1)}, f32[256,256]{1,0:T(8,128)}, f...) custom-call(s32[4]{0:T(128)} %lengths.3, ...), custom_call_target="tpu_custom_call" | custom-call | tf_op jit(solution)/shard_map/layer_forward/pallas_call | solution.py:564
  118.9 0.0 copy-start.7
  118.9 0.0 copy-start.10
  118.9 0.0 copy-start.5
  118.9 0.0 copy-start.9
  118.9 0.0 copy-start.4
  119.0 0.0 copy-start.6
  119.0 172.1 %layer_backward.1 = (bf16[256,2048]{1,0:T(8,128)(2,1)}, bf16[256,2048]{1,0:T(8,128)(2,1)}, f32[3,64,2048]{2,1,0:T(8,128)}, f32[8,8,256]{2,1,0:T(8,128)}, f32[8,256]{1,0:T(8,128)}) custom-call(s32[4]{0:T(128)} %lengths.3, f32[1,256]{1,0:T(1,128)} %bitcast.18, f32[256,1]{1,0:T(8,128)} %copy.26.alive_col, f32[2,2048]{1,0:T(2,128)} %gains.3, f32[4,2048]{1,0:T(4,128)} %shifts.3, ...), custom_call_target="tpu_custom_call" | custom-call | tf_op jit(solution)/shard_map/layer_backward/pallas_call | solution.py:1045
  291.1 0.8 reshape.29
  291.9 0.1 reshape.30
  292.0 0.0 copy-done.7
  292.0 0.6 multiply_subtract_fusion.2
  292.6 0.8 slice.20
  293.4 0.8 slice.21
  294.3 0.6 multiply_subtract_fusion.1
  294.9 0.6 multiply_subtract_fusion
  295.6 2.9 convert_element_type.7
  298.5 1.4 copy-done.2
  299.9 7.8 %panel_step.1 = (f32[3,64,2048]{2,1,0:T(8,128)}, f32[3,64,2048]{2,1,0:T(8,128)}) custom-call(f32[3,64,2048]{2,1,0:T(8,128)S(1)} %copy-done.2, f32[3,64,2048]{2,1,0:T(8,128)S(1)} %copy-done.1, f32[3,64,2048]{2,1,0:T(8,128)S(1)} %copy-done), custom_call_target="tpu_custom_call" | custom-call | tf_op jit(solution)/shard_map/panel_step/pallas_call | solution.py:1136
  307.8 1.0 copy.31
  (14 shorter events, 0.0 us)
Async XLA Ops:
  1.3 2.3 copy-start.8
  118.9 173.1 %copy-start.7 = (f32[4,384]{1,0:T(4,128)S(1)}, f32[4,384]{1,0:T(4,128)}, u32[]{:S(2)}) copy-start(f32[4,384]{1,0:T(4,128)} %param.18) | copy-start | bytes 18436
  118.9 173.1 %copy-start.10 = (f32[4,384]{1,0:T(4,128)S(1)}, f32[4,384]{1,0:T(4,128)}, u32[]{:S(2)}) copy-start(f32[4,384]{1,0:T(4,128)} %param.19) | copy-start | bytes 18436
  118.9 175.4 %copy-start.5 = (f32[2,2048]{1,0:T(2,128)S(1)}, f32[2,2048]{1,0:T(2,128)}, u32[]{:S(2)}) copy-start(f32[2,2048]{1,0:T(2,128)} %gains.3) | copy-start | bytes 49156
  118.9 175.4 %copy-start.9 = (f32[2,2048]{1,0:T(2,128)S(1)}, f32[2,2048]{1,0:T(2,128)}, u32[]{:S(2)}) copy-start(f32[2,2048]{1,0:T(2,128)} %param.21) | copy-start | bytes 49156
  118.9 176.0 %copy-start.4 = (f32[4,2048]{1,0:T(4,128)S(1)}, f32[4,2048]{1,0:T(4,128)}, u32[]{:S(2)}) copy-start(f32[4,2048]{1,0:T(4,128)} %shifts.3) | copy-start | bytes 98308
  119.0 176.0 %copy-start.6 = (f32[4,2048]{1,0:T(4,128)S(1)}, f32[4,2048]{1,0:T(4,128)}, u32[]{:S(2)}) copy-start(f32[4,2048]{1,0:T(4,128)} %param.23) | copy-start | bytes 98308
  295.6 2.9 copy-start
  295.6 2.9 copy-start.1
  298.5 1.4 copy-start.2
  299.9 7.8 %copy-start.3 = (bf16[256,2048]{1,0:T(8,128)(2,1)S(1)}, bf16[256,2048]{1,0:T(8,128)(2,1)}, u32[]{:S(2)}) copy-start(bf16[256,2048]{1,0:T(8,128)(2,1)} %get-tuple-element.68) | copy-start | bytes 3145732

commit v3 on v2

--- a/solution.py
+++ b/solution.py
@@ -33,7 +33,8 @@
 BF = jnp.bfloat16
 F32 = jnp.float32
 
-Z_STEPS = (1, 3, 2)
+NEAR = (1, 3)
+HALF = 32
 T_STEPS = tuple((dy, dx) for dy in (2, 1, 3, 0) for dx in (1, 0) if (dy, dx) != (0, 0))
 
 
@@ -164,68 +165,83 @@
 
 
 class Panels:
-    def __init__(self, place, store, recv, across, along, beside):
+    def __init__(self, place, store, recv, across, along, half_send, half_recv, beside):
         self.p, self.store, self.recv = place, store, recv
-        self.sx, self.sz, self.sc = across, along, beside
-        p = place
-        self.own = 4 * p.z + 2 * p.x + p.c
-        self.nbr = 4 * p.z + 2 * (1 - p.x) + p.c
+        self.sx, self.sz, self.sh, self.rh, self.sc = across, along, half_send, half_recv, beside
 
     def piece(self, which, i, send, to):
         ref = self.store.at[which, i]
         return remote(ref, ref, send, self.recv.at[which, i], to)
 
-    def to_across(self, i):
-        return self.piece(self.own, i, self.sx.at[i], self.p.across())
-
-    def to_along(self, kind, n, i):
-        which = self.own if kind == 0 else self.nbr
-        return self.piece(which, i, self.sz.at[kind, n, i], self.p.along(Z_STEPS[n]))
-
-    def to_beside(self, slot, which, i):
-        return self.piece(which, i, self.sc.at[slot, i], self.p.sibling())
-
-    def from_along(self, kind, n):
-        x = self.p.x if kind == 0 else 1 - self.p.x
-        return 4 * ((self.p.z - Z_STEPS[n]) % 4) + 2 * x + self.p.c
+    def across_copy(self, k, i):
+        return self.piece(4 * self.p.z + k, i, self.sx.at[i], self.p.across())
+
+    def along_copy(self, k, i, n):
+        return self.piece(4 * self.p.z + k, i, self.sz.at[k // 2, n, i], self.p.along(NEAR[n]))
+
+    def half_copy(self, k, i, n):
+        which = 4 * ((self.p.z - NEAR[n]) % 4) + k
+        ref = self.store.at[which, i, pl.ds(n * HALF, HALF)]
+        return remote(ref, ref, self.sh.at[k // 2, n, i], self.rh.at[k // 2, n, i], self.p.along(NEAR[n]))
+
+    def beside_copy(self, k, i, slot):
+        which = 4 * ((self.p.z - (0, 1, 3, 2)[slot]) % 4) + k
+        return self.piece(which, i, self.sc.at[k // 2, slot, i], self.p.sibling())
 
     def arrived(self, which, i):
         self.piece(which, i, self.sx.at[0], self.p.sibling()).wait_recv()
 
-    def own_across(self, i):
-        self.to_across(i).start()
-
-    def own_along(self, i):
-        for n in range(3):
-            self.to_along(0, n, i).start()
-        self.to_beside(0, self.own, i).start()
-
-    def nbr_on(self, i):
-        self.arrived(self.nbr, i)
-        for n in range(3):
-            self.to_along(1, n, i).start()
-        self.to_beside(1, self.nbr, i).start()
-
-    def along_on(self, kind, i):
-        for n in range(3):
-            which = self.from_along(kind, n)
-            self.arrived(which, i)
-            self.to_beside(2 + 3 * kind + n, which, i).start()
-
-    def beside_in(self, x, i):
-        for u in range(4):
-            self.arrived(4 * u + 2 * x + 1 - self.p.c, i)
-
-    def drain(self, i):
-        self.to_across(i).wait_send()
-        for kind in range(2):
-            for n in range(3):
-                self.to_along(kind, n, i).wait_send()
-        self.to_beside(0, self.own, i).wait_send()
-        self.to_beside(1, self.nbr, i).wait_send()
-        for kind in range(2):
-            for n in range(3):
-                self.to_beside(2 + 3 * kind + n, self.from_along(kind, n), i).wait_send()
+    def across(self, k, i):
+        @pl.when((self.p.c == k % 2) & (self.p.x == k // 2))
+        def _():
+            self.across_copy(k, i).start()
+
+    def along(self, k, i, ways=(0, 1), first=True):
+        @pl.when(self.p.c == k % 2)
+        def _():
+            if first:
+                @pl.when(self.p.x != k // 2)
+                def _():
+                    self.arrived(4 * self.p.z + k, i)
+
+            for n in ways:
+                self.along_copy(k, i, n).start()
+            if first:
+                self.beside_copy(k, i, 0).start()
+
+    def pass_on(self, k, i):
+        @pl.when(self.p.c == k % 2)
+        def _():
+            for n in (0, 1):
+                self.arrived(4 * ((self.p.z - NEAR[n]) % 4) + k, i)
+                self.half_copy(k, i, n).start()
+                self.beside_copy(k, i, 1 + n).start()
+
+    def far_in(self, k, i):
+        @pl.when(self.p.c == k % 2)
+        def _():
+            for n in (0, 1):
+                self.half_copy(k, i, n).wait_recv()
+            self.beside_copy(k, i, 3).start()
+
+    def beside_in(self, k, i):
+        @pl.when(self.p.c != k % 2)
+        def _():
+            for u in range(4):
+                self.arrived(4 * u + k, i)
+
+    def drain(self, k, i):
+        @pl.when(self.p.c == k % 2)
+        def _():
+            @pl.when(self.p.x == k // 2)
+            def _():
+                self.across_copy(k, i).wait_send()
+
+            for n in (0, 1):
+                self.along_copy(k, i, n).wait_send()
+                self.half_copy(k, i, n).wait_send()
+            for slot in range(4):
+                self.beside_copy(k, i, slot).wait_send()
 
     def kind_panels(self, j):
         return jnp.concatenate([self.store[4 * u + j // 3, j % 3] for u in range(GROUPS)], axis=0)
@@ -250,23 +266,27 @@
     low1_out, qt_out, window_out, ot_out, lse_out, hidden_out, low2_out, gt_out, dft_out, ffn_out, dn2_out, proj_out,
     dffn_out, unit_out,
     store, window, low1, qt, acc, top, mass, part, land, whole, g_rows, df_rows, dft, gt, dffn,
-    w_recv, w_across, w_along, w_beside, kv_send, kv_recv, kv_bsend, kv_brecv, rs_send, rs_recv, ag_send, ag_recv, out_sem,
+    w_recv, w_across, w_along, w_half_send, w_half_recv, w_beside, kv_send, kv_recv, kv_bsend, kv_brecv, rs_send, rs_recv, ag_send, ag_recv, out_sem,
 ):
     p = Place()
-    w = Panels(p, store, w_recv, w_across, w_along, w_beside)
-    first = 1 - p.c
+    w = Panels(p, store, w_recv, w_across, w_along, w_half_send, w_half_recv, w_beside)
     p.greet()
 
     for i in range(3):
-        store[w.own, i] = panels[i].astype(BF)
+        store[p.s, i] = panels[i].astype(BF)
 
     order = (1, 2, 0)
 
-    @pl.when((p.x == 0) & (p.c == 0))
+    for i in order:
+        w.across(0, i)
+    for k in (2, 3):
+        for i in range(3):
+            w.across(k, i)
+
+    @pl.when(p.x == 0)
     def _():
         for i in order:
-            w.own_across(i)
-            w.own_along(i)
+            w.along(0, i)
 
     def norm1(r, carry):
         rows = pl.ds(pl.multiple_of(r * 32, 32), 32)
@@ -277,20 +297,16 @@
 
     lax.fori_loop(0, ROWS // 32, norm1, 0)
 
+    @pl.when(p.x == 1)
+    def _():
+        for i in order:
+            w.along(0, i)
+
     for i in order:
-        @pl.when((p.x == 1) & (p.c == 0))
-        def _():
-            w.nbr_on(i)
-            w.along_on(1, i)
-
-        @pl.when((p.x == 0) & (p.c == 0))
-        def _():
-            w.along_on(0, i)
-
-        @pl.when(p.c == 1)
-        def _():
-            w.beside_in(0, i)
-
+        w.pass_on(0, i)
+    for i in order:
+        w.far_in(0, i)
+        w.beside_in(0, i)
         made = nt(w.kind_panels(i), low1[...])
         if i == 1:
             window[0, p.c, 0:ROWS, 0:SPAN] = made.astype(BF).T
@@ -310,22 +326,16 @@
             bias = jnp.concatenate([bias_t[0:HD, u : u + 1] for u in range(GROUPS)], axis=0)
             qt[...] = (made + bias).astype(BF)
 
-    @pl.when(p.c == 1)
+    for i in range(3):
+        w.across(1, i)
+
+    @pl.when(p.x == 0)
     def _():
-        w.own_across(0)
-
-        @pl.when(p.x == 0)
-        def _():
-            w.own_along(0)
-
-    @pl.when((p.c == 0) & (p.x == 1))
-    def _():
-        w.own_across(0)
-
-    @pl.when((p.c == 1) | (p.x == 1))
-    def _():
-        for i in (1, 2):
-            w.own_across(i)
+        w.along(1, 0)
+
+    for i in range(3):
+        w.along(3, i, ways=(1,))
+        w.along(2, i, ways=(1,))
 
     acc[...] = jnp.zeros_like(acc)
     top[...] = jnp.full_like(top, FLOOR)
@@ -377,45 +387,27 @@
     kv_in(1)
     attend_chip(0)
 
-    @pl.when((p.c == 1) & (p.x == 1))
+    @pl.when(p.x == 1)
     def _():
-        w.nbr_on(0)
+        w.along(1, 0)
 
     kv_beside(1)
     kv_in(2)
     attend_chip(1)
+    w.pass_on(1, 0)
     kv_beside(2)
     kv_in(3)
+    for i in range(3):
+        w.along(3, i, ways=(0,), first=False)
+        w.along(2, i, ways=(0,), first=False)
     attend_chip(2)
     kv_beside(3)
     kv_in(4)
-
-    @pl.when((p.c == 1) & (p.x == 1))
-    def _():
-        w.own_along(0)
-
-    @pl.when((p.c == 0) & (p.x == 1))
-    def _():
-        w.own_along(0)
-
-    @pl.when((p.c == 1) | (p.x == 1))
-    def _():
-        for i in (1, 2):
-            w.own_along(i)
-
+    for i in (1, 2):
+        w.along(1, i)
     attend_chip(3)
+    w.far_in(1, 0)
     kv_beside(4)
-
-    @pl.when(p.c == 1)
-    def _():
-        @pl.when(p.x == 0)
-        def _():
-            w.along_on(0, 0)
-
-        @pl.when(p.x == 1)
-        def _():
-            w.along_on(1, 0)
-
     attend_chip(4)
 
     total = jnp.maximum(mass[...], 1e-30)
@@ -426,9 +418,7 @@
     ot_out[...] = acc[...]
     o_rows = acc[...].astype(BF).T
 
-    @pl.when(p.c == 0)
-    def _():
-        w.beside_in(0, 0)
+    w.beside_in(1, 0)
 
     def project(n, carry):
         cols = pl.ds(pl.multiple_of(n * 256, 256), 256)
@@ -440,19 +430,8 @@
     for copy in scatter:
         copy.start()
 
-    @pl.when((p.c == 0) & (p.x == 0))
-    def _():
-        w.nbr_on(0)
-
-    @pl.when((p.c == 1) & (p.x == 0))
-    def _():
-        w.nbr_on(0)
-
-    @pl.when((p.c == 1) | (p.x == 0))
-    def _():
-        for i in (1, 2):
-            w.nbr_on(i)
-
+    for k, i in ((3, 0), (2, 0), (3, 1), (2, 1)):
+        w.pass_on(k, i)
     for copy in scatter:
         copy.wait()
     mine = pl.ds(pl.multiple_of(p.t * SHARD, SHARD), SHARD)
@@ -465,41 +444,15 @@
     for copy in gather:
         copy.start()
 
-    @pl.when((p.c == 1) & (p.x == 0))
-    def _():
-        w.along_on(1, 0)
-
-    @pl.when((p.c == 1) & (p.x == 1))
-    def _():
-        w.along_on(0, 0)
-
-    @pl.when((p.c == 0) & (p.x == 0))
-    def _():
-        w.along_on(1, 0)
-
-    @pl.when((p.c == 0) & (p.x == 1))
-    def _():
-        w.along_on(0, 0)
-
-    for i in (1, 2):
-        @pl.when((p.c == 1) | (p.x == 1))
-        def _():
-            w.along_on(0, i)
-
-        @pl.when((p.c == 1) | (p.x == 0))
-        def _():
-            w.along_on(1, i)
-
+    for k, i in ((3, 2), (2, 2), (1, 1), (1, 2)):
+        w.pass_on(k, i)
+    rest = ((3, 0), (2, 0), (3, 1), (2, 1), (3, 2), (2, 2), (1, 1), (1, 2))
+    for k, i in rest:
+        w.far_in(k, i)
     for copy in gather:
         copy.wait()
-
-    @pl.when(p.c == 0)
-    def _():
-        w.beside_in(0, 1)
-        w.beside_in(0, 2)
-
-    for i in range(3):
-        w.beside_in(1, i)
+    for k, i in rest:
+        w.beside_in(k, i)
 
     out_copies = [
         pltpu.make_async_copy(dffn, dffn_out, out_sem.at[0]),
@@ -541,8 +494,9 @@
 
     lax.fori_loop(0, WIDTH // 256, feed, 0)
 
-    for i in range(3):
-        w.drain(i)
+    for k in range(4):
+        for i in range(3):
+            w.drain(k, i)
     mine_kv = window.at[0, p.c]
     for d in range(1, 5):
         @pl.when(p.chip + d < 8)
@@ -597,7 +551,7 @@
             pltpu.VMEM((UNITS, ROWS), BF),
             pltpu.VMEM((UNITS, ROWS), BF),
             pltpu.VMEM((ROWS, WIDTH), BF),
-            dma((16, 3)), dma((3,)), dma((2, 3, 3)), dma((8, 3)),
+            dma((16, 3)), dma((3,)), dma((2, 2, 3)), dma((2, 2, 3)), dma((2, 2, 3)), dma((2, 4, 3)),
             dma((5,)), dma((5,)), dma((5,)), dma((5,)),
             dma((7,)), dma((7,)), dma((7,)), dma((7,)), dma((13,)),
         ],
@@ -626,13 +580,11 @@
 
 
 class PanelSums:
-    def __init__(self, place, grads, pair, line, last, result, sems):
+    def __init__(self, place, grads, pair, half, line, last, result, sems):
         self.p, self.grads = place, grads
-        self.pair, self.line, self.last, self.result = pair, line, last, result
-        self.pair_send, self.pair_recv, self.line_send, self.line_recv, self.last_send, self.last_recv = sems
-
-    def kind(self, k):
-        return (k // 2 + self.p.x) % 2
+        self.pair, self.half, self.line, self.last, self.result = pair, half, line, last, result
+        self.pair_send, self.pair_recv, self.half_send, self.half_recv = sems[:4]
+        self.line_send, self.line_recv, self.last_send, self.last_recv = sems[4:]
 
     def pair_copy(self, u, k, i):
         return remote(
@@ -649,15 +601,23 @@
             for u in range(GROUPS):
                 self.pair_copy(u, k, i).start()
 
+    def half_copy(self, n, k, i):
+        rows = pl.ds(n * HALF, HALF)
+        return remote(
+            self.grads.at[4 * ((self.p.z + 2) % 4) + k, i, rows],
+            self.half.at[k // 2, n, i],
+            self.half_send.at[k // 2, n, i],
+            self.half_recv.at[k // 2, n, i],
+            self.p.along(NEAR[n]),
+        )
+
     def line_copy(self, n, k, i):
-        head = (self.p.z + Z_STEPS[n]) % 4
-        kind = self.kind(k)
         return remote(
-            self.grads.at[4 * head + k, i],
-            self.line.at[n, kind, i],
-            self.line_send.at[n, kind, i],
-            self.line_recv.at[n, kind, i],
-            self.p.along(Z_STEPS[n]),
+            self.grads.at[4 * ((self.p.z + NEAR[n]) % 4) + k, i],
+            self.line.at[k // 2, n, i],
+            self.line_send.at[k // 2, n, i],
+            self.line_recv.at[k // 2, n, i],
+            self.p.along(NEAR[n]),
         )
 
     def pair_add(self, k, i):
@@ -674,7 +634,26 @@
             for u in range(GROUPS):
                 self.pair_copy(u, k, i).wait_recv()
             lax.fori_loop(0, 4 * GROUPS, add, 0)
-            for n in range(3):
+            for n in (0, 1):
+                self.half_copy(n, k, i).start()
+
+    def line_mid(self, k, i):
+        @pl.when(self.p.c == k % 2)
+        def _():
+            for n in (0, 1):
+                self.half_copy(n, k, i).wait_recv()
+                which = 4 * ((self.p.z + NEAR[n]) % 4) + k
+
+                def add(step, carry):
+                    here = pl.ds(pl.multiple_of(step * 16, 16), 16)
+                    rows = pl.ds(pl.multiple_of(n * HALF + step * 16, 16), 16)
+                    self.grads[which, i, rows, :] = (
+                        self.grads[which, i, rows, :].astype(F32)
+                        + self.half[k // 2, n, i, here, :].astype(F32)
+                    ).astype(BF)
+                    return carry
+
+                lax.fori_loop(0, HALF // 16, add, 0)
                 self.line_copy(n, k, i).start()
 
     def across_copy(self, k, i):
@@ -687,18 +666,16 @@
         )
 
     def line_add(self, k, i):
-        kind = self.kind(k)
-
         @pl.when(self.p.c == k % 2)
         def _():
-            for n in range(3):
+            for n in (0, 1):
                 self.line_copy(n, k, i).wait_recv()
 
             def add(step, carry):
                 rows = pl.ds(pl.multiple_of(step * 16, 16), 16)
                 total = self.grads[4 * self.p.z + k, i, rows, :].astype(F32)
-                for n in range(3):
-                    total = total + self.line[n, kind, i, rows, :].astype(F32)
+                for n in (0, 1):
+                    total = total + self.line[k // 2, n, i, rows, :].astype(F32)
                 self.grads[4 * self.p.z + k, i, rows, :] = total.astype(BF)
 
                 @pl.when(self.p.x == k // 2)
@@ -728,7 +705,8 @@
 
                 @pl.when(self.p.c == k % 2)
                 def _():
-                    for n in range(3):
+                    for n in (0, 1):
+                        self.half_copy(n, k, i).wait_send()
                         self.line_copy(n, k, i).wait_send()
 
                     @pl.when(self.p.x != k // 2)
@@ -740,17 +718,17 @@
     lengths, alive_row, alive_col, gains, shifts, dn2_part, gt, dft, ot, lse, hidden, unit_rows, qt,
     tokens_any, cot_any, dffn_any, low2_any, low1_any, window_any, proj_any, ffn_any,
     out_any, grad_any, result, vec_out, unit_out,
-    grads, pair, line, last, window, d_kv, kv_pair, kv_far, dffn, low2, low1, proj, ffn_part, x_mine, cot_mine,
+    grads, pair, half, line, last, window, d_kv, kv_pair, kv_far, dffn, low2, low1, proj, ffn_part, x_mine, cot_mine,
     branch, out_whole, in_whole, dn1_part, land, q_rows, q_cols, do_rows, do_cols, delta, dqt, dkv_sum, d_hidden,
     bank, bank_land, small, small_pair, small_all, bank_back,
-    rs_send, rs_recv, ag_send, ag_recv, pair_send, pair_recv, line_send, line_recv, last_send, last_recv,
-    kv_bsend, kv_brecv, kv_send, kv_recv, v1_send, v1_recv, v2_send, v2_recv, v3_send, v3_recv, v4_send, v4_recv,
+    rs_send, rs_recv, ag_send, ag_recv, pair_send, pair_recv, half_send, half_recv,
+    line_send, line_recv, last_send, last_recv, kv_bsend, kv_brecv, kv_send, kv_recv, v1_send, v1_recv, v2_send, v2_recv, v3_send, v3_recv, v4_send, v4_recv,
     load_sem, out_sem,
 ):
     p = Place()
     sums = PanelSums(
-        p, grads, pair, line, last, result,
-        (pair_send, pair_recv, line_send, line_recv, last_send, last_recv),
+        p, grads, pair, half, line, last, result,
+        (pair_send, pair_recv, half_send, half_recv, line_send, line_recv, last_send, last_recv),
     )
     mine = pl.ds(pl.multiple_of(p.t * SHARD, SHARD), SHARD)
     sources = [
@@ -777,12 +755,19 @@
 
     loads[0].wait()
     loads[1].wait()
-    for n in (0, 1, 2, 3):
-        kinds_grad(8 + n, gt[n * SPAN : (n + 1) * SPAN, :], dffn)
-        sums.to_pair((8 + n) // 3, (8 + n) % 3)
-    for n in (2, 3, 0, 1):
-        kinds_grad(4 + n, dft[n * SPAN : (n + 1) * SPAN, :], low2)
-        sums.to_pair((4 + n) // 3, (4 + n) % 3)
+    early = []
+    for j in (9, 8, 4, 10, 6, 5, 11, 7):
+        n = j % 4
+        if j >= 8:
+            kinds_grad(j, gt[n * SPAN : (n + 1) * SPAN, :], dffn)
+        else:
+            kinds_grad(j, dft[n * SPAN : (n + 1) * SPAN, :], low2)
+        sums.to_pair(j // 3, j % 3)
+        early.append((j // 3, j % 3))
+        if len(early) > 1:
+            sums.pair_add(*early[-2])
+        if len(early) > 4:
+            sums.line_mid(*early[-5])
 
     loads[2].wait()
     loads[3].wait()
@@ -811,9 +796,9 @@
     to_bank(6, jnp.zeros((1, WIDTH), F32))
     to_bank(7, jnp.zeros((1, WIDTH), F32))
 
-    early = ((3, 0), (3, 1), (3, 2), (2, 2), (2, 0), (2, 1), (1, 1), (1, 2))
-    for k, i in early:
-        sums.pair_add(k, i)
+    sums.pair_add(*early[-1])
+    for k, i in early[-4:]:
+        sums.line_mid(k, i)
 
     loads[4].wait()
     loads[5].wait()
@@ -911,6 +896,12 @@
         copy.wait()
     summed = scatter_sum(p, ffn_part, land.at[1])
     out_whole[mine, :] = (hidden[...] + live * (summed + shifts[1:2, :])).astype(BF)
+    out_gather = gather_copies(p, out_whole, ag_send.at[1], ag_recv.at[1])
+    for copy in out_gather:
+        copy.start()
+    sums.pair_add(0, 0)
+    for k, i in early:
+        sums.line_add(k, i)
 
     dkv_sum[...] = d_kv[0, p.c].astype(F32)
     for d in (1, 2, 3, 4):
@@ -939,14 +930,13 @@
     sums.to_pair(0, 1)
     kinds_grad(2, dkv_t[SPAN:], low1)
     sums.to_pair(0, 2)
-    for i in range(3):
+    sums.line_mid(1, 0)
+    sums.line_mid(0, 0)
+    for i in (1, 2):
         sums.pair_add(0, i)
-    out_gather = gather_copies(p, out_whole, ag_send.at[1], ag_recv.at[1])
-    for copy in out_gather:
-        copy.start()
-    for k, i in early:
-        sums.line_add(k, i)
     sums.line_add(1, 0)
+    for i in (1, 2):
+        sums.line_mid(0, i)
 
     _, unit1, factor1 = normalize(x_mine[...].astype(F32), gains[0:1, :], shifts[2:3, :])
     for copy in last_scatter:
@@ -954,9 +944,6 @@
     d_norm1 = scatter_sum(p, dn1_part, land.at[2])
     d_in, d_gain1, d_shift1 = norm_back(d_norm1, unit1, factor1, gains[0:1, :])
     in_whole[mine, :] = (d_hidden[...] + d_in).astype(BF)
-    last_gather = gather_copies(p, in_whole, ag_send.at[2], ag_recv.at[2])
-    for copy in last_gather:
-        copy.start()
     to_bank(0, d_gain1)
     to_bank(4, d_shift1)
 
@@ -966,6 +953,11 @@
         slices.append(remote(bank.at[to], bank_land.at[n], v1_send.at[n], v1_recv.at[n], {"tensor": to}))
     for copy in slices:
         copy.start()
+    last_gather = gather_copies(p, in_whole, ag_send.at[2], ag_recv.at[2])
+    for copy in last_gather:
+        copy.start()
+    for i in range(3):
+        sums.line_add(0, i)
     for copy in slices:
         copy.wait()
     total = bank[p.t]
@@ -974,10 +966,6 @@
     small[0:8, :] = total
     pair_small = remote(small, small_pair, v2_send, v2_recv, p.sibling())
     pair_small.start()
-
-    for i in range(3):
-        sums.line_add(0, i)
-
     pair_small.wait()
     here = p.z * 2 + p.x
     small_all[here] = small[...] + small_pair[...]
@@ -1056,7 +1044,8 @@
         scratch_shapes=[
             pltpu.VMEM((16, 3, HD, WIDTH), BF),
             pltpu.VMEM((8, 3, HD, WIDTH), BF),
-            pltpu.VMEM((3, 2, 3, HD, WIDTH), BF),
+            pltpu.VMEM((2, 2, 3, HALF, WIDTH), BF),
+            pltpu.VMEM((2, 2, 3, HD, WIDTH), BF),
             pltpu.VMEM((3, HD, WIDTH), BF),
             pltpu.VMEM((5, 2, EXT, 2 * SPAN), BF),
             pltpu.VMEM((5, 2, ROWS, 2 * SPAN), BF),
@@ -1079,7 +1068,7 @@
             pltpu.VMEM((8, 16, 256), F32),
             pltpu.VMEM((8, 8, 256), F32),
             dma((3, 7)), dma((3, 7)), dma((3, 7)), dma((3, 7)),
-            dma((8, 3)), dma((8, 3)), dma((3, 2, 3)), dma((3, 2, 3)), dma((3,)), dma((3,)),
+            dma((8, 3)), dma((8, 3)), dma((2, 2, 3)), dma((2, 2, 3)), dma((2, 2, 3)), dma((2, 2, 3)), dma((3,)), dma((3,)),
             dma((5,)), dma((5,)), dma((5,)), dma((5,)),
             dma((7,)), dma((7,)), dma, dma, dma((7,)), dma((7,)), dma((7,)), dma((7,)),
             dma((8,)), dma((2,)),

time: 309 us -> 253 us (0.82)
  Pallas kernels: 295 us -> 237 us
    pallas_call x1, Pallas kernels: 172 us -> 128 us  [backward_call(): pl.pallas_call(backward_kernel, in_specs=[pl.BlockSpec(memory_space=pltpu...]
    pallas_call x1, Pallas kernels: 115 us -> 101 us  [forward_call(): pl.pallas_call(forward_kernel, in_specs=[pl.BlockSpec(memory_space=pltpu....]
where the time goes in v3:
time: 253 us; the launch traced here: 250 us
  Pallas kernels  237 us (94%)
  local copies, waits for them, and re-layouts  7.29 us (3%)
  other arithmetic  5.5 us (2%)
    pallas_call x1, Pallas kernels, backward_call(): pl.pallas_call(backward_kernel, in_specs=[pl.BlockSpec(memory_space=pltpu...  128 us
    pallas_call x1, Pallas kernels, forward_call(): pl.pallas_call(forward_kernel, in_specs=[pl.BlockSpec(memory_space=pltpu....  101 us
    pallas_call x1, Pallas kernels, muon_call(): pl.pallas_call(muon_kernel, in_specs=[vmem] * 3, out_specs=[vmem, vmem],...  7.81 us

profile of v3, /device:TPU:0, one launch (start us, length us, event | category | flops | bytes accessed | tf_op | source)
XLA Modules:
  0.0 250.5 jit_solution(11191643003584843892)
XLA Ops:
  0.6 0.7 compare_convert_fusion
  1.3 0.8 copy.26.alive_col
  2.1 1.5 copy.24
  3.6 0.0 copy-done.8
  3.6 101.0 %layer_forward.1 = (bf16[256,2048]{1,0:T(8,128)(2,1)}, bf16[256,256]{1,0:T(8,128)(2,1)}, bf16[5,2,272,512]{3,2,1,0:T(8,128)(2,1)}, f32[256,256]{1,0:T(8,128)}, f...) custom-call(s32[4]{0:T(128)} %lengths.3, ...), custom_call_target="tpu_custom_call" | custom-call | tf_op jit(solution)/shard_map/layer_forward/pallas_call | solution.py:518
  104.6 0.0 copy-start.7
  104.6 0.0 copy-start.10
  104.6 0.0 copy-start.5
  104.6 0.0 copy-start.9
  104.6 0.0 copy-start.4
  104.7 0.0 copy-start.6
  104.7 128.2 %layer_backward.1 = (bf16[256,2048]{1,0:T(8,128)(2,1)}, bf16[256,2048]{1,0:T(8,128)(2,1)}, f32[3,64,2048]{2,1,0:T(8,128)}, f32[8,8,256]{2,1,0:T(8,128)}, f32[8,256]{1,0:T(8,128)}) custom-call(s32[4]{0:T(128)} %lengths.3, f32[1,256]{1,0:T(1,128)} %bitcast.18, f32[256,1]{1,0:T(8,128)} %copy.26.alive_col, f32[2,2048]{1,0:T(2,128)} %gains.3, f32[4,2048]{1,0:T(4,128)} %shifts.3, ...), custom_call_target="tpu_custom_call" | custom-call | tf_op jit(solution)/shard_map/layer_backward/pallas_call | solution.py:1033
  232.9 0.8 reshape.29
  233.6 0.1 reshape.30
  233.7 0.0 copy-done.10
  233.7 0.6 multiply_subtract_fusion.2
  234.3 0.8 slice.20
  235.2 0.8 slice.21
  236.0 0.6 multiply_subtract_fusion.1
  236.7 0.6 multiply_subtract_fusion
  237.3 2.9 %convert_element_type.7 = f32[256,2048]{1,0:T(8,128)} convert(bf16[256,2048]{1,0:T(8,128)(2,1)} %get-tuple-element.46) | non-fusion elementwise | flops 524288 | bytes 3145728 | tf_op jit(solution)/shard_map/convert_element_type | solution.py:1157
  240.3 1.4 copy-done.2
  241.7 7.8 %panel_step.1 = (f32[3,64,2048]{2,1,0:T(8,128)}, f32[3,64,2048]{2,1,0:T(8,128)}) custom-call(f32[3,64,2048]{2,1,0:T(8,128)S(1)} %copy-done.2, f32[3,64,2048]{2,1,0:T(8,128)S(1)} %copy-done.1, f32[3,64,2048]{2,1,0:T(8,128)S(1)} %copy-done), custom_call_target="tpu_custom_call" | custom-call | tf_op jit(solution)/shard_map/panel_step/pallas_call | solution.py:1125
  249.5 1.0 copy.31
  (14 shorter events, 0.0 us)
Async XLA Ops:
  1.3 2.3 copy-start.8
  104.6 129.1 %copy-start.7 = (f32[4,384]{1,0:T(4,128)S(1)}, f32[4,384]{1,0:T(4,128)}, u32[]{:S(2)}) copy-start(f32[4,384]{1,0:T(4,128)} %param.18) | copy-start | bytes 18436
  104.6 129.1 %copy-start.10 = (f32[4,384]{1,0:T(4,128)S(1)}, f32[4,384]{1,0:T(4,128)}, u32[]{:S(2)}) copy-start(f32[4,384]{1,0:T(4,128)} %param.19) | copy-start | bytes 18436
  104.6 131.4 %copy-start.5 = (f32[2,2048]{1,0:T(2,128)S(1)}, f32[2,2048]{1,0:T(2,128)}, u32[]{:S(2)}) copy-start(f32[2,2048]{1,0:T(2,128)} %gains.3) | copy-start | bytes 49156
  104.6 131.4 %copy-start.9 = (f32[2,2048]{1,0:T(2,128)S(1)}, f32[2,2048]{1,0:T(2,128)}, u32[]{:S(2)}) copy-start(f32[2,2048]{1,0:T(2,128)} %param.21) | copy-start | bytes 49156
  104.6 132.0 %copy-start.4 = (f32[4,2048]{1,0:T(4,128)S(1)}, f32[4,2048]{1,0:T(4,128)}, u32[]{:S(2)}) copy-start(f32[4,2048]{1,0:T(4,128)} %shifts.3) | copy-start | bytes 98308
  104.7 132.0 %copy-start.6 = (f32[4,2048]{1,0:T(4,128)S(1)}, f32[4,2048]{1,0:T(4,128)}, u32[]{:S(2)}) copy-start(f32[4,2048]{1,0:T(4,128)} %param.23) | copy-start | bytes 98308
  237.3 2.9 %copy-start = (f32[3,64,2048]{2,1,0:T(8,128)S(1)}, f32[3,64,2048]{2,1,0:T(8,128)}, u32[]{:S(2)}) copy-start(f32[3,64,2048]{2,1,0:T(8,128)} %panels.3) | copy-start | bytes 4718596
  237.3 2.9 %copy-start.1 = (f32[3,64,2048]{2,1,0:T(8,128)S(1)}, f32[3,64,2048]{2,1,0:T(8,128)}, u32[]{:S(2)}) copy-start(f32[3,64,2048]{2,1,0:T(8,128)} %panel_mom.1) | copy-start | bytes 4718596
  240.3 1.4 copy-start.2
  241.7 7.8 %copy-start.3 = (bf16[256,2048]{1,0:T(8,128)(2,1)S(1)}, bf16[256,2048]{1,0:T(8,128)(2,1)}, u32[]{:S(2)}) copy-start(bf16[256,2048]{1,0:T(8,128)(2,1)} %get-tuple-element.68) | copy-start | bytes 3145732

commit v4 on v3

--- a/solution.py
+++ b/solution.py
@@ -136,6 +136,10 @@
     return jnp.sum(jnp.where(down == over, row, 0.0), axis=1, keepdims=True)
 
 
+def alive_of(exits):
+    return jnp.where(exits[...] >= LAYER, 1.0, 0.0)
+
+
 def segment_of(positions, lengths):
     end = jnp.int32(0)
     segment = jnp.zeros(positions.shape, F32)
@@ -262,10 +266,10 @@
 
 
 def forward_kernel(
-    lengths, tokens, cotangent, alive_row, alive_col, panels, bias_t, gains, shifts,
+    lengths, tokens, cotangent, exits, panels, unit_bias, gains, shifts,
     low1_out, qt_out, window_out, ot_out, lse_out, hidden_out, low2_out, gt_out, dft_out, ffn_out, dn2_out, proj_out,
     dffn_out, unit_out,
-    store, window, low1, qt, acc, top, mass, part, land, whole, g_rows, df_rows, dft, gt, dffn,
+    store, window, low1, qt, acc, top, mass, part, land, whole, g_rows, df_rows, dft, gt, dffn, alive_col, q_rows,
     w_recv, w_across, w_along, w_half_send, w_half_recv, w_beside, kv_send, kv_recv, kv_bsend, kv_brecv, rs_send, rs_recv, ag_send, ag_recv, out_sem,
 ):
     p = Place()
@@ -279,6 +283,9 @@
 
     for i in order:
         w.across(0, i)
+    alive_row = alive_of(exits)
+    alive_col[...] = column_of(alive_row)
+    bias_t = jnp.concatenate([unit_bias[...], unit_bias[...]], axis=0).T
     for k in (2, 3):
         for i in range(3):
             w.across(k, i)
@@ -302,9 +309,11 @@
         for i in order:
             w.along(0, i)
 
+    w.pass_on(0, 1)
+    w.pass_on(0, 2)
     for i in order:
-        w.pass_on(0, i)
-    for i in order:
+        if i == 2:
+            w.pass_on(0, 0)
         w.far_in(0, i)
         w.beside_in(0, i)
         made = nt(w.kind_panels(i), low1[...])
@@ -313,7 +322,7 @@
         elif i == 2:
             bias = jnp.concatenate([bias_t[HD : 2 * HD, u : u + 1] for u in range(GROUPS)], axis=0)
             window[0, p.c, 0:ROWS, SPAN : 2 * SPAN] = (made + bias).astype(BF).T
-            row = jnp.broadcast_to(alive_row[...], (16, ROWS)).astype(BF)
+            row = jnp.broadcast_to(alive_row, (16, ROWS)).astype(BF)
             window[0, p.c, ROWS:EXT, 0:SPAN] = row
             window[0, p.c, ROWS:EXT, SPAN : 2 * SPAN] = jnp.zeros((16, SPAN), BF)
             mine = window.at[0, p.c]
@@ -340,23 +349,27 @@
     acc[...] = jnp.zeros_like(acc)
     top[...] = jnp.full_like(top, FLOOR)
     mass[...] = jnp.zeros_like(mass)
-    code, at = query_code(p, lengths, alive_row[...])
+    code, at = query_code(p, lengths, alive_row)
     scaled = (qt[...].astype(F32) * (HD ** -0.5)).astype(BF)
+    for u in range(GROUPS):
+        q_rows[u] = head_rows(scaled, u)
 
     def attend(d, core):
         bias = block_bias(p, lengths, window, d, core, code, at)
         keys = window[d, core, 0:ROWS, 0:SPAN]
         values_t = window[d, core, 0:ROWS, SPAN : 2 * SPAN].T
+        old = top[0:GROUPS, :]
+        scores = [nn(keys, q_rows[u]) + bias for u in range(GROUPS)]
+        new = jnp.maximum(old, jnp.concatenate([jnp.max(s, axis=0, keepdims=True) for s in scores], axis=0))
+        fade = jnp.exp(old - new)
+        top[0:GROUPS, :] = new
+        weights = [jnp.exp(s - new[u : u + 1, :]) for u, s in enumerate(scores)]
+        sums = jnp.concatenate([jnp.sum(e, axis=0, keepdims=True) for e in weights], axis=0)
+        mass[0:GROUPS, :] = mass[0:GROUPS, :] * fade + sums
         for u in range(GROUPS):
             heads = slice(u * HD, (u + 1) * HD)
-            score = nn(keys, head_rows(scaled, u)) + bias
-            old = top[u : u + 1, :]
-            new = jnp.maximum(old, jnp.max(score, axis=0, keepdims=True))
-            weight = jnp.exp(score - new)
-            fade = jnp.exp(old - new)
-            top[u : u + 1, :] = new
-            mass[u : u + 1, :] = mass[u : u + 1, :] * fade + jnp.sum(weight, axis=0, keepdims=True)
-            acc[heads, :] = acc[heads, :] * fade + nn(values_t[heads, :], weight.astype(BF))
+            mixed = nn(values_t[heads, :], weights[u].astype(BF))
+            acc[heads, :] = acc[heads, :] * fade[u : u + 1, :] + mixed
 
     def attend_chip(d):
         def body(core, carry):
@@ -510,14 +523,14 @@
         copy.wait()
 
 
-def forward_call(lengths, tokens, cotangent, alive_row, alive_col, panels, bias_t, gains, shifts):
+def forward_call(lengths, tokens, cotangent, exits, panels, unit_bias, gains, shifts):
     vmem = pl.BlockSpec(memory_space=pltpu.VMEM)
     anywhere = pl.BlockSpec(memory_space=pl.ANY)
     shape = jax.ShapeDtypeStruct
     dma = pltpu.SemaphoreType.DMA
     return pl.pallas_call(
         forward_kernel,
-        in_specs=[pl.BlockSpec(memory_space=pltpu.SMEM)] + [vmem] * 8,
+        in_specs=[pl.BlockSpec(memory_space=pltpu.SMEM)] + [vmem] * 7,
         out_specs=[anywhere, anywhere, anywhere, vmem, vmem, vmem, anywhere, vmem, vmem, vmem, vmem, anywhere, anywhere, vmem],
         out_shape=[
             shape((ROWS, WIDTH), BF),
@@ -551,6 +564,8 @@
             pltpu.VMEM((UNITS, ROWS), BF),
             pltpu.VMEM((UNITS, ROWS), BF),
             pltpu.VMEM((ROWS, WIDTH), BF),
+            pltpu.VMEM((ROWS, 1), F32),
+            pltpu.VMEM((GROUPS, SPAN, ROWS), BF),
             dma((16, 3)), dma((3,)), dma((2, 2, 3)), dma((2, 2, 3)), dma((2, 2, 3)), dma((2, 4, 3)),
             dma((5,)), dma((5,)), dma((5,)), dma((5,)),
             dma((7,)), dma((7,)), dma((7,)), dma((7,)), dma((13,)),
@@ -559,7 +574,7 @@
             collective_id=0, has_side_effects=True, vmem_limit_bytes=56 * 2**20
         ),
         name="layer_forward",
-    )(lengths, tokens, cotangent, alive_row, alive_col, panels, bias_t, gains, shifts)
+    )(lengths, tokens, cotangent, exits, panels, unit_bias, gains, shifts)
 
 
 def head_columns(values, head):
@@ -715,13 +730,13 @@
 
 
 def backward_kernel(
-    lengths, alive_row, alive_col, gains, shifts, dn2_part, gt, dft, ot, lse, hidden, unit_rows, qt,
+    lengths, exits, gains, shifts, dn2_part, gt, dft, ot, lse, hidden, unit_rows, qt,
     tokens_any, cot_any, dffn_any, low2_any, low1_any, window_any, proj_any, ffn_any,
     out_any, grad_any, result, vec_out, unit_out,
-    grads, pair, half, line, last, window, d_kv, kv_pair, kv_far, dffn, low2, low1, proj, ffn_part, x_mine, cot_mine,
+    grads, pair, half, line, last, window, d_kv, kv_pair, kv_far, dffn, low2, low1, proj, ffn_part, x_rows, cot_mine,
     branch, out_whole, in_whole, dn1_part, land, q_rows, q_cols, do_rows, do_cols, delta, dqt, dkv_sum, d_hidden,
-    bank, bank_land, small, small_pair, small_all, bank_back,
-    rs_send, rs_recv, ag_send, ag_recv, pair_send, pair_recv, half_send, half_recv,
+    bank, bank_land, small, small_pair, small_all, bank_back, alive_col, norm1_mean, norm1_factor, mid, y_land, h_land,
+    rs_send, rs_recv, ag_send, ag_recv, ys_send, ys_recv, hs_send, hs_recv, pair_send, pair_recv, half_send, half_recv,
     line_send, line_recv, last_send, last_recv, kv_bsend, kv_brecv, kv_send, kv_recv, v1_send, v1_recv, v2_send, v2_recv, v3_send, v3_recv, v4_send, v4_recv,
     load_sem, out_sem,
 ):
@@ -732,7 +747,7 @@
     )
     mine = pl.ds(pl.multiple_of(p.t * SHARD, SHARD), SHARD)
     sources = [
-        (dffn_any, dffn), (low2_any, low2), (tokens_any.at[mine], x_mine), (cot_any.at[mine], cot_mine),
+        (dffn_any, dffn), (low2_any, low2), (tokens_any, x_rows), (cot_any.at[mine], cot_mine),
         (proj_any, proj), (window_any, window), (low1_any, low1), (ffn_any, ffn_part),
     ]
     loads = [pltpu.make_async_copy(a, b, load_sem.at[n]) for n, (a, b) in enumerate(sources)]
@@ -753,24 +768,35 @@
 
         lax.fori_loop(0, WIDTH // 256, tile, 0)
 
+    def four_grads(first, left, right):
+        def tile(n, carry):
+            cols = pl.ds(pl.multiple_of(n * 256, 256), 256)
+            made = nn(left[...], right[:, cols]).astype(BF)
+            for j in range(4):
+                for u in range(GROUPS):
+                    at_row = j * SPAN + u * HD
+                    grads[4 * u + (first + j) // 3, (first + j) % 3, :, cols] = made[at_row : at_row + HD]
+            return carry
+
+        lax.fori_loop(0, WIDTH // 256, tile, 0)
+
     loads[0].wait()
     loads[1].wait()
-    early = []
-    for j in (9, 8, 4, 10, 6, 5, 11, 7):
-        n = j % 4
-        if j >= 8:
-            kinds_grad(j, gt[n * SPAN : (n + 1) * SPAN, :], dffn)
-        else:
-            kinds_grad(j, dft[n * SPAN : (n + 1) * SPAN, :], low2)
+    four_grads(8, gt, dffn)
+    for j in (9, 10, 11, 8):
+        sums.to_pair(j // 3, j % 3)
+    four_grads(4, dft, low2)
+    early = [(3, 0), (3, 1), (3, 2), (2, 2)]
+    for j in (6, 4, 7, 5):
         sums.to_pair(j // 3, j % 3)
         early.append((j // 3, j % 3))
-        if len(early) > 1:
-            sums.pair_add(*early[-2])
-        if len(early) > 4:
-            sums.line_mid(*early[-5])
+    for k, i in early:
+        sums.pair_add(k, i)
 
     loads[2].wait()
     loads[3].wait()
+    alive_row = alive_of(exits)
+    alive_col[...] = column_of(alive_row)
     live = alive_col[mine, :]
     grad_out = cot_mine[...].astype(F32)
     _, unit2, factor2 = normalize(hidden[...], gains[1:2, :], shifts[3:4, :])
@@ -796,8 +822,7 @@
     to_bank(6, jnp.zeros((1, WIDTH), F32))
     to_bank(7, jnp.zeros((1, WIDTH), F32))
 
-    sums.pair_add(*early[-1])
-    for k, i in early[-4:]:
+    for k, i in early:
         sums.line_mid(k, i)
 
     loads[4].wait()
@@ -809,7 +834,7 @@
         q_cols[u] = head_columns(scaled_rows, u)
     dqt[...] = jnp.zeros_like(dqt)
     dkv_sum[...] = jnp.zeros_like(dkv_sum)
-    code, at = query_code(p, lengths, alive_row[...])
+    code, at = query_code(p, lengths, alive_row)
 
     for copy in first_gather:
         copy.wait()
@@ -822,7 +847,19 @@
         do_cols[u] = head_columns(do_turned, u)
         delta[u : u + 1, :] = jnp.sum(do_t[heads, :].astype(F32) * ot[heads, :], axis=0, keepdims=True)
     loads[7].wait()
-    out_scatter = scatter_copies(p, ffn_part, land.at[1], rs_send.at[1], rs_recv.at[1])
+    both = pl.ds(pl.multiple_of(p.y * 2 * SHARD, 2 * SHARD), 2 * SHARD)
+    out_scatter, out_spread = [], []
+    for n in range(3):
+        to_y = (p.y + n + 1) % 4
+        to = {"tensor": to_y * 2 + p.h}
+        theirs = pl.ds(pl.multiple_of(to_y * 2 * SHARD, 2 * SHARD), 2 * SHARD)
+        out_scatter.append(remote(ffn_part.at[theirs], y_land.at[n], ys_send.at[0, n], ys_recv.at[0, n], to))
+        out_spread.append(remote(out_whole.at[both], out_whole.at[both], ys_send.at[1, n], ys_recv.at[1, n], to))
+    partner = {"tensor": p.y * 2 + 1 - p.h}
+    near = pl.ds(pl.multiple_of(p.h * SHARD, SHARD), SHARD)
+    away = pl.ds(pl.multiple_of((1 - p.h) * SHARD, SHARD), SHARD)
+    out_swap = remote(mid.at[away], h_land, hs_send.at[0], hs_recv.at[0], partner)
+    out_join = remote(out_whole.at[mine], out_whole.at[mine], hs_send.at[1], hs_recv.at[1], partner)
     for copy in out_scatter:
         copy.start()
     kinds_grad(3, ot[...].astype(BF), branch)
@@ -883,6 +920,13 @@
     lax.fori_loop(0, 10, block_back, 0)
     finish(0)
     sums.pair_add(1, 0)
+    for copy in out_scatter:
+        copy.wait()
+    summed = ffn_part[both, :].astype(F32)
+    for n in range(3):
+        summed = summed + y_land[n].astype(F32)
+    mid[...] = summed.astype(BF)
+    out_swap.start()
 
     dq_t = (dqt[...] * (HD ** -0.5)).astype(BF)
     dq = dq_t.T
@@ -892,16 +936,25 @@
     kinds_grad(0, dq_t, low1)
     sums.to_pair(0, 0)
 
-    for copy in out_scatter:
-        copy.wait()
-    summed = scatter_sum(p, ffn_part, land.at[1])
-    out_whole[mine, :] = (hidden[...] + live * (summed + shifts[1:2, :])).astype(BF)
-    out_gather = gather_copies(p, out_whole, ag_send.at[1], ag_recv.at[1])
-    for copy in out_gather:
-        copy.start()
-    sums.pair_add(0, 0)
     for k, i in early:
         sums.line_add(k, i)
+
+    out_swap.wait()
+    summed = mid[near, :].astype(F32) + h_land[...].astype(F32)
+    out_whole[mine, :] = (hidden[...] + live * (summed + shifts[1:2, :])).astype(BF)
+    out_join.start()
+    sums.pair_add(0, 0)
+
+    def stats(r, carry):
+        rows = pl.ds(pl.multiple_of(r * 32, 32), 32)
+        values = x_rows[rows, :].astype(F32)
+        mean = jnp.mean(values, axis=-1, keepdims=True)
+        centred = values - mean
+        norm1_mean[rows, :] = mean
+        norm1_factor[rows, :] = lax.rsqrt(jnp.mean(centred * centred, axis=-1, keepdims=True) + EPS)
+        return carry
+
+    lax.fori_loop(0, ROWS // 32, stats, 0)
 
     dkv_sum[...] = d_kv[0, p.c].astype(F32)
     for d in (1, 2, 3, 4):
@@ -920,44 +973,25 @@
         for i, left in enumerate((dq, dkv[:, :SPAN], dkv[:, SPAN:])):
             total = total + nn(left, jnp.concatenate([proj[u, i, :, cols] for u in range(GROUPS)], axis=0))
         dn1_part[:, cols] = total.astype(BF)
+        unit = (x_rows[:, cols].astype(F32) - norm1_mean[...]) * norm1_factor[...]
+        bank[n, 0:1, :] = jnp.sum(total * unit, axis=0, keepdims=True)
+        bank[n, 4:5, :] = jnp.sum(total, axis=0, keepdims=True)
         return carry
 
     lax.fori_loop(0, WIDTH // 256, norm1_part, 0)
-    last_scatter = scatter_copies(p, dn1_part, land.at[2], rs_send.at[2], rs_recv.at[2])
+    slices = []
+    for n, (dy, dx) in enumerate(T_STEPS):
+        to = p.tensor_at(dy, dx)
+        slices.append(remote(bank.at[to], bank_land.at[n], v1_send.at[n], v1_recv.at[n], {"tensor": to}))
+    for copy in slices:
+        copy.start()
+    last_scatter = scatter_copies(p, dn1_part, land.at[1], rs_send.at[1], rs_recv.at[1])
     for copy in last_scatter:
         copy.start()
     kinds_grad(1, dkv_t[:SPAN], low1)
     sums.to_pair(0, 1)
     kinds_grad(2, dkv_t[SPAN:], low1)
     sums.to_pair(0, 2)
-    sums.line_mid(1, 0)
-    sums.line_mid(0, 0)
-    for i in (1, 2):
-        sums.pair_add(0, i)
-    sums.line_add(1, 0)
-    for i in (1, 2):
-        sums.line_mid(0, i)
-
-    _, unit1, factor1 = normalize(x_mine[...].astype(F32), gains[0:1, :], shifts[2:3, :])
-    for copy in last_scatter:
-        copy.wait()
-    d_norm1 = scatter_sum(p, dn1_part, land.at[2])
-    d_in, d_gain1, d_shift1 = norm_back(d_norm1, unit1, factor1, gains[0:1, :])
-    in_whole[mine, :] = (d_hidden[...] + d_in).astype(BF)
-    to_bank(0, d_gain1)
-    to_bank(4, d_shift1)
-
-    slices = []
-    for n, (dy, dx) in enumerate(T_STEPS):
-        to = p.tensor_at(dy, dx)
-        slices.append(remote(bank.at[to], bank_land.at[n], v1_send.at[n], v1_recv.at[n], {"tensor": to}))
-    for copy in slices:
-        copy.start()
-    last_gather = gather_copies(p, in_whole, ag_send.at[2], ag_recv.at[2])
-    for copy in last_gather:
-        copy.start()
-    for i in range(3):
-        sums.line_add(0, i)
     for copy in slices:
         copy.wait()
     total = bank[p.t]
@@ -975,8 +1009,17 @@
         spread.append(remote(small_all.at[here], small_all.at[here], v3_send.at[n - 1], v3_recv.at[n - 1], to))
     for copy in spread:
         copy.start()
-    for i in range(3):
-        sums.last_add(i)
+    sums.line_mid(1, 0)
+    sums.line_mid(0, 0)
+    out_join.wait()
+    for copy in out_spread:
+        copy.start()
+    for i in (1, 2):
+        sums.pair_add(0, i)
+    sums.line_add(1, 0)
+    for i in (1, 2):
+        sums.line_mid(0, i)
+
     for copy in spread:
         copy.wait()
     total = small_all[0]
@@ -991,7 +1034,20 @@
     for copy in back:
         copy.start()
 
-    for copy in out_gather:
+    _, unit1, factor1 = normalize(x_rows[mine, :].astype(F32), gains[0:1, :], shifts[2:3, :])
+    for copy in last_scatter:
+        copy.wait()
+    d_norm1 = scatter_sum(p, dn1_part, land.at[1])
+    d_in, _, _ = norm_back(d_norm1, unit1, factor1, gains[0:1, :])
+    in_whole[mine, :] = (d_hidden[...] + d_in).astype(BF)
+    last_gather = gather_copies(p, in_whole, ag_send.at[1], ag_recv.at[1])
+    for copy in last_gather:
+        copy.start()
+    for i in range(3):
+        sums.line_add(0, i)
+    for i in range(3):
+        sums.last_add(i)
+    for copy in out_spread:
         copy.wait()
     for copy in last_gather:
         copy.wait()
@@ -1020,7 +1076,7 @@
 
 
 def backward_call(
-    lengths, alive_row, alive_col, gains, shifts, dn2_part, gt, dft, ot, lse, hidden, unit_rows, qt,
+    lengths, exits, gains, shifts, dn2_part, gt, dft, ot, lse, hidden, unit_rows, qt,
     tokens, cotangent, dffn, low2, low1, window, proj, ffn_part,
 ):
     vmem = pl.BlockSpec(memory_space=pltpu.VMEM)
@@ -1032,7 +1088,7 @@
     masked = pltpu.VMEM((GROUPS, SPAN, ROWS), BF)
     return pl.pallas_call(
         backward_kernel,
-        in_specs=[pl.BlockSpec(memory_space=pltpu.SMEM)] + [vmem] * 12 + [anywhere] * 8,
+        in_specs=[pl.BlockSpec(memory_space=pltpu.SMEM)] + [vmem] * 11 + [anywhere] * 8,
         out_specs=[anywhere, anywhere, vmem, vmem, vmem],
         out_shape=[
             shape((ROWS, WIDTH), BF),
@@ -1053,9 +1109,9 @@
             pltpu.VMEM((5, ROWS, 2 * SPAN), BF),
             rows_low, rows_low, rows_low,
             pltpu.VMEM((GROUPS, 4, HD, WIDTH), BF),
-            rows_low, shard_low, shard_low,
+            rows_low, rows_low, shard_low,
             rows_low, rows_low, rows_low, rows_low,
-            pltpu.VMEM((3, 7, SHARD, WIDTH), BF),
+            pltpu.VMEM((2, 7, SHARD, WIDTH), BF),
             masked, masked, masked, masked,
             pltpu.VMEM((8, ROWS), F32),
             pltpu.VMEM((SPAN, ROWS), F32),
@@ -1067,7 +1123,14 @@
             pltpu.VMEM((16, 256), F32),
             pltpu.VMEM((8, 16, 256), F32),
             pltpu.VMEM((8, 8, 256), F32),
-            dma((3, 7)), dma((3, 7)), dma((3, 7)), dma((3, 7)),
+            pltpu.VMEM((ROWS, 1), F32),
+            pltpu.VMEM((ROWS, 1), F32),
+            pltpu.VMEM((ROWS, 1), F32),
+            pltpu.VMEM((2 * SHARD, WIDTH), BF),
+            pltpu.VMEM((3, 2 * SHARD, WIDTH), BF),
+            shard_low,
+            dma((2, 7)), dma((2, 7)), dma((2, 7)), dma((2, 7)),
+            dma((2, 3)), dma((2, 3)), dma((2,)), dma((2,)),
             dma((8, 3)), dma((8, 3)), dma((2, 2, 3)), dma((2, 2, 3)), dma((2, 2, 3)), dma((2, 2, 3)), dma((3,)), dma((3,)),
             dma((5,)), dma((5,)), dma((5,)), dma((5,)),
             dma((7,)), dma((7,)), dma, dma, dma((7,)), dma((7,)), dma((7,)), dma((7,)),
@@ -1078,7 +1141,7 @@
         ),
         name="layer_backward",
     )(
-        lengths, alive_row, alive_col, gains, shifts, dn2_part, gt, dft, ot, lse, hidden, unit_rows, qt,
+        lengths, exits, gains, shifts, dn2_part, gt, dft, ot, lse, hidden, unit_rows, qt,
         tokens, cotangent, dffn, low2, low1, window, proj, ffn_part,
     )
 
@@ -1087,7 +1150,14 @@
     return jnp.dot(left, right, precision=HIGH, preferred_element_type=F32)
 
 
-def muon_kernel(grads, panel_mom, panels, new_panels, new_mom):
+def step_kernel(
+    grads, panel_mom, panels, vec_sums, unit_sums, unit_bias, unit_bias_mom, gains, gains_mom, vec_bias, vec_bias_mom,
+    in_low, out_low,
+    out_any, in_grad, new_panels, new_mom, new_unit, new_unit_mom, new_gains, new_gains_mom, new_vec, new_vec_mom,
+    sem,
+):
+    whole = pltpu.make_async_copy(out_low, out_any, sem)
+    whole.start()
     count = panels.shape[0]
     eye = jnp.where(
         lax.broadcasted_iota(jnp.int32, (HD, HD), 0) == lax.broadcasted_iota(jnp.int32, (HD, HD), 1), 1.0, 0.0
@@ -1104,6 +1174,20 @@
                 current, current, (((1,), (1,)), ((), ())), precision=HIGH, preferred_element_type=F32
             )
         )
+    in_grad[...] = in_low[...].astype(F32)
+    vec_rows = [jnp.concatenate([vec_sums[n, r : r + 1, :] for n in range(8)], axis=1) for r in range(6)]
+    unit_rows = [
+        jnp.concatenate([unit_sums[n : n + 1, u * HD : (u + 1) * HD] for n in range(6)], axis=1)
+        for u in range(GROUPS)
+    ]
+    for rows, old, old_mom, new, mom in (
+        (vec_rows[0:2], gains, gains_mom, new_gains, new_gains_mom),
+        (vec_rows[2:6], vec_bias, vec_bias_mom, new_vec, new_vec_mom),
+        (unit_rows, unit_bias, unit_bias_mom, new_unit, new_unit_mom),
+    ):
+        moment = DECAY * old_mom[...] + jnp.concatenate(rows, axis=0)
+        mom[...] = moment
+        new[...] = old[...] - LR_VECTOR * moment
     for sweep in range(NS_ITERS):
         squares = [high(a, a) for a in gram]
         steps = [NS_A * eye + NS_B * a + NS_C * s for a, s in zip(gram, squares)]
@@ -1117,47 +1201,44 @@
         held = panels[n]
         size_w = jnp.sum(held * held, axis=(0, 1), keepdims=True)
         new_panels[n] = held - LR_MATRIX * jnp.sqrt(size_w) * lax.rsqrt(size_u + 1e-06) * direction
-
-
-def muon_call(grads, panel_mom, panels):
+    whole.wait()
+
+
+def step_call(*args):
     vmem = pl.BlockSpec(memory_space=pltpu.VMEM)
-    shape = jax.ShapeDtypeStruct(panels.shape, F32)
+    anywhere = pl.BlockSpec(memory_space=pl.ANY)
+    shape = jax.ShapeDtypeStruct
+    panels, unit, gain, vec = (shape(args[n].shape, F32) for n in (2, 5, 7, 9))
     return pl.pallas_call(
-        muon_kernel,
-        in_specs=[vmem] * 3,
-        out_specs=[vmem, vmem],
-        out_shape=[shape, shape],
-        compiler_params=pltpu.CompilerParams(vmem_limit_bytes=32 * 2**20),
+        step_kernel,
+        in_specs=[vmem] * 12 + [anywhere],
+        out_specs=[anywhere] + [vmem] * 9,
+        out_shape=[
+            shape((ROWS, WIDTH), BF), shape((ROWS, WIDTH), F32), panels, panels, unit, unit, gain, gain, vec, vec,
+        ],
+        scratch_shapes=[pltpu.SemaphoreType.DMA],
+        compiler_params=pltpu.CompilerParams(vmem_limit_bytes=40 * 2**20),
         name="panel_step",
-    )(grads, panel_mom, panels)
+    )(*args)
 
 
 def per_device(
     tokens, cotangent, exits, lengths, panels, panel_mom,
     unit_bias, unit_bias_mom, gains, gains_mom, vec_bias, vec_bias_mom,
 ):
-    live = (exits >= LAYER).astype(F32)
-    alive_row, alive_col = live[None, :], live[:, None]
+    exits = exits[None, :]
     (
         low1, qt, window, ot, lse, hidden, low2, gt, dft, ffn_part, dn2_part, proj, dffn, unit_rows,
     ) = forward_call(
-        lengths, tokens, cotangent, alive_row, alive_col, panels, unit_bias.T, gains, vec_bias
+        lengths, tokens, cotangent, exits, panels, unit_bias, gains, vec_bias
     )
     output, input_grad, panel_grads, vec_sums, unit_sums = backward_call(
-        lengths, alive_row, alive_col, gains, vec_bias, dn2_part, gt, dft, ot, lse, hidden, unit_rows, qt,
+        lengths, exits, gains, vec_bias, dn2_part, gt, dft, ot, lse, hidden, unit_rows, qt,
         tokens, cotangent, dffn, low2, low1, window, proj, ffn_part,
     )
-    new_panels, moment = muon_call(panel_grads, panel_mom, panels)
-    vec_sums = vec_sums.transpose(1, 0, 2).reshape(8, WIDTH)
-    unit_sum = unit_sums[0:6].reshape(6, GROUPS, HD).transpose(1, 0, 2).reshape(GROUPS, 6 * HD)
-    unit_moment = DECAY * unit_bias_mom + unit_sum
-    gains_moment = DECAY * gains_mom + vec_sums[0:2]
-    vec_moment = DECAY * vec_bias_mom + vec_sums[2:6]
-    return (
-        output, input_grad.astype(F32), new_panels, moment,
-        unit_bias - LR_VECTOR * unit_moment, unit_moment,
-        gains - LR_VECTOR * gains_moment, gains_moment,
-        vec_bias - LR_VECTOR * vec_moment, vec_moment,
+    return step_call(
+        panel_grads, panel_mom, panels, vec_sums, unit_sums, unit_bias, unit_bias_mom,
+        gains, gains_mom, vec_bias, vec_bias_mom, input_grad, output,
     )
 
 

time: 253 us -> 239 us (0.945)
  other arithmetic: 5.5 us -> 0 us
  Pallas kernels: 237 us -> 232 us
    pallas_call x1, Pallas kernels: 128 us -> 122 us  [backward_call(): pl.pallas_call(backward_kernel, in_specs=[pl.BlockSpec(memory_space=pltpu...]
    convert_element_type x2 -> x0, other arithmetic: 3.62 us -> none  [the longest x1 2.94 us: per_device(): input_grad.astype(F32)]
    unnamed x24 -> x26, local copies, waits for them, and re-layouts: 3.94 us -> 5.44 us
where the time goes in v4:
time: 239 us
  Pallas kernels  232 us (97%)
  local copies, waits for them, and re-layouts  5.44 us (2%)
    pallas_call x1, Pallas kernels, backward_call(): pl.pallas_call(backward_kernel, in_specs=[pl.BlockSpec(memory_space=pltpu...  122 us
    pallas_call x1, Pallas kernels, forward_call(): pl.pallas_call(forward_kernel, in_specs=[pl.BlockSpec(memory_space=pltpu....  101 us
    pallas_call x1, Pallas kernels, step_call(): pl.pallas_call(step_kernel, in_specs=[vmem] * 12 + [anywhere], out_specs=...  9.16 us
    unnamed x26, local copies, waits for them, and re-layouts  5.44 us

profile of v4, /device:TPU:0, one launch (start us, length us, event | category | flops | bytes accessed | tf_op | source)
XLA Modules:
  0.0 238.8 jit_solution(5899704135368054808)
XLA Ops:
  0.6 101.0 %layer_forward.1 = (bf16[256,2048]{1,0:T(8,128)(2,1)}, bf16[256,256]{1,0:T(8,128)(2,1)}, bf16[5,2,272,512]{3,2,1,0:T(8,128)(2,1)}, f32[256,256]{1,0:T(8,128)}, f...) custom-call(s32[4]{0:T(128)} %lengths.3, ...), custom_call_target="tpu_custom_call" | custom-call | tf_op jit(solution)/shard_map/layer_forward/pallas_call | solution.py:531
  101.7 0.0 copy-start
  101.7 0.0 copy-start.1
  101.7 0.0 copy-start.5
  101.7 0.0 copy-start.6
  101.7 0.0 copy-start.8
  101.8 0.0 copy-start.9
  101.8 0.0 copy-start.10
  101.8 0.0 copy-start.12
  101.8 122.2 %layer_backward.1 = (bf16[256,2048]{1,0:T(8,128)(2,1)}, bf16[256,2048]{1,0:T(8,128)(2,1)}, f32[3,64,2048]{2,1,0:T(8,128)}, f32[8,8,256]{2,1,0:T(8,128)}, f32[8,256]{1,0:T(8,128)}) custom-call(s32[4]{0:T(128)} %lengths.3, s32[1,256]{1,0:T(1,128)} %bitcast.2, f32[2,2048]{1,0:T(2,128)} %gains.5, f32[4,2048]{1,0:T(4,128)} %vec_bias.1, ...), custom_call_target="tpu_custom_call" | custom-call | tf_op jit(solution)/shard_map/layer_backward/pallas_call | solution.py:1089
  224.0 0.0 copy-done
  224.0 0.0 copy-done.1
  224.0 0.0 copy-done.5
  224.0 0.0 copy-done.6
  224.1 0.0 copy-done.8
  224.1 0.0 copy-done.9
  224.1 0.0 copy-done.10
  224.1 0.0 copy-done.12
  224.1 1.4 copy-done.2
  225.5 1.2 copy-done.3
  226.7 1.2 copy-done.4
  228.0 0.8 copy-done.7
  228.8 0.7 copy-done.11
  229.5 9.2 %panel_step.1 = (bf16[256,2048]{1,0:T(8,128)(2,1)}, f32[256,2048]{1,0:T(8,128)}, f32[3,64,2048]{2,1,0:T(8,128)}, f32[3,64,2048]{2,1,0:T(8,128)}, f32[4,384]{1,0:...) custom-call(f32[3,64,2048]{2,1,0:T(8,128)S(1)} %copy-done.2, ...), custom_call_target="tpu_custom_call" | custom-call | tf_op jit(solution)/shard_map/panel_step/pallas_call | solution.py:1212
  (5 shorter events, 0.0 us)
Async XLA Ops:
  101.7 122.3 %copy-start = (f32[3,64,2048]{2,1,0:T(8,128)S(1)}, f32[3,64,2048]{2,1,0:T(8,128)}, u32[]{:S(2)}) copy-start(f32[3,64,2048]{2,1,0:T(8,128)} %panels.3) | copy-start | bytes 4718596
  101.7 122.3 %copy-start.1 = (f32[3,64,2048]{2,1,0:T(8,128)S(1)}, f32[3,64,2048]{2,1,0:T(8,128)}, u32[]{:S(2)}) copy-start(f32[3,64,2048]{2,1,0:T(8,128)} %panel_mom.1) | copy-start | bytes 4718596
  101.7 122.3 %copy-start.5 = (f32[4,2048]{1,0:T(4,128)S(1)}, f32[4,2048]{1,0:T(4,128)}, u32[]{:S(2)}) copy-start(f32[4,2048]{1,0:T(4,128)} %vec_bias.1) | copy-start | bytes 98308
  101.7 122.3 %copy-start.6 = (f32[2,2048]{1,0:T(2,128)S(1)}, f32[2,2048]{1,0:T(2,128)}, u32[]{:S(2)}) copy-start(f32[2,2048]{1,0:T(2,128)} %gains.5) | copy-start | bytes 49156
  101.7 122.3 %copy-start.8 = (f32[4,2048]{1,0:T(4,128)S(1)}, f32[4,2048]{1,0:T(4,128)}, u32[]{:S(2)}) copy-start(f32[4,2048]{1,0:T(4,128)} %vec_bias_mom.1) | copy-start | bytes 98308
  101.8 122.3 %copy-start.9 = (f32[4,384]{1,0:T(4,128)S(1)}, f32[4,384]{1,0:T(4,128)}, u32[]{:S(2)}) copy-start(f32[4,384]{1,0:T(4,128)} %unit_bias.3) | copy-start | bytes 18436
  101.8 122.3 %copy-start.10 = (f32[2,2048]{1,0:T(2,128)S(1)}, f32[2,2048]{1,0:T(2,128)}, u32[]{:S(2)}) copy-start(f32[2,2048]{1,0:T(2,128)} %gains_mom.1) | copy-start | bytes 49156
  101.8 122.3 %copy-start.12 = (f32[4,384]{1,0:T(4,128)S(1)}, f32[4,384]{1,0:T(4,128)}, u32[]{:S(2)}) copy-start(f32[4,384]{1,0:T(4,128)} %unit_bias_mom.1) | copy-start | bytes 18436
  224.1 1.4 copy-start.2
  225.5 1.2 copy-start.3
  226.7 1.2 copy-start.4
  228.0 0.8 copy-start.7
  228.8 0.7 copy-start.11

commit v5 on v4

--- a/solution.py
+++ b/solution.py
@@ -896,14 +896,17 @@
             keys_t = keys.T
             d_key = jnp.zeros((ROWS, SPAN), F32)
             d_value = jnp.zeros((ROWS, SPAN), F32)
+            probs = [jnp.exp(nn(keys, q_rows[u]) + bias - lse[u : u + 1, :]) for u in range(GROUPS)]
+            d_scores = [
+                (probs[u] * (nn(values, do_rows[u]) - delta[u : u + 1, :])).astype(BF) for u in range(GROUPS)
+            ]
+            for u in range(GROUPS):
+                d_value = d_value + nn(probs[u].astype(BF), do_cols[u])
+            for u in range(GROUPS):
+                d_key = d_key + nn(d_scores[u], q_cols[u])
             for u in range(GROUPS):
                 heads = slice(u * HD, (u + 1) * HD)
-                prob = jnp.exp(nn(keys, q_rows[u]) + bias - lse[u : u + 1, :])
-                d_prob = nn(values, do_rows[u])
-                d_score = (prob * (d_prob - delta[u : u + 1, :])).astype(BF)
-                d_value = d_value + nn(prob.astype(BF), do_cols[u])
-                d_key = d_key + nn(d_score, q_cols[u])
-                dqt[heads, :] = dqt[heads, :] + nn(keys_t[heads, :], d_score)
+                dqt[heads, :] = dqt[heads, :] + nn(keys_t[heads, :], d_scores[u])
             d_kv[d, core, :, 0:SPAN] = d_key.astype(BF)
             d_kv[d, core, :, SPAN : 2 * SPAN] = d_value.astype(BF)
 
@@ -1217,7 +1220,7 @@
             shape((ROWS, WIDTH), BF), shape((ROWS, WIDTH), F32), panels, panels, unit, unit, gain, gain, vec, vec,
         ],
         scratch_shapes=[pltpu.SemaphoreType.DMA],
-        compiler_params=pltpu.CompilerParams(vmem_limit_bytes=40 * 2**20),
+        compiler_params=pltpu.CompilerParams(vmem_limit_bytes=60 * 2**20),
         name="panel_step",
     )(*args)
 

time: 239 us -> 263 us (1.10)
  Pallas kernels: 232 us -> 261 us
  local copies, waits for them, and re-layouts: 5.44 us -> 0 us
    pallas_call x1, Pallas kernels: 9.16 us -> 38 us  [step_call(): pl.pallas_call(step_kernel, in_specs=[vmem] * 12 + [anywhere], out_specs=...]
    unnamed x26 -> x0, local copies, waits for them, and re-layouts: 5.44 us -> none
where the time goes in v5:
time: 263 us; the launch traced here: 262 us
  Pallas kernels  261 us (99%)
    pallas_call x1, Pallas kernels, backward_call(): pl.pallas_call(backward_kernel, in_specs=[pl.BlockSpec(memory_space=pltpu...  122 us
    pallas_call x1, Pallas kernels, forward_call(): pl.pallas_call(forward_kernel, in_specs=[pl.BlockSpec(memory_space=pltpu....  101 us
    pallas_call x1, Pallas kernels, step_call(): pl.pallas_call(step_kernel, in_specs=[vmem] * 12 + [anywhere], out_specs=...  38 us

profile of v5, /device:TPU:0, one launch (start us, length us, event | category | flops | bytes accessed | tf_op | source)
XLA Modules:
  0.0 262.0 jit_solution(16156785900512030316)
XLA Ops:
  0.6 101.0 %layer_forward.1 = (bf16[256,2048]{1,0:T(8,128)(2,1)}, bf16[256,256]{1,0:T(8,128)(2,1)}, bf16[5,2,272,512]{3,2,1,0:T(8,128)(2,1)}, f32[256,256]{1,0:T(8,128)}, f...) custom-call(s32[4]{0:T(128)} %lengths.3, ...), custom_call_target="tpu_custom_call" | custom-call | tf_op jit(solution)/shard_map/layer_forward/pallas_call | solution.py:531
  101.7 122.2 %layer_backward.1 = (bf16[256,2048]{1,0:T(8,128)(2,1)}, bf16[256,2048]{1,0:T(8,128)(2,1)}, f32[3,64,2048]{2,1,0:T(8,128)}, f32[8,8,256]{2,1,0:T(8,128)}, f32[8,256]{1,0:T(8,128)}) custom-call(s32[4]{0:T(128)} %lengths.3, s32[1,256]{1,0:T(1,128)} %bitcast.2, f32[2,2048]{1,0:T(2,128)} %gains.5, f32[4,2048]{1,0:T(4,128)} %vec_bias.1, ...), custom_call_target="tpu_custom_call" | custom-call | tf_op jit(solution)/shard_map/layer_backward/pallas_call | solution.py:1092
  223.8 38.0 %panel_step.1 = (bf16[256,2048]{1,0:T(8,128)(2,1)}, f32[256,2048]{1,0:T(8,128)}, f32[3,64,2048]{2,1,0:T(8,128)}, f32[3,64,2048]{2,1,0:T(8,128)}, f32[4,384]{1,0:...) custom-call(f32[3,64,2048]{2,1,0:T(8,128)} %get-tuple-element.43.gra, ...), custom_call_target="tpu_custom_call" | custom-call | tf_op jit(solution)/shard_map/panel_step/pallas_call | solution.py:1215

commit v6 on v5

--- a/solution.py
+++ b/solution.py
@@ -1156,11 +1156,9 @@
 def step_kernel(
     grads, panel_mom, panels, vec_sums, unit_sums, unit_bias, unit_bias_mom, gains, gains_mom, vec_bias, vec_bias_mom,
     in_low, out_low,
-    out_any, in_grad, new_panels, new_mom, new_unit, new_unit_mom, new_gains, new_gains_mom, new_vec, new_vec_mom,
-    sem,
+    out_copy, in_grad, new_panels, new_mom, new_unit, new_unit_mom, new_gains, new_gains_mom, new_vec, new_vec_mom,
 ):
-    whole = pltpu.make_async_copy(out_low, out_any, sem)
-    whole.start()
+    out_copy[...] = out_low[...]
     count = panels.shape[0]
     eye = jnp.where(
         lax.broadcasted_iota(jnp.int32, (HD, HD), 0) == lax.broadcasted_iota(jnp.int32, (HD, HD), 1), 1.0, 0.0
@@ -1204,22 +1202,19 @@
         held = panels[n]
         size_w = jnp.sum(held * held, axis=(0, 1), keepdims=True)
         new_panels[n] = held - LR_MATRIX * jnp.sqrt(size_w) * lax.rsqrt(size_u + 1e-06) * direction
-    whole.wait()
 
 
 def step_call(*args):
     vmem = pl.BlockSpec(memory_space=pltpu.VMEM)
-    anywhere = pl.BlockSpec(memory_space=pl.ANY)
     shape = jax.ShapeDtypeStruct
     panels, unit, gain, vec = (shape(args[n].shape, F32) for n in (2, 5, 7, 9))
     return pl.pallas_call(
         step_kernel,
-        in_specs=[vmem] * 12 + [anywhere],
-        out_specs=[anywhere] + [vmem] * 9,
+        in_specs=[vmem] * 13,
+        out_specs=[vmem] * 10,
         out_shape=[
             shape((ROWS, WIDTH), BF), shape((ROWS, WIDTH), F32), panels, panels, unit, unit, gain, gain, vec, vec,
         ],
-        scratch_shapes=[pltpu.SemaphoreType.DMA],
         compiler_params=pltpu.CompilerParams(vmem_limit_bytes=60 * 2**20),
         name="panel_step",
     )(*args)

time: 263 us -> 237 us (0.901)
  Pallas kernels: 261 us -> 235 us
    pallas_call x1, Pallas kernels: 38 us -> 12.1 us  [step_call(): pl.pallas_call(step_kernel, in_specs=[vmem] * 13, out_specs=[vmem] * 10,...]
where the time goes in v6:
time: 237 us; the launch traced here: 236 us
  Pallas kernels  235 us (99%)
    pallas_call x1, Pallas kernels, backward_call(): pl.pallas_call(backward_kernel, in_specs=[pl.BlockSpec(memory_space=pltpu...  122 us
    pallas_call x1, Pallas kernels, forward_call(): pl.pallas_call(forward_kernel, in_specs=[pl.BlockSpec(memory_space=pltpu....  101 us
    pallas_call x1, Pallas kernels, step_call(): pl.pallas_call(step_kernel, in_specs=[vmem] * 13, out_specs=[vmem] * 10,...  12.1 us

profile of v6, /device:TPU:0, one launch (start us, length us, event | category | flops | bytes accessed | tf_op | source)
XLA Modules:
  0.0 236.1 jit_solution(1107681801292374090)
XLA Ops:
  0.6 101.0 %layer_forward.1 = (bf16[256,2048]{1,0:T(8,128)(2,1)}, bf16[256,256]{1,0:T(8,128)(2,1)}, bf16[5,2,272,512]{3,2,1,0:T(8,128)(2,1)}, f32[256,256]{1,0:T(8,128)}, f...) custom-call(s32[4]{0:T(128)} %lengths.3, ...), custom_call_target="tpu_custom_call" | custom-call | tf_op jit(solution)/shard_map/layer_forward/pallas_call | solution.py:531
  101.7 122.2 %layer_backward.1 = (bf16[256,2048]{1,0:T(8,128)(2,1)}, bf16[256,2048]{1,0:T(8,128)(2,1)}, f32[3,64,2048]{2,1,0:T(8,128)}, f32[8,8,256]{2,1,0:T(8,128)}, f32[8,256]{1,0:T(8,128)}) custom-call(s32[4]{0:T(128)} %lengths.3, s32[1,256]{1,0:T(1,128)} %bitcast.2, f32[2,2048]{1,0:T(2,128)} %gains.5, f32[4,2048]{1,0:T(4,128)} %vec_bias.1, ...), custom_call_target="tpu_custom_call" | custom-call | tf_op jit(solution)/shard_map/layer_backward/pallas_call | solution.py:1092
  223.8 12.1 %panel_step.1 = (bf16[256,2048]{1,0:T(8,128)(2,1)}, f32[256,2048]{1,0:T(8,128)}, f32[3,64,2048]{2,1,0:T(8,128)}, f32[3,64,2048]{2,1,0:T(8,128)}, f32[4,384]{1,0:...) custom-call(f32[3,64,2048]{2,1,0:T(8,128)} %get-tuple-element.43.gra, ...), custom_call_target="tpu_custom_call" | custom-call | tf_op jit(solution)/shard_map/panel_step/pallas_call | solution.py:1211
